TPU v7x, 512 devices: a whole 4x8x8 slice. The times are simulated.
512 devices in a mesh: lat: 64 (over y, z), tok: 8 (over x, core).
Axes of the slice: x: 4, y: 8, z: 8, core: 2. Of those that a mesh axis runs over, the one named last changes fastest.
Arguments:
- tokens: bfloat16 [512, 9216], P(None, 'tok'), may hold values from -6 to 6
- enc_weight: bfloat16 [9216, 32768], P('tok', 'lat'), may hold values from -0.0625 to 0.0625
- enc_bias: float32 [32768], P('lat'), may hold values from -1.5 to 0.5
- dec_weight: bfloat16 [32768, 9216], P('lat', 'tok'), may hold values from -0.03125 to 0.03125
- pairs: int32 [64, 32], P('lat'), may hold values from 0 to 31, as said below
- counts: int32 [64], P('lat'), may hold values from 1 to 32, as said below
Outputs:
- error: bfloat16 [512, 9216], P('lat', 'tok')
- enc_grad: bfloat16 [9216, 32768], P('tok', 'lat')
- dec_grad: bfloat16 [32768, 9216], P('lat', 'tok')
- bias_grad: float32 [32768], P('lat')
Inputs may be any that keep to these rules, and one draw needn't show every extreme that they name: `pairs`: each code is g * 8 + k for a row block g and a latent block k of the shard; the first counts[j] codes of row j are distinct; codes past counts[j] are to be ignored. `counts`: some shard has all 32 slots active.
All inputs are finite; a program needn't handle non-finite values.
Results may differ from a plain program's by a relative error of at most 0.023.
Values may be sent and summed in bfloat16 or wider, within the bound.
No kernel may reach another device: no remote copies, remote signals or barrier semaphores. Data moves between devices by JAX's collectives and lax.ppermute only.
A program may use at most 128 MiB of HBM per device.

v0:
```python
import jax
import jax.numpy as jnp
from jax import lax
from jax.sharding import PartitionSpec as P

BR = 128
BL = 64


PENALTY = 0.3
EPSILON = 1e-06


def body(tokens, enc_weight, enc_bias, dec_weight, pairs, counts):
    rows_total, width = tokens.shape
    local_lat = enc_weight.shape[1]
    nblk = local_lat // BL
    rblk = rows_total // BR
    slots = pairs.shape[1]
    lat_count = lax.axis_size("lat")
    tok_count = lax.axis_size("tok")
    half = lax.axis_index("tok") * 2 // tok_count
    codes = pairs[0]
    row_of = codes // nblk
    lat_of = codes % nblk
    valid = jnp.arange(slots, dtype=jnp.int32) < counts[0]
    x_sel = jnp.take(tokens.reshape(rblk, BR, width), row_of, axis=0)
    enc_sel = jnp.take(enc_weight.reshape(width, nblk, BL), lat_of, axis=1)
    dec_sel = jnp.take(dec_weight.reshape(nblk, BL, width), lat_of, axis=0)
    bias_sel = jnp.take(enc_bias.reshape(nblk, BL), lat_of, axis=0)
    squares = jnp.sum(jnp.square(dec_weight.astype(jnp.float32)), axis=1)
    halves = jnp.where((jnp.arange(2) == half)[:, None], squares[None, :], 0.0)
    partial_value = jnp.einsum("prf,fpl->prl", x_sel, enc_sel, preferred_element_type=jnp.float32)
    partial_value = jnp.where(valid[:, None, None], partial_value, 0.0)
    pre_sum, halves_sum = (
        lax.psum(partial_value.astype(jnp.bfloat16), "tok").astype(jnp.float32),
        lax.psum(halves.astype(jnp.bfloat16), "tok").astype(jnp.float32),
    )
    pre = pre_sum + bias_sel[:, None, :]
    acts = jnp.where(valid[:, None, None], jax.nn.softplus(pre), 0.0).astype(jnp.bfloat16)
    norms = jnp.sqrt(halves_sum + EPSILON)
    total_norm = norms[0] + norms[1]
    own_norm = jnp.where(half == 0, norms[0], norms[1])
    place = (
        (row_of[:, None] == jnp.arange(rblk, dtype=jnp.int32)[None, :]) & valid[:, None]
    ).astype(jnp.bfloat16)
    pick_low = (
        (lat_of[:, None] == jnp.arange(nblk, dtype=jnp.int32)[None, :]) & valid[:, None]
    ).astype(jnp.bfloat16)
    dense = (
        jnp.einsum("pg,pk,prl->grkl", place, pick_low, acts, preferred_element_type=jnp.float32)
        .astype(jnp.bfloat16)
        .reshape(rows_total, local_lat)
    )
    share_rows = rows_total // lat_count
    own_start = lax.axis_index("lat") * share_rows
    recon = lax.psum(jnp.dot(dense, dec_weight, preferred_element_type=jnp.float32), "lat")
    err_full = (recon - tokens.astype(jnp.float32)).astype(jnp.bfloat16)
    err_own = lax.dynamic_slice_in_dim(err_full, own_start, share_rows, 0)
    err_sel = jnp.take(err_full.reshape(rblk, BR, width), row_of, axis=0)
    back = jnp.einsum("prf,plf->prl", err_sel, dec_sel, preferred_element_type=jnp.float32)
    back_sum = lax.psum(back.astype(jnp.bfloat16), "tok").astype(jnp.float32)
    norm_sel = jnp.take(total_norm.reshape(nblk, BL), lat_of, axis=0)
    grad_act = jnp.where(valid[:, None, None], back_sum + PENALTY * norm_sel[:, None, :], 0.0)
    grad_pre = (grad_act * jax.nn.sigmoid(pre)).astype(jnp.bfloat16)
    pick = pick_low.astype(jnp.float32)
    enc_terms = jnp.einsum("prf,prl->pfl", x_sel, grad_pre, preferred_element_type=jnp.float32)
    enc_grad = jnp.einsum("pk,pfl->fkl", pick, enc_terms, precision=lax.Precision.HIGHEST).reshape(
        width, local_lat
    )
    dec_terms = jnp.einsum("prl,prf->plf", acts, err_sel, preferred_element_type=jnp.float32)
    dec_data = jnp.einsum("pk,plf->klf", pick, dec_terms, precision=lax.Precision.HIGHEST).reshape(
        local_lat, width
    )
    act_sum = jnp.einsum(
        "pk,pl->kl",
        pick,
        jnp.sum(acts.astype(jnp.float32), axis=1),
        precision=lax.Precision.HIGHEST,
    ).reshape(local_lat)
    bias_grad = jnp.einsum(
        "pk,pl->kl",
        pick,
        jnp.sum(grad_pre.astype(jnp.float32), axis=1),
        precision=lax.Precision.HIGHEST,
    ).reshape(local_lat)
    dec_grad = dec_data + PENALTY * (act_sum / own_norm)[:, None] * dec_weight.astype(jnp.float32)
    return (err_own, enc_grad.astype(jnp.bfloat16), dec_grad.astype(jnp.bfloat16), bias_grad)


def solution(mesh):
    return jax.shard_map(
        body,
        mesh=mesh,
        in_specs=(
            P(None, "tok"),
            P("tok", "lat"),
            P("lat"),
            P("lat", "tok"),
            P("lat", None),
            P("lat"),
        ),
        out_specs=(P("lat", "tok"), P("tok", "lat"), P("lat", "tok"), P("lat")),
        check_vma=False,
    )
```

profile of v0, /device:TPU:1, one launch (start us, length us, event | category | flops | bytes accessed | tf_op | source)
XLA Modules:
  0.0 394.9 jit_solution(1506934706287057482)
XLA Ops:
  7.2 0.0 all-reduce.4.cloned.1.call-start
  7.2 0.7 compare_select_fusion.3
  7.9 0.7 fusion.65
  8.5 0.7 compare_and_fusion
  9.2 0.0 copy-start.14
  9.2 0.0 copy-start.16
  9.2 1.7 copy.11
  11.0 0.0 copy-start.13
  11.6 0.0 copy-start.6
  11.6 0.0 copy-start
  11.7 3.3 gather_fusion
  14.9 0.0 copy-done.13
  14.9 0.0 copy-done
  14.9 5.5 %gather_fusion.2 = bf16[32,128,1152]{2,1,0:T(8,128)(2,1)} fusion(bf16[4,128,1152]{2,1,0:T(8,128)(2,1)S(1)} %bitcast.67, s32[1024]{0:T(1024)S(1)} %pad_clamp_fusion.2), kind=kCustom, calls=%fused_computation.clone | custom fusion | bytes 18874496 | tf_op jit(solution)/shard_map/jit(_take)/gather | solution.py:27
  20.5 0.0 copy-done.14
  20.5 9.7 %fusion.30 = bf16[32,128,64]{1,2,0:T(8,128)(2,1)} fusion(bf16[32,1152,64]{1,2,0:T(8,128)(2,1)} %gather_fusion, pred[32]{0:T(512)(128)(4,1)S(1)} %get-tuple-element.22, bf16[32,128,1152]{2,1,0:T(8,128)(2,1)} %gather_fusion.2, pred[32]{0:T(512)(128)(4,1)S(1)} %get-tuple-element.16, pred[32]{0:T(512)(128)(4,1)S(1)} %iota_compare_fusion.3), kind=kOutput, calls=%fused_computation.35 | convolution fusion | flops 611581952 | bytes 14680160 | tf_op jit(solution)/shard_map/prf,fpl->prl/dot_general | solution.py:33
  30.1 0.0 all-reduce.4.cloned.1.call-update
  30.1 0.0 all-reduce.6.cloned.1.call-start
  30.3 0.0 copy-done.1
  30.3 0.3 fusion.19
  30.6 0.1 select_convert_fusion
  30.6 18.6 %psum.31 = bf16[2,512]{1,0:T(2,128)(2,1)S(1)} all-reduce(bf16[2,512]{1,0:T(2,128)(2,1)S(1)} %select_convert_fusion), channel_id=1, replica_groups=mesh['lat'=64,'tok'=8] {'tok'}, use_global_device_ids=true, to_apply=%region_4.7 | all-reduce | flops 1024 | bytes 4096 | tf_op jit(solution)/shard_map/psum | solution.py:37
  49.4 0.1 add.120
  49.4 0.1 reshape.189
  49.5 0.6 gather_fusion.5
  50.1 0.6 gather_fusion.3
  50.7 0.7 select_multiply_fusion
  51.3 54.4 %all-reduce.4.cloned.1.call-done = bf16[32,128,64]{1,2,0:T(8,128)(2,1)} async-done(((bf16[32,128,64]{1,2,0:T(8,128)(2,1)}), bf16[32,128,64]{1,2,0:T(8,128)(2,1)}) %all-reduce.4.cloned.1.call-update) | async-done | bytes 524304 | tf_op jit(solution)/shard_map/psum | solution.py:36
  105.7 2.0 convert_reduce_fusion.1
  107.7 0.0 copy-start.2
  107.7 0.8 copy-done.2
  108.5 0.4 fusion.33
  108.9 0.4 copy.13
  109.3 2.3 fusion.36
  111.7 0.0 all-reduce.6.cloned.1.call-update
  111.7 0.0 all-reduce.8.cloned.1.call-start
  111.8 3.2 gather_fusion.1
  114.9 0.0 copy-done.6
  114.9 0.1 fusion.46
  115.1 0.1 reshape.194
  115.1 0.6 divide_multiply_fusion
  115.7 157.4 %all-reduce.6.cloned.1.call-done = f32[512,1152]{1,0:T(8,128)} async-done(((f32[512,1152]{1,0:T(8,128)}), f32[512,1152]{1,0:T(8,128)}) %all-reduce.6.cloned.1.call-update) | async-done | bytes 2359312 | tf_op jit(solution)/shard_map/psum | solution.py:57
  273.2 1.9 subtract_convert_fusion
  275.0 0.0 copy-start.3
  275.0 6.0 %gather_fusion.4 = bf16[32,128,1152]{2,1,0:T(8,128)(2,1)} fusion(bf16[4,128,1152]{2,1,0:T(8,128)(2,1)S(1)} %bitcast.66, s32[1024]{0:T(1024)} %copy-done.13), kind=kCustom, calls=%fused_computation.2.clone | custom fusion | bytes 18874496 | tf_op jit(solution)/shard_map/jit(_take)/gather | solution.py:60
  281.0 9.1 %fusion.12 = f32[32,64,1152]{2,1,0:T(8,128)} fusion(bf16[32,128,64]{1,2,0:T(8,128)(2,1)S(1)} %copy-done.3, bf16[32,128,1152]{2,1,0:T(8,128)(2,1)} %gather_fusion.4, pred[32]{0:T(512)(128)(4,1)S(1)} %copy-done.15), kind=kOutput, calls=%fused_computation.20 | convolution fusion | flops 608698368 | bytes 19398688 | tf_op jit(solution)/shard_map/prl,prf->plf/dot_general | solution.py:71
  290.2 9.7 %fusion.24 = bf16[32,128,64]{1,2,0:T(8,128)(2,1)} fusion(bf16[32,64,1152]{2,1,0:T(8,128)(2,1)} %gather_fusion.1, pred[32]{0:T(512)(128)(4,1)S(1)} %copy-done.17, bf16[32,128,1152]{2,1,0:T(8,128)(2,1)} %gather_fusion.4, pred[32]{0:T(512)(128)(4,1)S(1)} %copy-done.15), kind=kOutput, calls=%fused_computation.32 | convolution fusion | flops 611319808 | bytes 14680128 | tf_op jit(solution)/shard_map/prf,plf->prl/dot_general | solution.py:61
  299.9 0.0 all-reduce.8.cloned.1.call-update
  299.9 0.0 copy-done.7
  299.9 0.0 copy-done.10
  299.9 11.9 %fusion = f32[8,64,1152]{2,0,1:T(8,128)S(1)} fusion(f32[32,64,1152]{2,1,0:T(8,128)} %fusion.12, s32[32]{0:T(128)S(1)} %copy-done.10, pred[32]{0:T(512)(128)(4,1)S(1)} %copy-done.7), kind=kOutput, calls=%fused_computation.6 | convolution fusion | flops 226492928 | bytes 11796640 | tf_op jit(solution)/shard_map/pk,plf->klf/dot_general | solution.py:72
  311.8 0.0 copy-start.12
  311.8 0.5 copy.15
  312.3 0.2 copy-done.12
  312.5 1.4 fusion.21
  313.9 0.6 constant_dynamic-slice_fusion
  314.5 55.7 %all-reduce.8.cloned.1.call-done = bf16[32,128,64]{1,2,0:T(8,128)(2,1)} async-done(((bf16[32,128,64]{1,2,0:T(8,128)(2,1)}), bf16[32,128,64]{1,2,0:T(8,128)(2,1)}) %all-reduce.8.cloned.1.call-update) | async-done | bytes 524304 | tf_op jit(solution)/shard_map/psum | solution.py:62
  370.2 2.1 convert_reduce_fusion
  372.3 5.1 %fusion.11 = f32[32,1152,64]{1,2,0:T(8,128)S(1)} fusion(bf16[32,128,64]{1,2,0:T(8,128)(2,1)S(1)} %get-tuple-element.11, bf16[32,128,1152]{2,1,0:T(8,128)(2,1)} %gather_fusion.2, pred[32]{0:T(512)(128)(4,1)S(1)} %copy-done.15), kind=kOutput, calls=%fused_computation.19 | convolution fusion | flops 608698368 | bytes 19398688 | tf_op jit(solution)/shard_map/prf,prl->pfl/dot_general | solution.py:67
  377.5 8.5 %fusion.16 = bf16[1152,8,64]{0,1,2:T(8,128)(2,1)S(1)} fusion(f32[32,1152,64]{1,2,0:T(8,128)S(1)} %fusion.11, s32[32]{0:T(128)S(1)} %copy-done.11, pred[32]{0:T(512)(128)(4,1)S(1)} %copy-done.8), kind=kOutput, calls=%fused_computation.25 | convolution fusion | flops 227082752 | bytes 10616992 | tf_op jit(solution)/shard_map/pk,pfl->fkl/dot_general | solution.py:68
  386.0 0.2 copy.14
  386.2 1.4 copy.16
  387.6 0.1 fusion.48
  387.7 0.7 reshape.195
  (31 shorter events, 0.1 us)
Async XLA Ops:
  7.2 98.6 %all-reduce.4.cloned.1.call-start = ((), (), s32[]{:S(2)}) async-start(), calls=%async_computation | async-start | bytes 1048576 | tf_op jit(solution)/shard_map/psum | solution.py:36
  7.9 107.1 %copy-start.9 = (s32[32]{0:T(128)}, s32[32]{0:T(128)S(1)}, u32[]{:S(2)}) copy-start(s32[32]{0:T(128)S(1)} %get-tuple-element.15) | copy-start | bytes 388
  9.2 11.2 %copy-start.14 = (pred[32]{0:T(512)(128)(4,1)}, pred[32]{0:T(512)(128)(4,1)S(1)}, u32[]{:S(2)}) copy-start(pred[32]{0:T(512)(128)(4,1)S(1)} %get-tuple-element.16) | copy-start | bytes 100
  9.2 41.4 %copy-start.16 = (pred[32]{0:T(512)(128)(4,1)}, pred[32]{0:T(512)(128)(4,1)S(1)}, u32[]{:S(2)}) copy-start(pred[32]{0:T(512)(128)(4,1)S(1)} %get-tuple-element.22) | copy-start | bytes 100
  11.0 4.0 %copy-start.13 = (s32[1024]{0:T(1024)}, s32[1024]{0:T(1024)S(1)}, u32[]{:S(2)}) copy-start(s32[1024]{0:T(1024)S(1)} %pad_clamp_fusion.2) | copy-start | bytes 12292
  11.6 103.3 %copy-start.6 = (pred[32]{0:T(512)(128)(4,1)}, pred[32]{0:T(512)(128)(4,1)S(1)}, u32[]{:S(2)}) copy-start(pred[32]{0:T(512)(128)(4,1)S(1)} %iota_compare_fusion.3) | copy-start | bytes 100
  11.6 3.3 copy-start
  20.5 9.8 %copy-start.1 = (bf16[512,1152]{1,0:T(8,128)(2,1)S(1)}, bf16[512,1152]{1,0:T(8,128)(2,1)}, u32[]{:S(2)}) copy-start(bf16[512,1152]{1,0:T(8,128)(2,1)} %param.13) | copy-start | bytes 3538948
  20.5 29.0 %copy-start.18 = (f32[512]{0:T(512)S(1)}, f32[512]{0:T(512)}, u32[]{:S(2)}) copy-start(f32[512]{0:T(512)} %param.12) | copy-start | bytes 6148
  30.1 243.0 %all-reduce.6.cloned.1.call-start = ((), (), s32[]{:S(2)}) async-start(), calls=%async_computation.1 | async-start | bytes 4718592 | tf_op jit(solution)/shard_map/psum | solution.py:57
  107.7 0.8 copy-start.2
  111.7 258.5 %all-reduce.8.cloned.1.call-start = ((), (), s32[]{:S(2)}) async-start(), calls=%async_computation.2 | async-start | bytes 1048576 | tf_op jit(solution)/shard_map/psum | solution.py:62
  275.0 6.0 %copy-start.3 = (bf16[32,128,64]{1,2,0:T(8,128)(2,1)S(1)}, bf16[32,128,64]{1,2,0:T(8,128)(2,1)}, u32[]{:S(2)}) copy-start(bf16[32,128,64]{1,2,0:T(8,128)(2,1)} %copy-done.2) | copy-start | bytes 1572868
  275.0 6.0 %copy-start.15 = (pred[32]{0:T(512)(128)(4,1)S(1)}, pred[32]{0:T(512)(128)(4,1)}, u32[]{:S(2)}) copy-start(pred[32]{0:T(512)(128)(4,1)} %copy-done.14) | copy-start | bytes 100
  281.0 9.1 %copy-start.17 = (pred[32]{0:T(512)(128)(4,1)S(1)}, pred[32]{0:T(512)(128)(4,1)}, u32[]{:S(2)}) copy-start(pred[32]{0:T(512)(128)(4,1)} %copy-done.16) | copy-start | bytes 100
  290.2 9.7 %copy-start.7 = (pred[32]{0:T(512)(128)(4,1)S(1)}, pred[32]{0:T(512)(128)(4,1)}, u32[]{:S(2)}) copy-start(pred[32]{0:T(512)(128)(4,1)} %copy-done.6) | copy-start | bytes 100
  290.2 9.7 %copy-start.10 = (s32[32]{0:T(128)S(1)}, s32[32]{0:T(128)}, u32[]{:S(2)}) copy-start(s32[32]{0:T(128)} %copy-done.9) | copy-start | bytes 388
  311.8 0.7 copy-start.12
  311.8 58.4 %copy-start.4 = (bf16[32,128,64]{1,2,0:T(8,128)(2,1)S(1)}, bf16[32,128,64]{1,2,0:T(8,128)(2,1)}, u32[]{:S(2)}) copy-start(bf16[32,128,64]{1,2,0:T(8,128)(2,1)} %all-reduce.4.cloned.1.call-done) | copy-start | bytes 1572868
  311.8 58.4 %copy-start.5 = (f32[32,64]{1,0:T(8,128)S(1)}, f32[32,64]{1,0:T(8,128)}, u32[]{:S(2)}) copy-start(f32[32,64]{1,0:T(8,128)} %get-tuple-element.20) | copy-start | bytes 24580
  372.3 5.1 %copy-start.8 = (pred[32]{0:T(512)(128)(4,1)S(1)}, pred[32]{0:T(512)(128)(4,1)}, u32[]{:S(2)}) copy-start(pred[32]{0:T(512)(128)(4,1)} %copy-done.6) | copy-start | bytes 100
  372.3 5.1 %copy-start.11 = (s32[32]{0:T(128)S(1)}, s32[32]{0:T(128)}, u32[]{:S(2)}) copy-start(s32[32]{0:T(128)} %copy-done.9) | copy-start | bytes 388
Sparse Core Ops, SparseCore 0:
  30.3 75.4 all-reduce.3
  111.8 161.2 all-reduce.5
  300.0 70.1 all-reduce.7
where the time goes:
time: 396 us; the launch traced here: 395 us
  waiting for transfers between devices  268 us (68%)
  matrix products  57 us (14%)
  local copies, waits for them, and re-layouts  25.8 us (7%)
  blocking collectives  18.6 us (5%)
  between operations  14.7 us (4%)
  other arithmetic  11.1 us (3%)
    psum x1, waiting for transfers between devices, body(): lax.psum(jnp.dot(dense, dec_weight, preferred_element_type=jnp.float32),...  157 us
    psum x1, waiting for transfers between devices, body(): back_sum = lax.psum(back.astype(jnp.bfloat16), 'tok').astype(jnp.float32)  55.7 us
    psum x1, waiting for transfers between devices, body(): lax.psum(partial_value.astype(jnp.bfloat16), 'tok').astype(jnp.float32)  54.4 us
    psum x1, blocking collectives, body(): lax.psum(halves.astype(jnp.bfloat16), 'tok').astype(jnp.float32)  18.6 us
    dot_general x1, matrix products, body(): jnp.einsum('pk,plf->klf', pick, dec_terms, precision=lax.Precision.HIGHEST)  11.9 us
    dot_general x1, matrix products, body(): jnp.einsum('prf,plf->prl', err_sel, dec_sel, preferred_element_type=jnp.f...  9.69 us
    dot_general x1, matrix products, body(): jnp.einsum('prf,fpl->prl', x_sel, enc_sel, preferred_element_type=jnp.flo...  9.65 us
    dot_general x1, matrix products, body(): jnp.einsum('prl,prf->plf', acts, err_sel, preferred_element_type=jnp.floa...  9.14 us
  transfers between devices with their start and end apart: 3, of which 3 were waited for; matrix products, arithmetic and copies ran while one was open for 5% of the time, Pallas kernels for 0%

commit v1 on v0

v1 whole, which is shorter than its diff:
```python
import jax
import jax.numpy as jnp
from jax import lax
from jax.sharding import PartitionSpec as P

BR = 128
BL = 64
PENALTY = 0.3
EPSILON = 1e-06
EXTRA = 16

f32 = jnp.float32
bf16 = jnp.bfloat16


def body(tokens, enc_weight, enc_bias, dec_weight, pairs, counts):
    rows, width = tokens.shape
    local_lat = enc_weight.shape[1]
    nblk = local_lat // BL
    rblk = rows // BR
    slots = pairs.shape[1]
    n_lat = lax.axis_size("lat")
    n_tok = lax.axis_size("tok")
    tok = lax.axis_index("tok")
    half = tok * 2 // n_tok
    own = rows // n_tok
    share = rows // n_lat

    codes = pairs[0]
    valid = jnp.arange(slots, dtype=jnp.int32) < counts[0]
    g_own = tok * own // BR
    hit = valid[:, None] & (
        codes[:, None] == g_own * nblk + jnp.arange(local_lat, dtype=jnp.int32)[None, :] // BL
    )
    mask = jnp.any(hit, axis=0)[None, :]

    dec32 = dec_weight.astype(f32)
    squares = jnp.sum(dec32 * dec32, axis=1).astype(bf16)
    part = jnp.dot(tokens, enc_weight, preferred_element_type=f32).astype(bf16)
    packed = jnp.concatenate(
        [
            part.reshape(n_tok, own, local_lat),
            jnp.broadcast_to(squares[None, None, :], (n_tok, EXTRA, local_lat)),
        ],
        axis=1,
    )
    got = lax.all_to_all(packed, "tok", 0, 0, tiled=True)
    pre = jnp.sum(got[:, :own].astype(f32), axis=0) + enc_bias[None, :]
    sq = got[:, own].astype(f32)
    norm_a = jnp.sqrt(jnp.sum(sq[: n_tok // 2], axis=0) + EPSILON)
    norm_b = jnp.sqrt(jnp.sum(sq[n_tok // 2 :], axis=0) + EPSILON)
    total_norm = norm_a + norm_b
    own_norm = jnp.where(half == 0, norm_a, norm_b)

    acts_own = jnp.where(mask, jax.nn.softplus(pre), 0.0).astype(bf16)
    acts = lax.all_gather(acts_own, "tok", axis=0, tiled=True)

    recon = jnp.dot(acts, dec_weight, preferred_element_type=f32).astype(bf16)
    got = lax.all_to_all(recon.reshape(n_lat, share, width), "lat", 0, 0, tiled=True)
    x_own = lax.dynamic_slice_in_dim(tokens, lax.axis_index("lat") * share, share, 0)
    err_own = (jnp.sum(got.astype(f32), axis=0) - x_own.astype(f32)).astype(bf16)
    err = lax.all_to_all(
        jnp.broadcast_to(err_own[None], (n_lat, share, width)), "lat", 0, 0, tiled=True
    ).reshape(rows, width)

    back = lax.dot_general(
        err, dec_weight, (((1,), (1,)), ((), ())), preferred_element_type=f32
    ).astype(bf16)
    got = lax.all_to_all(back.reshape(n_tok, own, local_lat), "tok", 0, 0, tiled=True)
    grad_act = jnp.sum(got.astype(f32), axis=0) + PENALTY * total_norm[None, :]
    grad_own = jnp.where(mask, grad_act * jax.nn.sigmoid(pre), 0.0).astype(bf16)
    grad_pre = lax.all_gather(grad_own, "tok", axis=0, tiled=True)

    act_sum = jnp.sum(acts.astype(f32), axis=0)
    dec_data = lax.dot_general(acts, err, (((0,), (0,)), ((), ())), preferred_element_type=f32)
    dec_grad = dec_data + PENALTY * (act_sum / own_norm)[:, None] * dec32
    enc_grad = lax.dot_general(tokens, grad_pre, (((0,), (0,)), ((), ())), preferred_element_type=f32)
    bias_grad = jnp.sum(grad_pre.astype(f32), axis=0)
    return err_own, enc_grad.astype(bf16), dec_grad.astype(bf16), bias_grad


def solution(mesh):
    return jax.shard_map(
        body,
        mesh=mesh,
        in_specs=(
            P(None, "tok"),
            P("tok", "lat"),
            P("lat"),
            P("lat", "tok"),
            P("lat", None),
            P("lat"),
        ),
        out_specs=(P("lat", "tok"), P("tok", "lat"), P("lat", "tok"), P("lat")),
        check_vma=False,
    )
```

time: 396 us -> 163 us (0.41)
  waiting for transfers between devices: 268 us -> 75.5 us
  matrix products: 57 us -> 11 us
  starting transfers between devices: 0.12 us -> 38.5 us
  local copies, waits for them, and re-layouts: 25.8 us -> 3.4 us
  between operations: 14.7 us -> 1.47 us
  blocking collectives: 18.6 us -> 27.8 us
  other arithmetic: 11.1 us -> 4.79 us
    psum x3 -> x0, waiting for transfers between devices: 268 us -> none  [the longest x1 157 us: body(): lax.psum(jnp.dot(dense, dec_weight, preferred_element_type=jnp.float32),...]
    all_to_all x0 -> x4, waiting for transfers between devices: none -> 75.5 us  [the longest x1 30.2 us: body(): lax.all_to_all(recon.reshape(n_lat, share, width), 'lat', 0, 0, tiled=True)]
    dot_general x10 -> x5, matrix products: 57 us -> 11 us  [the longest x1 3.19 us: body(): lax.dot_general(acts, err, (((0,), (0,)), ((), ())), preferred_element_ty...]
    all_to_all x0 -> x4, starting transfers between devices: none -> 38.5 us  [the longest x1 11.8 us: body(): lax.all_to_all(recon.reshape(n_lat, share, width), 'lat', 0, 0, tiled=True)]
    all_gather x0 -> x2, blocking collectives: none -> 27.8 us  [the longest x1 14 us: body(): grad_pre = lax.all_gather(grad_own, 'tok', axis=0, tiled=True)]
    gather x6 -> x0, local copies, waits for them, and re-layouts: 19.1 us -> none  [the longest x1 5.97 us: body(): err_sel = jnp.take(err_full.reshape(rblk, BR, width), row_of, axis=0)]
    psum x1 -> x0, blocking collectives: 18.6 us -> none  [body(): lax.psum(halves.astype(jnp.bfloat16), 'tok').astype(jnp.float32)]
  transfers between devices with their start and end apart: 3 -> 4, of which waited for: 3 -> 4; matrix products, arithmetic and copies ran while one was open for 5% -> 2% of each run, Pallas kernels for 0% -> 0%
where the time goes in v1:
time: 163 us; the launch traced here: 162 us
  waiting for transfers between devices  75.5 us (46%)
  starting transfers between devices  38.5 us (24%)
  blocking collectives  27.8 us (17%)
  matrix products  11 us (7%)
  other arithmetic  4.79 us (3%)
  local copies, waits for them, and re-layouts  3.4 us (2%)
    all_to_all x1, waiting for transfers between devices, body(): lax.all_to_all(recon.reshape(n_lat, share, width), 'lat', 0, 0, tiled=True)  30.2 us
    all_to_all x1, waiting for transfers between devices, body(): lax.all_to_all(jnp.broadcast_to(err_own[None], (n_lat, share, width)), 'l...  28.9 us
    all_gather x1, blocking collectives, body(): grad_pre = lax.all_gather(grad_own, 'tok', axis=0, tiled=True)  14 us
    all_gather x1, blocking collectives, body(): acts = lax.all_gather(acts_own, 'tok', axis=0, tiled=True)  13.8 us
    all_to_all x1, starting transfers between devices, body(): lax.all_to_all(recon.reshape(n_lat, share, width), 'lat', 0, 0, tiled=True)  11.8 us
    all_to_all x1, starting transfers between devices, body(): got = lax.all_to_all(packed, 'tok', 0, 0, tiled=True)  10.5 us
    all_to_all x1, waiting for transfers between devices, body(): got = lax.all_to_all(packed, 'tok', 0, 0, tiled=True)  10.1 us
    all_to_all x1, starting transfers between devices, body(): lax.all_to_all(jnp.broadcast_to(err_own[None], (n_lat, share, width)), 'l...  8.59 us
  transfers between devices with their start and end apart: 4, of which 4 were waited for; matrix products, arithmetic and copies ran while one was open for 2% of the time, Pallas kernels for 0%

profile of v1, /device:TPU:1, one launch (start us, length us, event | category | flops | bytes accessed | tf_op | source)
XLA Modules:
  0.0 162.4 jit_solution(5626988605311592522)
XLA Ops:
  0.6 0.0 copy-start
  0.6 0.0 copy-start.6
  0.7 1.7 %fusion.3 = bf16[512]{0:T(512)(128)(2,1)S(1)} fusion(bf16[512,1152]{1,0:T(8,128)(2,1)} %param.9), kind=kLoop, calls=%fused_computation.8 | loop fusion | flops 1768960 | bytes 1180672 | tf_op jit(solution)/shard_map/reduce_sum | solution.py:38
  2.4 0.0 copy-done
  2.4 0.2 copy-done.6
  2.6 0.8 convolution_convert_fusion.3
  3.5 0.0 copy-start.5
  3.5 0.9 pad_maximum_fusion
  4.4 0.0 copy-start.4
  4.4 10.5 %all-to-all-start = ((bf16[8,80,512]{2,1,0:T(8,128)(2,1)}), bf16[8,80,512]{2,1,0:T(8,128)(2,1)S(1)}, u32[]{:S(2)}, u32[]{:S(2)}) async-start(bf16[8,80,512]{2,1,0:T(8,128)(2,1)} %pad_maximum_fusion), calls=%async_computation | async-start | bytes 1310720 | tf_op jit(solution)/shard_map/all_to_all | solution.py:47
  15.5 0.0 copy-done.5
  15.5 0.1 and_reduce_fusion
  15.6 10.1 %all-to-all-done = bf16[8,80,512]{2,1,0:T(8,128)(2,1)S(1)} async-done(((bf16[8,80,512]{2,1,0:T(8,128)(2,1)}), bf16[8,80,512]{2,1,0:T(8,128)(2,1)S(1)}, u32[]{:S(2)}, u32[]{:S(2)}) %all-to-all-start) | async-done | bytes 655392 | tf_op jit(solution)/shard_map/all_to_all | solution.py:47
  25.8 0.1 convert_reduce_fusion.4
  25.8 0.0 copy-done.4
  25.8 0.0 copy-start.1
  25.8 0.1 fusion.7
  25.9 13.8 %all_gather.6 = bf16[512,512]{1,0:T(8,128)(2,1)S(1)} all-gather(bf16[64,512]{1,0:T(8,128)(2,1)S(1)} %fusion.7), channel_id=1, replica_groups=mesh['lat'=64,'tok'=8] {'tok'}, dimensions={0}, use_global_device_ids=true | all-gather | bytes 589824 | tf_op jit(solution)/shard_map/all_gather | solution.py:56
  39.8 3.1 %fusion.1 = bf16[64,8,1152]{2,1,0:T(8,128)(2,1)} fusion(bf16[512,512]{1,0:T(8,128)(2,1)S(1)} %all_gather.6, bf16[512,1152]{1,0:T(8,128)(2,1)} %param.9), kind=kOutput, calls=%fused_computation.6 | convolution fusion | flops 604569600 | bytes 2883584 | tf_op jit(solution)/shard_map/dot_general | solution.py:58
  42.9 0.0 copy-done.1
  42.9 11.8 %all-to-all-start.1 = ((bf16[64,8,1152]{2,1,0:T(8,128)(2,1)}), bf16[64,8,1152]{2,1,0:T(8,128)(2,1)S(1)}, u32[]{:S(2)}, u32[]{:S(2)}) async-start(bf16[64,8,1152]{2,1,0:T(8,128)(2,1)} %fusion.1), calls=%async_computation.1 | async-start | bytes 2359296 | tf_op jit(solution)/shard_map/all_to_all | solution.py:59
  54.7 30.2 %all-to-all-done.1 = bf16[64,8,1152]{2,1,0:T(8,128)(2,1)S(1)} async-done(((bf16[64,8,1152]{2,1,0:T(8,128)(2,1)}), bf16[64,8,1152]{2,1,0:T(8,128)(2,1)S(1)}, u32[]{:S(2)}, u32[]{:S(2)}) %all-to-all-start.1) | async-done | bytes 1179680 | tf_op jit(solution)/shard_map/all_to_all | solution.py:59
  84.9 0.2 convert_reduce_fusion
  85.1 0.7 subtract_convert_fusion
  85.8 0.0 copy-start.3
  85.8 0.6 copy-done.3
  86.4 1.1 broadcast_in_dim.20
  87.5 8.6 %all-to-all-start.2 = ((bf16[64,8,1152]{2,1,0:T(8,128)(2,1)}), bf16[64,8,1152]{2,1,0:T(8,128)(2,1)S(1)}, u32[]{:S(2)}, u32[]{:S(2)}) async-start(bf16[64,8,1152]{2,1,0:T(8,128)(2,1)} %broadcast_in_dim.20), calls=%async_computation.2 | async-start | bytes 2359296 | tf_op jit(solution)/shard_map/all_to_all | solution.py:62
  96.2 0.1 convert_reduce_fusion.2
  96.3 28.9 %all-to-all-done.2 = bf16[64,8,1152]{2,1,0:T(8,128)(2,1)S(1)} async-done(((bf16[64,8,1152]{2,1,0:T(8,128)(2,1)}), bf16[64,8,1152]{2,1,0:T(8,128)(2,1)S(1)}, u32[]{:S(2)}, u32[]{:S(2)}) %all-to-all-start.2) | async-done | bytes 1179680 | tf_op jit(solution)/shard_map/all_to_all | solution.py:62
  125.2 2.9 %convolution_convert_fusion.2 = bf16[512,512]{1,0:T(8,128)(2,1)} fusion(bf16[512,1152]{1,0:T(8,128)(2,1)} %param.9, bf16[64,8,1152]{2,1,0:T(8,128)(2,1)S(1)} %all-to-all-done.2), kind=kOutput, calls=%fused_computation.10 | convolution fusion | flops 604241920 | bytes 2883584 | tf_op jit(solution)/shard_map/dot_general | solution.py:66
  128.2 7.7 %all-to-all-start.3 = ((bf16[8,64,512]{2,1,0:T(8,128)(2,1)}), bf16[8,64,512]{2,1,0:T(8,128)(2,1)S(1)}, u32[]{:S(2)}, u32[]{:S(2)}) async-start(bf16[8,64,512]{2,1,0:T(8,128)(2,1)} %bitcast.22), calls=%async_computation.3 | async-start | bytes 1048576 | tf_op jit(solution)/shard_map/all_to_all | solution.py:69
  135.8 0.0 copy-start.2
  135.8 3.2 %fusion = bf16[512,1152]{1,0:T(8,128)(2,1)} fusion(bf16[512,512]{1,0:T(8,128)(2,1)S(1)} %all_gather.6, bf16[512,1152]{1,0:T(8,128)(2,1)} %param.9, bf16[64,8,1152]{2,1,0:T(8,128)(2,1)S(1)} %all-to-all-done.2, f32[512]{0:T(512)S(1)} %get-tuple-element.14), kind=kOutput, calls=%fused_computation.1 | convolution fusion | flops 606339072 | bytes 4065280 | tf_op jit(solution)/shard_map/dot_general | solution.py:75
  139.0 6.3 %all-to-all-done.3 = bf16[8,64,512]{2,1,0:T(8,128)(2,1)S(1)} async-done(((bf16[8,64,512]{2,1,0:T(8,128)(2,1)}), bf16[8,64,512]{2,1,0:T(8,128)(2,1)S(1)}, u32[]{:S(2)}, u32[]{:S(2)}) %all-to-all-start.3) | async-done | bytes 524320 | tf_op jit(solution)/shard_map/all_to_all | solution.py:69
  145.3 0.0 copy-start.7
  145.3 0.1 convert_reduce_fusion.3
  145.4 0.0 copy-done.2
  145.4 0.1 select_convert_fusion
  145.5 14.0 %all_gather.7 = bf16[512,512]{1,0:T(8,128)(2,1)S(1)} all-gather(bf16[64,512]{1,0:T(8,128)(2,1)S(1)} %select_convert_fusion), channel_id=1, replica_groups=mesh['lat'=64,'tok'=8] {'tok'}, dimensions={0}, use_global_device_ids=true | all-gather | bytes 589824 | tf_op jit(solution)/shard_map/all_gather | solution.py:72
  159.4 0.7 convert_reduce_fusion.1
  160.1 0.0 copy-done.7
  160.1 0.9 fusion.2
  161.0 1.4 copy.11
  (6 shorter events, 0.1 us)
Async XLA Ops:
  0.6 1.8 %copy-start = (bf16[1152,512]{1,0:T(8,128)(2,1)S(1)}, bf16[1152,512]{1,0:T(8,128)(2,1)}, u32[]{:S(2)}) copy-start(bf16[1152,512]{1,0:T(8,128)(2,1)} %param.7) | copy-start | bytes 3538948
  0.6 2.0 %copy-start.6 = (bf16[512,1152]{1,0:T(8,128)(2,1)S(1)}, bf16[512,1152]{1,0:T(8,128)(2,1)}, u32[]{:S(2)}) copy-start(bf16[512,1152]{1,0:T(8,128)(2,1)} %param.6) | copy-start | bytes 3538948
  3.5 12.0 %copy-start.5 = (s32[1,32]{1,0:T(1,128)S(1)}, s32[1,32]{1,0:T(1,128)}, u32[]{:S(2)}) copy-start(s32[1,32]{1,0:T(1,128)} %param.10) | copy-start | bytes 388
  4.4 21.4 %copy-start.4 = (f32[512]{0:T(512)S(1)}, f32[512]{0:T(512)}, u32[]{:S(2)}) copy-start(f32[512]{0:T(512)} %param.8) | copy-start | bytes 6148
  4.4 21.4 %all-to-all-start = ((bf16[8,80,512]{2,1,0:T(8,128)(2,1)}), bf16[8,80,512]{2,1,0:T(8,128)(2,1)S(1)}, u32[]{:S(2)}, u32[]{:S(2)}) async-start(bf16[8,80,512]{2,1,0:T(8,128)(2,1)} %pad_maximum_fusion), calls=%async_computation | async-start | bytes 1310720 | tf_op jit(solution)/shard_map/all_to_all | solution.py:47
  25.8 17.1 %copy-start.1 = (f32[64,512]{1,0:T(8,128)}, f32[64,512]{1,0:T(8,128)S(1)}, u32[]{:S(2)}) copy-start(f32[64,512]{1,0:T(8,128)S(1)} %convert_reduce_fusion.4) | copy-start | bytes 393220
  42.9 42.0 %all-to-all-start.1 = ((bf16[64,8,1152]{2,1,0:T(8,128)(2,1)}), bf16[64,8,1152]{2,1,0:T(8,128)(2,1)S(1)}, u32[]{:S(2)}, u32[]{:S(2)}) async-start(bf16[64,8,1152]{2,1,0:T(8,128)(2,1)} %fusion.1), calls=%async_computation.1 | async-start | bytes 2359296 | tf_op jit(solution)/shard_map/all_to_all | solution.py:59
  85.8 0.6 copy-start.3
  87.5 37.7 %all-to-all-start.2 = ((bf16[64,8,1152]{2,1,0:T(8,128)(2,1)}), bf16[64,8,1152]{2,1,0:T(8,128)(2,1)S(1)}, u32[]{:S(2)}, u32[]{:S(2)}) async-start(bf16[64,8,1152]{2,1,0:T(8,128)(2,1)} %broadcast_in_dim.20), calls=%async_computation.2 | async-start | bytes 2359296 | tf_op jit(solution)/shard_map/all_to_all | solution.py:62
  128.2 17.2 %all-to-all-start.3 = ((bf16[8,64,512]{2,1,0:T(8,128)(2,1)}), bf16[8,64,512]{2,1,0:T(8,128)(2,1)S(1)}, u32[]{:S(2)}, u32[]{:S(2)}) async-start(bf16[8,64,512]{2,1,0:T(8,128)(2,1)} %bitcast.22), calls=%async_computation.3 | async-start | bytes 1048576 | tf_op jit(solution)/shard_map/all_to_all | solution.py:69
  135.8 9.6 %copy-start.2 = (f32[64,512]{1,0:T(8,128)S(1)}, f32[64,512]{1,0:T(8,128)}, u32[]{:S(2)}) copy-start(f32[64,512]{1,0:T(8,128)} %copy-done.1) | copy-start | bytes 393220
  145.3 14.8 %copy-start.7 = (bf16[512,1152]{1,0:T(8,128)(2,1)S(1)}, bf16[512,1152]{1,0:T(8,128)(2,1)}, u32[]{:S(2)}) copy-start(bf16[512,1152]{1,0:T(8,128)(2,1)} %param.6) | copy-start | bytes 3538948

commit v2 on v1

--- a/solution.py
+++ b/solution.py
@@ -11,6 +11,23 @@
 
 f32 = jnp.float32
 bf16 = jnp.bfloat16
+
+
+def lat_groups(n_lat, n_tok, first):
+    side = round(n_lat**0.5)
+    groups = []
+    for tok in range(n_tok):
+        inner = (tok % 2 == 0) == first
+        for a in range(side):
+            line = [a * side + b if inner else b * side + a for b in range(side)]
+            groups.append([lat * n_tok + tok for lat in line])
+    return groups
+
+
+def exchange(x, groups):
+    return lax.all_to_all(
+        x, ("lat", "tok"), 0, 0, axis_index_groups=groups, tiled=True
+    )
 
 
 def body(tokens, enc_weight, enc_bias, dec_weight, pairs, counts):
@@ -55,24 +72,38 @@
     acts_own = jnp.where(mask, jax.nn.softplus(pre), 0.0).astype(bf16)
     acts = lax.all_gather(acts_own, "tok", axis=0, tiled=True)
 
-    recon = jnp.dot(acts, dec_weight, preferred_element_type=f32).astype(bf16)
-    got = lax.all_to_all(recon.reshape(n_lat, share, width), "lat", 0, 0, tiled=True)
+    side = round(n_lat**0.5)
+    first = lat_groups(n_lat, n_tok, True)
+    second = lat_groups(n_lat, n_tok, False)
+    even = tok % 2 == 0
+
+    def turn(v):
+        v4 = v.reshape(side, side, share, v.shape[-1])
+        return jnp.where(even, v4.transpose(1, 0, 2, 3), v4).reshape(v.shape)
+
+    acts_t = turn(acts)
+    recon = jnp.dot(acts_t, dec_weight, preferred_element_type=f32).astype(bf16)
+    got = exchange(recon.reshape(side, side * share, width), first)
+    line = jnp.sum(got.astype(f32), axis=0).astype(bf16)
+    got = exchange(line.reshape(side, share, width), second)
     x_own = lax.dynamic_slice_in_dim(tokens, lax.axis_index("lat") * share, share, 0)
     err_own = (jnp.sum(got.astype(f32), axis=0) - x_own.astype(f32)).astype(bf16)
-    err = lax.all_to_all(
-        jnp.broadcast_to(err_own[None], (n_lat, share, width)), "lat", 0, 0, tiled=True
-    ).reshape(rows, width)
+    line = exchange(jnp.broadcast_to(err_own[None], (side, share, width)), second)
+    line = line.reshape(1, side * share, width)
+    err = exchange(jnp.broadcast_to(line, (side, side * share, width)), first)
+    err = err.reshape(rows, width)
 
     back = lax.dot_general(
         err, dec_weight, (((1,), (1,)), ((), ())), preferred_element_type=f32
     ).astype(bf16)
+    back = turn(back)
     got = lax.all_to_all(back.reshape(n_tok, own, local_lat), "tok", 0, 0, tiled=True)
     grad_act = jnp.sum(got.astype(f32), axis=0) + PENALTY * total_norm[None, :]
     grad_own = jnp.where(mask, grad_act * jax.nn.sigmoid(pre), 0.0).astype(bf16)
     grad_pre = lax.all_gather(grad_own, "tok", axis=0, tiled=True)
 
     act_sum = jnp.sum(acts.astype(f32), axis=0)
-    dec_data = lax.dot_general(acts, err, (((0,), (0,)), ((), ())), preferred_element_type=f32)
+    dec_data = lax.dot_general(acts_t, err, (((0,), (0,)), ((), ())), preferred_element_type=f32)
     dec_grad = dec_data + PENALTY * (act_sum / own_norm)[:, None] * dec32
     enc_grad = lax.dot_general(tokens, grad_pre, (((0,), (0,)), ((), ())), preferred_element_type=f32)
     bias_grad = jnp.sum(grad_pre.astype(f32), axis=0)

time: 163 us -> 156 us (0.957)
  waiting for transfers between devices: 75.5 us -> 42.9 us
  blocking collectives: 27.8 us -> 60 us
  starting transfers between devices: 38.5 us -> 32.5 us
  matrix products: 11 us -> 8.31 us
  other arithmetic: 4.79 us -> 6.94 us
    all_to_all x2, waiting for transfers between devices: 59.1 us -> 27 us  [exchange(): lax.all_to_all(x, ('lat', 'tok'), 0, 0, axis_index_groups=groups, tiled=T...]
    all_to_all x0 -> x2, blocking collectives: none -> 32 us  [exchange(): lax.all_to_all(x, ('lat', 'tok'), 0, 0, axis_index_groups=groups, tiled=T...]
    all_to_all x2, starting transfers between devices: 20.4 us -> 13.3 us  [exchange(): lax.all_to_all(x, ('lat', 'tok'), 0, 0, axis_index_groups=groups, tiled=T...]
    dot_general x2, matrix products: 6.32 us -> 4.03 us  [the longest x1 3.19 us: body(): lax.dot_general(acts_t, err, (((0,), (0,)), ((), ())), preferred_element_...]
  transfers between devices with their start and end apart: 4 -> 4, of which waited for: 4 -> 4; matrix products, arithmetic and copies ran while one was open for 2% -> 3% of each run, Pallas kernels for 0% -> 0%
where the time goes in v2:
time: 156 us
  blocking collectives  60 us (38%)
  waiting for transfers between devices  42.9 us (28%)
  starting transfers between devices  32.5 us (21%)
  matrix products  8.31 us (5%)
  other arithmetic  6.94 us (4%)
  local copies, waits for them, and re-layouts  3.55 us (2%)
    all_to_all x2, blocking collectives, exchange(): lax.all_to_all(x, ('lat', 'tok'), 0, 0, axis_index_groups=groups, tiled=T...  32 us
    all_to_all x2, waiting for transfers between devices, exchange(): lax.all_to_all(x, ('lat', 'tok'), 0, 0, axis_index_groups=groups, tiled=T...  27 us
    all_gather x1, blocking collectives, body(): acts = lax.all_gather(acts_own, 'tok', axis=0, tiled=True)  14 us
    all_gather x1, blocking collectives, body(): grad_pre = lax.all_gather(grad_own, 'tok', axis=0, tiled=True)  14 us
    all_to_all x2, starting transfers between devices, exchange(): lax.all_to_all(x, ('lat', 'tok'), 0, 0, axis_index_groups=groups, tiled=T...  13.3 us
    all_to_all x1, starting transfers between devices, body(): got = lax.all_to_all(packed, 'tok', 0, 0, tiled=True)  10.5 us
    all_to_all x1, waiting for transfers between devices, body(): got = lax.all_to_all(packed, 'tok', 0, 0, tiled=True)  10.1 us
    all_to_all x1, starting transfers between devices, body(): lax.all_to_all(back.reshape(n_tok, own, local_lat), 'tok', 0, 0, tiled=True)  8.73 us
  transfers between devices with their start and end apart: 4, of which 4 were waited for; matrix products, arithmetic and copies ran while one was open for 3% of the time, Pallas kernels for 0%

profile of v2, /device:TPU:1, one launch (start us, length us, event | category | flops | bytes accessed | tf_op | source)
XLA Modules:
  0.0 155.6 jit_solution(1030104007978796825)
XLA Ops:
  0.6 0.0 copy-start
  0.6 0.0 copy-start.14
  0.7 1.7 %fusion.2 = bf16[512]{0:T(512)(128)(2,1)S(1)} fusion(bf16[512,1152]{1,0:T(8,128)(2,1)} %param.9), kind=kLoop, calls=%fused_computation.7 | loop fusion | flops 1768960 | bytes 1180672 | tf_op jit(solution)/shard_map/reduce_sum | solution.py:55
  2.4 0.0 copy-done
  2.4 0.2 copy-done.14
  2.6 0.8 convolution_convert_fusion.3
  3.5 0.0 copy-start.13
  3.5 0.9 pad_maximum_fusion
  4.4 0.0 copy-start.9
  4.4 10.5 %all-to-all-start = ((bf16[8,80,512]{2,1,0:T(8,128)(2,1)}), bf16[8,80,512]{2,1,0:T(8,128)(2,1)S(1)}, u32[]{:S(2)}, u32[]{:S(2)}) async-start(bf16[8,80,512]{2,1,0:T(8,128)(2,1)} %pad_maximum_fusion), calls=%async_computation | async-start | bytes 1310720 | tf_op jit(solution)/shard_map/all_to_all | solution.py:64
  15.5 0.0 copy-done.13
  15.5 0.1 and_reduce_fusion
  15.6 0.0 copy-start.11
  15.6 10.1 %all-to-all-done = bf16[8,80,512]{2,1,0:T(8,128)(2,1)S(1)} async-done(((bf16[8,80,512]{2,1,0:T(8,128)(2,1)}), bf16[8,80,512]{2,1,0:T(8,128)(2,1)S(1)}, u32[]{:S(2)}, u32[]{:S(2)}) %all-to-all-start) | async-done | bytes 655392 | tf_op jit(solution)/shard_map/all_to_all | solution.py:64
  25.8 0.1 convert_reduce_fusion.3
  25.8 0.0 copy-done.11
  25.8 0.0 copy-start.1
  25.9 0.6 copy-done.1
  26.5 0.0 copy-done.9
  26.5 0.0 copy-start.5
  26.5 0.1 fusion.5
  26.6 14.0 %all_gather.6 = bf16[512,512]{1,0:T(8,128)(2,1)S(1)} all-gather(bf16[64,512]{1,0:T(8,128)(2,1)S(1)} %fusion.5), channel_id=1, replica_groups=mesh['lat'=64,'tok'=8] {'tok'}, dimensions={0}, use_global_device_ids=true | all-gather | bytes 589824 | tf_op jit(solution)/shard_map/all_gather | solution.py:73
  40.5 0.1 copy_select_fusion
  40.6 0.0 copy-start.6
  40.6 0.0 copy-done.5
  40.6 0.8 convolution_convert_fusion.1
  41.5 0.0 copy-done.6
  41.5 21.6 %all_to_all.30 = bf16[8,64,1152]{2,1,0:T(8,128)(2,1)S(1)} all-to-all(bf16[8,64,1152]{2,1,0:T(8,128)(2,1)S(1)} %bitcast.35), channel_id=1, replica_groups={{0,8,16,24,32,40,48,56},{64,72,80,88,96,104,112,120},{128,136,144,152,1..., dimensions={0} | all-to-all | bytes 2359296 | tf_op jit(solution)/shard_map/all_to_all | solution.py:28
  63.0 0.8 reduce_sum.86
  63.9 9.7 %all-to-all-start.2 = ((bf16[8,8,1152]{2,1,0:T(8,128)(2,1)}), bf16[8,8,1152]{2,1,0:T(8,128)(2,1)S(1)}, u32[]{:S(2)}, u32[]{:S(2)}) async-start(bf16[8,8,1152]{2,1,0:T(8,128)(2,1)} %bitcast.36), calls=%async_computation.2 | async-start | bytes 294912 | tf_op jit(solution)/shard_map/all_to_all | solution.py:28
  73.6 8.1 %all-to-all-done.2 = bf16[8,8,1152]{2,1,0:T(8,128)(2,1)S(1)} async-done(((bf16[8,8,1152]{2,1,0:T(8,128)(2,1)}), bf16[8,8,1152]{2,1,0:T(8,128)(2,1)S(1)}, u32[]{:S(2)}, u32[]{:S(2)}) %all-to-all-start.2) | async-done | bytes 147488 | tf_op jit(solution)/shard_map/all_to_all | solution.py:28
  81.7 0.7 subtract_convert_fusion
  82.5 0.0 copy-start.8
  82.5 10.5 %all_to_all.31 = bf16[8,8,1152]{2,1,0:T(8,128)(2,1)S(1)} all-to-all(bf16[8,8,1152]{2,1,0:T(8,128)(2,1)S(1)} %broadcast_in_dim.24), channel_id=1, replica_groups={{0,64,128,192,256,320,384,448},{8,72,136,200,264,328,392,456},{16,80,14..., dimensions={0} | all-to-all | bytes 294912 | tf_op jit(solution)/shard_map/all_to_all | solution.py:28
  93.0 0.0 copy-done.8
  93.0 1.2 broadcast_in_dim.43
  94.1 3.6 %all-to-all-start.4 = ((bf16[8,64,1152]{2,1,0:T(8,128)(2,1)}), bf16[8,64,1152]{2,1,0:T(8,128)(2,1)S(1)}, u32[]{:S(2)}, u32[]{:S(2)}) async-start(bf16[8,64,1152]{2,1,0:T(8,128)(2,1)} %broadcast_in_dim.43), calls=%async_computation.4 | async-start | bytes 2359296 | tf_op jit(solution)/shard_map/all_to_all | solution.py:28
  97.8 0.1 convert_reduce_fusion.1
  97.9 18.9 %all-to-all-done.4 = bf16[8,64,1152]{2,1,0:T(8,128)(2,1)S(1)} async-done(((bf16[8,64,1152]{2,1,0:T(8,128)(2,1)}), bf16[8,64,1152]{2,1,0:T(8,128)(2,1)S(1)}, u32[]{:S(2)}, u32[]{:S(2)}) %all-to-all-start.4) | async-done | bytes 1179680 | tf_op jit(solution)/shard_map/all_to_all | solution.py:28
  116.8 0.0 copy-start.3
  116.8 2.6 %convolution_convert_fusion.2 = bf16[512,512]{1,0:T(8,128)(2,1)S(1)} fusion(bf16[512,1152]{1,0:T(8,128)(2,1)S(1)} %bitcast.33, bf16[512,1152]{1,0:T(8,128)(2,1)} %param.9), kind=kOutput, calls=%fused_computation.8 | convolution fusion | flops 604241920 | bytes 2883584 | tf_op jit(solution)/shard_map/dot_general | solution.py:96
  119.4 0.0 copy-done.3
  119.4 0.0 copy-start.4
  119.4 0.0 copy-start.7
  119.4 0.8 fusion.3
  120.3 8.7 %all-to-all-start.5 = ((bf16[8,64,512]{2,1,0:T(8,128)(2,1)}), bf16[8,64,512]{2,1,0:T(8,128)(2,1)S(1)}, u32[]{:S(2)}, u32[]{:S(2)}) async-start(bf16[8,64,512]{2,1,0:T(8,128)(2,1)} %fusion.3), calls=%async_computation.5 | async-start | bytes 1048576 | tf_op jit(solution)/shard_map/all_to_all | solution.py:100
  129.0 0.6 fusion.9
  129.6 0.0 copy-done.4
  129.6 0.0 copy-done.7
  129.6 0.0 copy-start.2
  129.6 0.0 copy-start.10
  129.6 0.0 copy-start.12
  129.6 3.2 %fusion = bf16[512,1152]{1,0:T(8,128)(2,1)} fusion(bf16[512,512]{1,0:T(8,128)(2,1)S(1)} %bitcast.39, bf16[512,1152]{1,0:T(8,128)(2,1)S(1)} %bitcast.34, bf16[512,1152]{1,0:T(8,128)(2,1)} %param.9, f32[512]{0:T(512)S(1)} %get-tuple-element.14), kind=kOutput, calls=%fused_computation.1 | convolution fusion | flops 606339072 | bytes 4065280 | tf_op jit(solution)/shard_map/dot_general | solution.py:106
  132.8 5.7 %all-to-all-done.5 = bf16[8,64,512]{2,1,0:T(8,128)(2,1)S(1)} async-done(((bf16[8,64,512]{2,1,0:T(8,128)(2,1)}), bf16[8,64,512]{2,1,0:T(8,128)(2,1)S(1)}, u32[]{:S(2)}, u32[]{:S(2)}) %all-to-all-start.5) | async-done | bytes 524320 | tf_op jit(solution)/shard_map/all_to_all | solution.py:100
  138.5 0.1 convert_reduce_fusion.2
  138.6 0.0 copy-done.2
  138.6 0.0 copy-done.10
  138.6 0.0 copy-done.12
  138.6 0.1 select_convert_fusion
  138.7 14.0 %all_gather.7 = bf16[512,512]{1,0:T(8,128)(2,1)S(1)} all-gather(bf16[64,512]{1,0:T(8,128)(2,1)S(1)} %select_convert_fusion), channel_id=1, replica_groups=mesh['lat'=64,'tok'=8] {'tok'}, dimensions={0}, use_global_device_ids=true | all-gather | bytes 589824 | tf_op jit(solution)/shard_map/all_gather | solution.py:103
  152.6 0.7 convert_reduce_fusion
  153.3 0.0 copy-done.15
  153.3 0.9 fusion.1
  154.2 1.4 copy.15
  (8 shorter events, 0.1 us)
Async XLA Ops:
  0.6 1.8 %copy-start = (bf16[1152,512]{1,0:T(8,128)(2,1)S(1)}, bf16[1152,512]{1,0:T(8,128)(2,1)}, u32[]{:S(2)}) copy-start(bf16[1152,512]{1,0:T(8,128)(2,1)} %param.7) | copy-start | bytes 3538948
  0.6 2.0 %copy-start.14 = (bf16[512,1152]{1,0:T(8,128)(2,1)S(1)}, bf16[512,1152]{1,0:T(8,128)(2,1)}, u32[]{:S(2)}) copy-start(bf16[512,1152]{1,0:T(8,128)(2,1)} %param.6) | copy-start | bytes 3538948
  3.5 12.0 %copy-start.13 = (s32[1,32]{1,0:T(1,128)S(1)}, s32[1,32]{1,0:T(1,128)}, u32[]{:S(2)}) copy-start(s32[1,32]{1,0:T(1,128)} %param.10) | copy-start | bytes 388
  4.4 22.1 %copy-start.9 = (f32[512]{0:T(512)S(1)}, f32[512]{0:T(512)}, u32[]{:S(2)}) copy-start(f32[512]{0:T(512)} %param.8) | copy-start | bytes 6148
  4.4 21.4 %all-to-all-start = ((bf16[8,80,512]{2,1,0:T(8,128)(2,1)}), bf16[8,80,512]{2,1,0:T(8,128)(2,1)S(1)}, u32[]{:S(2)}, u32[]{:S(2)}) async-start(bf16[8,80,512]{2,1,0:T(8,128)(2,1)} %pad_maximum_fusion), calls=%async_computation | async-start | bytes 1310720 | tf_op jit(solution)/shard_map/all_to_all | solution.py:64
  15.6 10.2 %copy-start.11 = (pred[512]{0:T(512)(128)(4,1)}, pred[512]{0:T(512)(128)(4,1)S(1)}, u32[]{:S(2)}) copy-start(pred[512]{0:T(512)(128)(4,1)S(1)} %and_reduce_fusion) | copy-start | bytes 1540
  25.8 0.7 copy-start.1
  26.5 14.1 %copy-start.5 = (bf16[512,1152]{1,0:T(8,128)(2,1)S(1)}, bf16[512,1152]{1,0:T(8,128)(2,1)}, u32[]{:S(2)}) copy-start(bf16[512,1152]{1,0:T(8,128)(2,1)} %param.9) | copy-start | bytes 3538948
  40.6 0.9 copy-start.6
  63.9 17.8 %all-to-all-start.2 = ((bf16[8,8,1152]{2,1,0:T(8,128)(2,1)}), bf16[8,8,1152]{2,1,0:T(8,128)(2,1)S(1)}, u32[]{:S(2)}, u32[]{:S(2)}) async-start(bf16[8,8,1152]{2,1,0:T(8,128)(2,1)} %bitcast.36), calls=%async_computation.2 | async-start | bytes 294912 | tf_op jit(solution)/shard_map/all_to_all | solution.py:28
  82.5 10.5 %copy-start.8 = (bf16[8,1152]{1,0:T(8,128)(2,1)}, bf16[8,1152]{1,0:T(8,128)(2,1)S(1)}, u32[]{:S(2)}) copy-start(bf16[8,1152]{1,0:T(8,128)(2,1)S(1)} %subtract_convert_fusion) | copy-start | bytes 55300
  94.1 22.7 %all-to-all-start.4 = ((bf16[8,64,1152]{2,1,0:T(8,128)(2,1)}), bf16[8,64,1152]{2,1,0:T(8,128)(2,1)S(1)}, u32[]{:S(2)}, u32[]{:S(2)}) async-start(bf16[8,64,1152]{2,1,0:T(8,128)(2,1)} %broadcast_in_dim.43), calls=%async_computation.4 | async-start | bytes 2359296 | tf_op jit(solution)/shard_map/all_to_all | solution.py:28
  116.8 2.6 %copy-start.3 = (bf16[8,64,1152]{2,1,0:T(8,128)(2,1)}, bf16[8,64,1152]{2,1,0:T(8,128)(2,1)S(1)}, u32[]{:S(2)}) copy-start(bf16[8,64,1152]{2,1,0:T(8,128)(2,1)S(1)} %all-to-all-done.4) | copy-start | bytes 3538948
  119.4 10.2 %copy-start.4 = (bf16[8,64,1152]{2,1,0:T(8,128)(2,1)S(1)}, bf16[8,64,1152]{2,1,0:T(8,128)(2,1)}, u32[]{:S(2)}) copy-start(bf16[8,64,1152]{2,1,0:T(8,128)(2,1)} %copy-done.3) | copy-start | bytes 3538948
  119.4 10.2 %copy-start.7 = (bf16[8,8,8,512]{3,2,1,0:T(8,128)(2,1)S(1)}, bf16[8,8,8,512]{3,2,1,0:T(8,128)(2,1)}, u32[]{:S(2)}) copy-start(bf16[8,8,8,512]{3,2,1,0:T(8,128)(2,1)} %copy-done.6) | copy-start | bytes 1572868
  120.3 18.2 %all-to-all-start.5 = ((bf16[8,64,512]{2,1,0:T(8,128)(2,1)}), bf16[8,64,512]{2,1,0:T(8,128)(2,1)S(1)}, u32[]{:S(2)}, u32[]{:S(2)}) async-start(bf16[8,64,512]{2,1,0:T(8,128)(2,1)} %fusion.3), calls=%async_computation.5 | async-start | bytes 1048576 | tf_op jit(solution)/shard_map/all_to_all | solution.py:100
  129.6 9.0 %copy-start.2 = (f32[64,512]{1,0:T(8,128)S(1)}, f32[64,512]{1,0:T(8,128)}, u32[]{:S(2)}) copy-start(f32[64,512]{1,0:T(8,128)} %copy-done.1) | copy-start | bytes 393220
  129.6 9.0 %copy-start.10 = (f32[512]{0:T(512)S(1)}, f32[512]{0:T(512)}, u32[]{:S(2)}) copy-start(f32[512]{0:T(512)} %get-tuple-element.15) | copy-start | bytes 6148
  129.6 9.0 %copy-start.12 = (pred[512]{0:T(512)(128)(4,1)S(1)}, pred[512]{0:T(512)(128)(4,1)}, u32[]{:S(2)}) copy-start(pred[512]{0:T(512)(128)(4,1)} %copy-done.11) | copy-start | bytes 1540
  138.5 14.8 %copy-start.15 = (bf16[512,1152]{1,0:T(8,128)(2,1)S(1)}, bf16[512,1152]{1,0:T(8,128)(2,1)}, u32[]{:S(2)}) copy-start(bf16[512,1152]{1,0:T(8,128)(2,1)} %param.6) | copy-start | bytes 3538948

commit v3 on v1

v3 whole, which is shorter than its diff:
```python
import jax
import jax.numpy as jnp
from jax import lax
from jax.sharding import PartitionSpec as P

BR = 128
BL = 64
PENALTY = 0.3
EPSILON = 1e-06
EXTRA = 8

f32 = jnp.float32
bf16 = jnp.bfloat16


def lat_groups(n_lat, n_tok):
    side = round(n_lat**0.5)
    quads = side // 2
    big, small = [], []
    for tok in range(n_tok):
        swap = tok % 2 == 1

        def device(a, p, b):
            pair = 2 * a + p
            lat = b * side + pair if swap else pair * side + b
            return lat * n_tok + tok

        for a in range(quads):
            big.append([device(a, p, b) for p in range(2) for b in range(side)])
        for p in range(2):
            for b in range(side):
                small.append([device(a, p, b) for a in range(quads)])
    return big, small


def exchange(x, axis, groups):
    return lax.all_to_all(x, axis, 0, 0, axis_index_groups=groups, tiled=True)


def body(tokens, enc_weight, enc_bias, dec_weight, pairs, counts):
    rows, width = tokens.shape
    local_lat = enc_weight.shape[1]
    nblk = local_lat // BL
    slots = pairs.shape[1]
    n_lat = lax.axis_size("lat")
    n_tok = lax.axis_size("tok")
    lat = lax.axis_index("lat")
    tok = lax.axis_index("tok")
    half = tok * 2 // n_tok
    own = rows // n_tok
    share = rows // n_lat
    side = round(n_lat**0.5)
    quads = side // 2
    n_x = n_tok // 2
    even = tok % 2 == 0
    both = ("lat", "tok")
    big, small = lat_groups(n_lat, n_tok)
    x_groups = [[2 * x + c for x in range(n_x)] for c in range(2)]
    c_groups = [[2 * x, 2 * x + 1] for x in range(n_x)]

    def gather_tok(v):
        spread = jnp.broadcast_to(v[None], (n_x,) + v.shape)
        got = exchange(spread, "tok", x_groups)
        return lax.all_gather(
            got.reshape(n_x * own, local_lat), "tok", axis_index_groups=c_groups, axis=0, tiled=True
        )

    codes = pairs[0]
    valid = jnp.arange(slots, dtype=jnp.int32) < counts[0]
    g_own = tok * own // BR
    hit = valid[:, None] & (
        codes[:, None] == g_own * nblk + jnp.arange(local_lat, dtype=jnp.int32)[None, :] // BL
    )
    mask = jnp.any(hit, axis=0)[None, :]

    part = jnp.dot(tokens, enc_weight, preferred_element_type=f32).astype(bf16)
    got = exchange(part.reshape(n_tok, own, local_lat), "tok", None)
    pre = jnp.sum(got.astype(f32), axis=0) + enc_bias[None, :]
    acts_own = jnp.where(mask, jax.nn.softplus(pre), 0.0).astype(bf16)
    acts = gather_tok(acts_own)

    acts_even = acts.reshape(2, n_x, side, share, local_lat).transpose(0, 2, 1, 3, 4)
    acts_odd = acts.reshape(2, n_x, quads, 2, share, local_lat).transpose(3, 1, 0, 2, 4, 5)
    acts_t = jnp.where(
        even, acts_even.reshape(rows, local_lat), acts_odd.reshape(rows, local_lat)
    )

    recon = jnp.dot(acts_t, dec_weight, preferred_element_type=f32).astype(bf16)
    got = exchange(recon.reshape(2 * side, quads * share, width), both, big)
    line = jnp.sum(got.astype(f32), axis=0).astype(bf16)
    got = exchange(jnp.broadcast_to(line[None], (quads,) + line.shape), both, small)
    y, z = lat // side, lat % side
    x_rows = []
    for a in range(quads):
        at = jnp.where(even, (2 * a + y % 2) * side + z, y * side + 2 * a + z % 2)
        x_rows.append(lax.dynamic_slice_in_dim(tokens, at * share, share, 0))
    x_line = jnp.concatenate(x_rows, axis=0)
    err_line = (jnp.sum(got.astype(f32), axis=0) - x_line.astype(f32)).astype(bf16)
    a_own = jnp.where(even, y, z) // 2
    err_own = lax.dynamic_slice_in_dim(err_line, a_own * share, share, 0)
    err = exchange(jnp.broadcast_to(err_line[None], (2 * side,) + err_line.shape), both, big)
    err = err.reshape(rows, width)

    back = lax.dot_general(
        err, dec_weight, (((1,), (1,)), ((), ())), preferred_element_type=f32
    ).astype(bf16)
    back_even = back.reshape(2, side, quads, share, local_lat).transpose(2, 0, 1, 3, 4)
    back_odd = back.reshape(2, side, quads, share, local_lat).transpose(1, 2, 0, 3, 4)
    shape = (n_tok, own, local_lat)
    back = jnp.where(even, back_even.reshape(shape), back_odd.reshape(shape))
    dec32 = dec_weight.astype(f32)
    squares = jnp.sum(dec32 * dec32, axis=1).astype(bf16)
    packed = jnp.concatenate(
        [back, jnp.broadcast_to(squares[None, None, :], (n_tok, EXTRA, local_lat))], axis=1
    )
    got = exchange(packed, "tok", None)
    sq = got[:, own].astype(f32)
    norm_a = jnp.sqrt(jnp.sum(sq[: n_tok // 2], axis=0) + EPSILON)
    norm_b = jnp.sqrt(jnp.sum(sq[n_tok // 2 :], axis=0) + EPSILON)
    own_norm = jnp.where(half == 0, norm_a, norm_b)
    grad_act = jnp.sum(got[:, :own].astype(f32), axis=0) + PENALTY * (norm_a + norm_b)[None, :]
    grad_own = jnp.where(mask, grad_act * jax.nn.sigmoid(pre), 0.0).astype(bf16)
    grad_pre = gather_tok(grad_own)

    act_sum = jnp.sum(acts.astype(f32), axis=0)
    dec_data = lax.dot_general(acts_t, err, (((0,), (0,)), ((), ())), preferred_element_type=f32)
    dec_grad = dec_data + PENALTY * (act_sum / own_norm)[:, None] * dec32
    tokens_t = tokens.reshape(n_x, 2, own, width).transpose(1, 0, 2, 3).reshape(rows, width)
    enc_grad = lax.dot_general(
        tokens_t, grad_pre, (((0,), (0,)), ((), ())), preferred_element_type=f32
    )
    bias_grad = jnp.sum(grad_pre.astype(f32), axis=0)
    return err_own, enc_grad.astype(bf16), dec_grad.astype(bf16), bias_grad


def solution(mesh):
    return jax.shard_map(
        body,
        mesh=mesh,
        in_specs=(
            P(None, "tok"),
            P("tok", "lat"),
            P("lat"),
            P("lat", "tok"),
            P("lat", None),
            P("lat"),
        ),
        out_specs=(P("lat", "tok"), P("tok", "lat"), P("lat", "tok"), P("lat")),
        check_vma=False,
    )
```

time: 163 us -> 155 us (0.951)
  waiting for transfers between devices: 75.5 us -> 53.4 us
  local copies, waits for them, and re-layouts: 3.4 us -> 12.2 us
  blocking collectives: 27.8 us -> 34.9 us
  starting transfers between devices: 38.5 us -> 35.9 us
    all_to_all x0 -> x1, blocking collectives: none -> 27.2 us  [exchange(): return lax.all_to_all(x, axis, 0, 0, axis_index_groups=groups, tiled=True)]
    all_to_all x4 -> x6, waiting for transfers between devices: 75.5 us -> 53.4 us  [exchange(): return lax.all_to_all(x, axis, 0, 0, axis_index_groups=groups, tiled=True)]
    all_gather x2, blocking collectives: 27.8 us -> 7.7 us  [gather_tok(): lax.all_gather(got.reshape(n_x * own, local_lat), 'tok', axis_index_group...]
    unnamed x17, local copies, waits for them, and re-layouts: 2.29 us -> 5.34 us
    all_to_all x4 -> x6, starting transfers between devices: 38.5 us -> 35.9 us  [exchange(): return lax.all_to_all(x, axis, 0, 0, axis_index_groups=groups, tiled=True)]
    broadcast_in_dim x1 -> x4, local copies, waits for them, and re-layouts: 1.1 us -> 3.28 us  [the longest x2 1.44 us: gather_tok(): spread = jnp.broadcast_to(v[None], (n_x,) + v.shape)]
    dynamic_slice x0 -> x2, local copies, waits for them, and re-layouts: none -> 2.11 us  [the longest x1 1.33 us: body(): err_own = lax.dynamic_slice_in_dim(err_line, a_own * share, share, 0)]
    dot_general x1, matrix products: 0.84 us -> 2.91 us  [body(): part = jnp.dot(tokens, enc_weight, preferred_element_type=f32).astype(bf16)]
  transfers between devices with their start and end apart: 4 -> 6, of which waited for: 4 -> 6; matrix products, arithmetic and copies ran while one was open for 2% -> 6% of each run, Pallas kernels for 0% -> 0%
where the time goes in v3:
time: 155 us; the launch traced here: 153 us
  waiting for transfers between devices  53.4 us (34%)
  starting transfers between devices  35.9 us (23%)
  blocking collectives  34.9 us (23%)
  local copies, waits for them, and re-layouts  12.2 us (8%)
  matrix products  11.3 us (7%)
  other arithmetic  4.29 us (3%)
  between operations  1.59 us (1%)
    all_to_all x6, waiting for transfers between devices, exchange(): return lax.all_to_all(x, axis, 0, 0, axis_index_groups=groups, tiled=True)  53.4 us
    all_to_all x6, starting transfers between devices, exchange(): return lax.all_to_all(x, axis, 0, 0, axis_index_groups=groups, tiled=True)  35.9 us
    all_to_all x1, blocking collectives, exchange(): return lax.all_to_all(x, axis, 0, 0, axis_index_groups=groups, tiled=True)  27.2 us
    all_gather x2, blocking collectives, gather_tok(): lax.all_gather(got.reshape(n_x * own, local_lat), 'tok', axis_index_group...  7.7 us
    unnamed x17, local copies, waits for them, and re-layouts  5.34 us
    dot_general x1, matrix products, body(): lax.dot_general(acts_t, err, (((0,), (0,)), ((), ())), preferred_element_...  3.51 us
  transfers between devices with their start and end apart: 6, of which 6 were waited for; matrix products, arithmetic and copies ran while one was open for 6% of the time, Pallas kernels for 0%

profile of v3, /device:TPU:1, one launch (start us, length us, event | category | flops | bytes accessed | tf_op | source)
XLA Modules:
  0.0 153.5 jit_solution(5584330624992696649)
XLA Ops:
  0.6 0.0 copy-start
  0.6 0.0 copy-start.7
  0.7 1.3 copy-done
  1.9 2.9 %convolution_convert_fusion.3 = bf16[512,512]{1,0:T(8,128)(2,1)} fusion(bf16[512,1152]{1,0:T(8,128)(2,1)} %param.6, bf16[1152,512]{1,0:T(8,128)(2,1)S(1)} %copy-done), kind=kOutput, calls=%fused_computation.9 | convolution fusion | flops 604241920 | bytes 2883584 | tf_op jit(solution)/shard_map/dot_general | solution.py:76
  4.8 0.0 copy-start.6
  4.8 10.4 %all-to-all-start = ((bf16[8,64,512]{2,1,0:T(8,128)(2,1)}), bf16[8,64,512]{2,1,0:T(8,128)(2,1)S(1)}, u32[]{:S(2)}, u32[]{:S(2)}) async-start(bf16[8,64,512]{2,1,0:T(8,128)(2,1)} %bitcast.2), calls=%async_computation | async-start | bytes 1048576 | tf_op jit(solution)/shard_map/all_to_all | solution.py:37
  15.9 0.0 copy-done.7
  15.9 0.1 and_reduce_fusion
  16.0 8.7 %all-to-all-done = bf16[8,64,512]{2,1,0:T(8,128)(2,1)S(1)} async-done(((bf16[8,64,512]{2,1,0:T(8,128)(2,1)}), bf16[8,64,512]{2,1,0:T(8,128)(2,1)S(1)}, u32[]{:S(2)}, u32[]{:S(2)}) %all-to-all-start) | async-done | bytes 524320 | tf_op jit(solution)/shard_map/all_to_all | solution.py:37
  24.7 0.1 convert_reduce_fusion.3
  24.8 0.0 copy-done.6
  24.8 0.1 fusion.4
  24.9 0.7 broadcast_in_dim.25
  25.6 3.4 %all-to-all-start.1 = ((bf16[4,64,512]{2,1,0:T(8,128)(2,1)}), bf16[4,64,512]{2,1,0:T(8,128)(2,1)S(1)}, u32[]{:S(2)}, u32[]{:S(2)}) async-start(bf16[4,64,512]{2,1,0:T(8,128)(2,1)} %broadcast_in_dim.25), calls=%async_computation.1 | async-start | bytes 524288 | tf_op jit(solution)/shard_map/all_to_all | solution.py:37
  29.1 5.5 %all-to-all-done.1 = bf16[4,64,512]{2,1,0:T(8,128)(2,1)S(1)} async-done(((bf16[4,64,512]{2,1,0:T(8,128)(2,1)}), bf16[4,64,512]{2,1,0:T(8,128)(2,1)S(1)}, u32[]{:S(2)}, u32[]{:S(2)}) %all-to-all-start.1) | async-done | bytes 262176 | tf_op jit(solution)/shard_map/all_to_all | solution.py:37
  34.6 3.9 %all_gather.6 = bf16[512,512]{1,0:T(8,128)(2,1)S(1)} all-gather(bf16[256,512]{1,0:T(8,128)(2,1)S(1)} %bitcast.55), channel_id=1, replica_groups={{0,1},{2,3},{4,5},{6,7},{8,9},{10,11},{12,13},{14,15},{16,17},{18,19},{..., dimensions={0}, use_global_device_ids=true | all-gather | bytes 786432 | tf_op jit(solution)/shard_map/all_gather | solution.py:64
  38.5 0.0 copy-start.3
  38.5 0.1 copy.24
  38.6 0.1 bitcast_select_fusion.1
  38.7 1.1 copy-done.3
  39.8 0.8 convolution_convert_fusion.1
  40.6 27.2 %all_to_all.35 = bf16[16,32,1152]{2,1,0:T(8,128)(2,1)S(1)} all-to-all(bf16[16,32,1152]{2,1,0:T(8,128)(2,1)S(1)} %bitcast.54), channel_id=1, replica_groups={{0,8,16,24,32,40,48,56,64,72,80,88,96,104,112,120},{128,136,144,152,160..., dimensions={0} | all-to-all | bytes 2359296 | tf_op jit(solution)/shard_map/all_to_all | solution.py:37
  67.8 0.2 reduce_sum.85
  67.9 0.7 broadcast_in_dim.26
  68.7 10.7 %all-to-all-start.3 = ((bf16[4,32,1152]{2,1,0:T(8,128)(2,1)}), bf16[4,32,1152]{2,1,0:T(8,128)(2,1)S(1)}, u32[]{:S(2)}, u32[]{:S(2)}) async-start(bf16[4,32,1152]{2,1,0:T(8,128)(2,1)} %broadcast_in_dim.26), calls=%async_computation.3 | async-start | bytes 589824 | tf_op jit(solution)/shard_map/all_to_all | solution.py:37
  79.3 0.8 constant_dynamic-slice_fusion.4
  80.1 7.4 %all-to-all-done.3 = bf16[4,32,1152]{2,1,0:T(8,128)(2,1)S(1)} async-done(((bf16[4,32,1152]{2,1,0:T(8,128)(2,1)}), bf16[4,32,1152]{2,1,0:T(8,128)(2,1)S(1)}, u32[]{:S(2)}, u32[]{:S(2)}) %all-to-all-start.3) | async-done | bytes 294944 | tf_op jit(solution)/shard_map/all_to_all | solution.py:37
  87.6 0.0 copy-start.5
  87.6 0.6 copy-done.5
  88.3 1.1 broadcast_in_dim.27
  89.4 0.0 copy-start.1
  89.4 4.5 %all-to-all-start.4 = ((bf16[16,32,1152]{2,1,0:T(8,128)(2,1)}), bf16[16,32,1152]{2,1,0:T(8,128)(2,1)}, u32[]{:S(2)}, u32[]{:S(2)}) async-start(bf16[16,32,1152]{2,1,0:T(8,128)(2,1)} %broadcast_in_dim.27), calls=%async_computation.4 | async-start | bytes 2359296 | tf_op jit(solution)/shard_map/all_to_all | solution.py:37
  93.9 0.0 copy-done.1
  93.9 1.1 copy.27
  95.0 0.0 copy-start.4
  95.0 1.7 %fusion.2 = bf16[512]{0:T(512)(128)(2,1)S(1)} fusion(bf16[512,1152]{1,0:T(8,128)(2,1)} %param.9), kind=kLoop, calls=%fused_computation.7 | loop fusion | flops 1768960 | bytes 1180672 | tf_op jit(solution)/shard_map/reduce_sum | solution.py:112
  96.7 0.1 copy.28
  96.8 21.1 %all-to-all-done.4 = bf16[16,32,1152]{2,1,0:T(8,128)(2,1)} async-done(((bf16[16,32,1152]{2,1,0:T(8,128)(2,1)}), bf16[16,32,1152]{2,1,0:T(8,128)(2,1)}, u32[]{:S(2)}, u32[]{:S(2)}) %all-to-all-start.4) | async-done | bytes 1179680 | tf_op jit(solution)/shard_map/all_to_all | solution.py:37
  117.8 0.0 copy-done.4
  117.8 2.1 %convolution_convert_fusion.2 = bf16[512,512]{1,0:T(8,128)(2,1)S(1)} fusion(bf16[512,1152]{1,0:T(8,128)(2,1)} %bitcast.11, bf16[512,1152]{1,0:T(8,128)(2,1)S(1)} %copy-done.4), kind=kOutput, calls=%fused_computation.8 | convolution fusion | flops 604241920 | bytes 2883584 | tf_op jit(solution)/shard_map/dot_general | solution.py:104
  120.0 0.1 copy.26
  120.1 0.1 bitcast_select_fusion
  120.2 0.9 pad_maximum_fusion
  121.1 3.5 %all-to-all-start.5 = ((bf16[8,72,512]{2,1,0:T(8,128)(2,1)}), bf16[8,72,512]{2,1,0:T(8,128)(2,1)S(1)}, u32[]{:S(2)}, u32[]{:S(2)}) async-start(bf16[8,72,512]{2,1,0:T(8,128)(2,1)} %pad_maximum_fusion), calls=%async_computation.5 | async-start | bytes 1179648 | tf_op jit(solution)/shard_map/all_to_all | solution.py:37
  124.6 0.1 broadcast_select_fusion
  124.7 0.1 convert_reduce_fusion.1
  124.8 1.3 constant_dynamic-slice_fusion
  126.2 8.6 %all-to-all-done.5 = bf16[8,72,512]{2,1,0:T(8,128)(2,1)S(1)} async-done(((bf16[8,72,512]{2,1,0:T(8,128)(2,1)}), bf16[8,72,512]{2,1,0:T(8,128)(2,1)S(1)}, u32[]{:S(2)}, u32[]{:S(2)}) %all-to-all-start.5) | async-done | bytes 589856 | tf_op jit(solution)/shard_map/all_to_all | solution.py:37
  134.9 0.1 convert_reduce_fusion.2
  134.9 0.1 select_convert_fusion
  135.0 0.7 broadcast_in_dim.29
  135.7 3.4 %all-to-all-start.6 = ((bf16[4,64,512]{2,1,0:T(8,128)(2,1)}), bf16[4,64,512]{2,1,0:T(8,128)(2,1)S(1)}, u32[]{:S(2)}, u32[]{:S(2)}) async-start(bf16[4,64,512]{2,1,0:T(8,128)(2,1)} %broadcast_in_dim.29), calls=%async_computation.6 | async-start | bytes 524288 | tf_op jit(solution)/shard_map/all_to_all | solution.py:37
  139.1 3.5 %fusion = bf16[512,1152]{1,0:T(8,128)(2,1)} fusion(bf16[512,512]{1,0:T(8,128)(2,1)S(1)} %bitcast.57, bf16[512,1152]{1,0:T(8,128)(2,1)} %bitcast.11, bf16[512,1152]{1,0:T(8,128)(2,1)} %param.9, f32[512]{0:T(512)S(1)} %get-tuple-element.26), kind=kOutput, calls=%fused_computation.1 | convolution fusion | flops 606339072 | bytes 4065280 | tf_op jit(solution)/shard_map/dot_general | solution.py:126
  142.6 0.0 copy-start.2
  142.6 2.0 %all-to-all-done.6 = bf16[4,64,512]{2,1,0:T(8,128)(2,1)S(1)} async-done(((bf16[4,64,512]{2,1,0:T(8,128)(2,1)}), bf16[4,64,512]{2,1,0:T(8,128)(2,1)S(1)}, u32[]{:S(2)}, u32[]{:S(2)}) %all-to-all-start.6) | async-done | bytes 262176 | tf_op jit(solution)/shard_map/all_to_all | solution.py:37
  144.7 3.9 %all_gather.7 = bf16[512,512]{1,0:T(8,128)(2,1)S(1)} all-gather(bf16[256,512]{1,0:T(8,128)(2,1)S(1)} %bitcast.56), channel_id=1, replica_groups={{0,1},{2,3},{4,5},{6,7},{8,9},{10,11},{12,13},{14,15},{16,17},{18,19},{..., dimensions={0}, use_global_device_ids=true | all-gather | bytes 786432 | tf_op jit(solution)/shard_map/all_gather | solution.py:64
  148.5 0.7 convert_reduce_fusion
  149.2 0.0 copy-done.2
  149.2 1.9 %fusion.1 = bf16[1152,512]{0,1:T(8,128)(2,1)} fusion(bf16[512,512]{1,0:T(8,128)(2,1)S(1)} %all_gather.7, bf16[512,1152]{1,0:T(8,128)(2,1)S(1)} %bitcast.53), kind=kOutput, calls=%fused_computation.6 | convolution fusion | flops 604569600 | bytes 2883584 | tf_op jit(solution)/shard_map/dot_general | solution.py:129
  151.1 2.4 %copy.30 = bf16[1152,512]{1,0:T(8,128)(2,1)} copy(bf16[1152,512]{0,1:T(8,128)(2,1)} %fusion.1) | data formatting | bytes 2359296
  (11 shorter events, 0.3 us)
Async XLA Ops:
  0.6 1.3 copy-start
  0.6 15.3 %copy-start.7 = (s32[1,32]{1,0:T(1,128)S(1)}, s32[1,32]{1,0:T(1,128)}, u32[]{:S(2)}) copy-start(s32[1,32]{1,0:T(1,128)} %param.10) | copy-start | bytes 388
  4.8 20.0 %copy-start.6 = (f32[512]{0:T(512)S(1)}, f32[512]{0:T(512)}, u32[]{:S(2)}) copy-start(f32[512]{0:T(512)} %param.8) | copy-start | bytes 6148
  4.8 19.9 %all-to-all-start = ((bf16[8,64,512]{2,1,0:T(8,128)(2,1)}), bf16[8,64,512]{2,1,0:T(8,128)(2,1)S(1)}, u32[]{:S(2)}, u32[]{:S(2)}) async-start(bf16[8,64,512]{2,1,0:T(8,128)(2,1)} %bitcast.2), calls=%async_computation | async-start | bytes 1048576 | tf_op jit(solution)/shard_map/all_to_all | solution.py:37
  25.6 8.9 %all-to-all-start.1 = ((bf16[4,64,512]{2,1,0:T(8,128)(2,1)}), bf16[4,64,512]{2,1,0:T(8,128)(2,1)S(1)}, u32[]{:S(2)}, u32[]{:S(2)}) async-start(bf16[4,64,512]{2,1,0:T(8,128)(2,1)} %broadcast_in_dim.25), calls=%async_computation.1 | async-start | bytes 524288 | tf_op jit(solution)/shard_map/all_to_all | solution.py:37
  38.5 1.3 copy-start.3
  68.7 18.9 %all-to-all-start.3 = ((bf16[4,32,1152]{2,1,0:T(8,128)(2,1)}), bf16[4,32,1152]{2,1,0:T(8,128)(2,1)S(1)}, u32[]{:S(2)}, u32[]{:S(2)}) async-start(bf16[4,32,1152]{2,1,0:T(8,128)(2,1)} %broadcast_in_dim.26), calls=%async_computation.3 | async-start | bytes 589824 | tf_op jit(solution)/shard_map/all_to_all | solution.py:37
  87.6 0.6 copy-start.5
  89.4 4.6 %copy-start.1 = (bf16[512,1152]{1,0:T(8,128)(2,1)S(1)}, bf16[512,1152]{1,0:T(8,128)(2,1)}, u32[]{:S(2)}) copy-start(bf16[512,1152]{1,0:T(8,128)(2,1)} %param.6) | copy-start | bytes 3538948
  89.4 28.5 %all-to-all-start.4 = ((bf16[16,32,1152]{2,1,0:T(8,128)(2,1)}), bf16[16,32,1152]{2,1,0:T(8,128)(2,1)}, u32[]{:S(2)}, u32[]{:S(2)}) async-start(bf16[16,32,1152]{2,1,0:T(8,128)(2,1)} %broadcast_in_dim.27), calls=%async_computation.4 | async-start | bytes 2359296 | tf_op jit(solution)/shard_map/all_to_all | solution.py:37
  95.0 22.8 %copy-start.4 = (bf16[512,1152]{1,0:T(8,128)(2,1)S(1)}, bf16[512,1152]{1,0:T(8,128)(2,1)}, u32[]{:S(2)}) copy-start(bf16[512,1152]{1,0:T(8,128)(2,1)} %param.9) | copy-start | bytes 3538948
  121.1 13.7 %all-to-all-start.5 = ((bf16[8,72,512]{2,1,0:T(8,128)(2,1)}), bf16[8,72,512]{2,1,0:T(8,128)(2,1)S(1)}, u32[]{:S(2)}, u32[]{:S(2)}) async-start(bf16[8,72,512]{2,1,0:T(8,128)(2,1)} %pad_maximum_fusion), calls=%async_computation.5 | async-start | bytes 1179648 | tf_op jit(solution)/shard_map/all_to_all | solution.py:37
  135.7 8.9 %all-to-all-start.6 = ((bf16[4,64,512]{2,1,0:T(8,128)(2,1)}), bf16[4,64,512]{2,1,0:T(8,128)(2,1)S(1)}, u32[]{:S(2)}, u32[]{:S(2)}) async-start(bf16[4,64,512]{2,1,0:T(8,128)(2,1)} %broadcast_in_dim.29), calls=%async_computation.6 | async-start | bytes 524288 | tf_op jit(solution)/shard_map/all_to_all | solution.py:37
  142.6 6.6 %copy-start.2 = (bf16[2,4,64,1152]{3,2,1,0:T(8,128)(2,1)S(1)}, bf16[2,4,64,1152]{3,2,1,0:T(8,128)(2,1)}, u32[]{:S(2)}) copy-start(bf16[2,4,64,1152]{3,2,1,0:T(8,128)(2,1)} %copy.27) | copy-start | bytes 3538948

commit v4 on v3

v4 whole, which is shorter than its diff:
```python
import jax
import jax.numpy as jnp
from jax import lax
from jax.experimental import pallas as pl
from jax.experimental.pallas import tpu as pltpu
from jax.sharding import PartitionSpec as P

BR = 128
BL = 64
PENALTY = 0.3
EPSILON = 1e-06
EXTRA = 8

f32 = jnp.float32
bf16 = jnp.bfloat16


def lat_groups(n_lat, n_tok):
    side = round(n_lat**0.5)
    quads = side // 2
    big, near, far = [], [], []
    for tok in range(n_tok):
        swap = tok % 2 == 1

        def device(a, p, b):
            pair = 2 * a + p
            lat = b * side + pair if swap else pair * side + b
            return lat * n_tok + tok

        for a in range(quads):
            big.append([device(a, p, b) for p in range(2) for b in range(side)])
        for p in range(2):
            for b in range(side):
                four = [device(a, p, b) for a in range(quads)]
                near += [four[:2], four[2:]]
                far += [four[1:3], [four[0], four[3]]]
    return big, near, far


def exchange(x, axis, groups):
    return lax.all_to_all(x, axis, 0, 0, axis_index_groups=groups, tiled=True)


def head_kernel(x_ref, w_ref, out_ref, total):
    step = pl.program_id(0)
    part = jnp.dot(x_ref[...], w_ref[...], preferred_element_type=f32)

    @pl.when(step == 0)
    def _():
        total[...] = part

    @pl.when(step > 0)
    def _():
        total[...] += part

    @pl.when(step == pl.num_programs(0) - 1)
    def _():
        out_ref[...] = total[...].astype(bf16)


def head(x, w):
    rows, depth = x.shape
    cols = w.shape[1]
    step = depth // 3
    return pl.pallas_call(
        head_kernel,
        grid=(3,),
        in_specs=[
            pl.BlockSpec((rows, step), lambda i: (0, i)),
            pl.BlockSpec((step, cols), lambda i: (i, 0)),
        ],
        out_specs=pl.BlockSpec((rows, cols), lambda i: (0, 0)),
        out_shape=jax.ShapeDtypeStruct((rows, cols), bf16),
        scratch_shapes=[pltpu.VMEM((rows, cols), f32)],
        compiler_params=pltpu.CompilerParams(vmem_limit_bytes=24 * 2**20),
    )(x, w)


def tail_kernel(x_ref, g_ref, out_ref, bias_ref):
    out_ref[...] = jnp.dot(x_ref[...], g_ref[...], preferred_element_type=f32).astype(bf16)

    @pl.when(pl.program_id(0) == 0)
    def _():
        ones = jnp.ones((8, g_ref.shape[0]), bf16)
        bias_ref[...] = jnp.dot(ones, g_ref[...], preferred_element_type=f32)


def tail(x_t, g):
    depth, rows = x_t.shape
    cols = g.shape[1]
    step = depth // 3
    enc, bias = pl.pallas_call(
        tail_kernel,
        grid=(3,),
        in_specs=[
            pl.BlockSpec((step, rows), lambda i: (i, 0)),
            pl.BlockSpec((rows, cols), lambda i: (0, 0)),
        ],
        out_specs=[
            pl.BlockSpec((step, cols), lambda i: (i, 0)),
            pl.BlockSpec((8, cols), lambda i: (0, 0)),
        ],
        out_shape=[
            jax.ShapeDtypeStruct((depth, cols), bf16),
            jax.ShapeDtypeStruct((8, cols), f32),
        ],
        compiler_params=pltpu.CompilerParams(vmem_limit_bytes=24 * 2**20),
    )(x_t, g)
    return enc, bias[0]


def body(tokens, enc_weight, enc_bias, dec_weight, pairs, counts):
    rows, width = tokens.shape
    local_lat = enc_weight.shape[1]
    nblk = local_lat // BL
    slots = pairs.shape[1]
    n_lat = lax.axis_size("lat")
    n_tok = lax.axis_size("tok")
    lat = lax.axis_index("lat")
    tok = lax.axis_index("tok")
    half = tok * 2 // n_tok
    own = rows // n_tok
    share = rows // n_lat
    side = round(n_lat**0.5)
    quads = side // 2
    n_x = n_tok // 2
    even = tok % 2 == 0
    both = ("lat", "tok")
    big, near, far = lat_groups(n_lat, n_tok)
    x_groups = [[2 * x + c for x in range(n_x)] for c in range(2)]
    c_groups = [[2 * x, 2 * x + 1] for x in range(n_x)]

    def gather_tok(v):
        spread = jnp.broadcast_to(v[None], (n_x,) + v.shape)
        got = exchange(spread, "tok", x_groups)
        return lax.all_gather(
            got.reshape(-1, local_lat), "tok", axis_index_groups=c_groups, axis=0, tiled=True
        )

    codes = pairs[0]
    valid = jnp.arange(slots, dtype=jnp.int32) < counts[0]
    g_own = tok * own // BR
    hit = valid[:, None] & (
        codes[:, None] == g_own * nblk + jnp.arange(local_lat, dtype=jnp.int32)[None, :] // BL
    )
    mask = jnp.any(hit, axis=0)[None, :]

    dec32 = dec_weight.astype(f32)
    squares = jnp.sum(dec32 * dec32, axis=1).astype(bf16)
    part = head(tokens, enc_weight)
    got = exchange(part.reshape(n_tok, own, local_lat), "tok", None)
    pre = jnp.sum(got.astype(f32), axis=0) + enc_bias[None, :]
    acts_own = jnp.where(mask, jax.nn.softplus(pre), 0.0).astype(bf16)
    extra = jnp.broadcast_to(squares[None, :], (EXTRA, local_lat))
    got = gather_tok(jnp.concatenate([acts_own, extra], axis=0))
    got = got.reshape(2, n_x, own + EXTRA, local_lat)
    acts = got[:, :, :own]
    sq = got[:, :, own].astype(f32)
    norm_a = jnp.sqrt(jnp.sum(sq[:, : n_x // 2], axis=(0, 1)) + EPSILON)
    norm_b = jnp.sqrt(jnp.sum(sq[:, n_x // 2 :], axis=(0, 1)) + EPSILON)
    own_norm = jnp.where(half == 0, norm_a, norm_b)

    acts_even = acts.reshape(2, n_x, side, share, local_lat).transpose(0, 2, 1, 3, 4)
    acts_odd = acts.reshape(2, n_x, quads, 2, share, local_lat).transpose(3, 1, 0, 2, 4, 5)
    acts_t = jnp.where(
        even, acts_even.reshape(rows, local_lat), acts_odd.reshape(rows, local_lat)
    )

    recon = jnp.dot(acts_t, dec_weight, preferred_element_type=f32).astype(bf16)
    got = exchange(recon.reshape(2 * side, quads * share, width), both, big)
    line = jnp.sum(got.astype(f32), axis=0).astype(bf16)
    for groups in (near, far):
        two = lax.all_gather(line, both, axis_index_groups=groups, axis=0)
        total = jnp.sum(two.astype(f32), axis=0)
        line = total.astype(bf16)
    y, z = lat // side, lat % side
    x_rows = []
    for a in range(quads):
        at = jnp.where(even, (2 * a + y % 2) * side + z, y * side + 2 * a + z % 2)
        x_rows.append(lax.dynamic_slice_in_dim(tokens, at * share, share, 0))
    x_line = jnp.concatenate(x_rows, axis=0)
    err_line = (total - x_line.astype(f32)).astype(bf16)
    a_own = jnp.where(even, y, z) // 2
    err_own = lax.dynamic_slice_in_dim(err_line, a_own * share, share, 0)
    err = exchange(jnp.broadcast_to(err_line[None], (2 * side,) + err_line.shape), both, big)
    err = err.reshape(rows, width)

    back = lax.dot_general(
        err, dec_weight, (((1,), (1,)), ((), ())), preferred_element_type=f32
    ).astype(bf16)
    back_even = back.reshape(2, side, quads, share, local_lat).transpose(2, 0, 1, 3, 4)
    back_odd = back.reshape(2, side, quads, share, local_lat).transpose(1, 2, 0, 3, 4)
    shape = (n_tok, own, local_lat)
    back = jnp.where(even, back_even.reshape(shape), back_odd.reshape(shape))
    got = exchange(back, "tok", None)
    grad_act = jnp.sum(got.astype(f32), axis=0) + PENALTY * (norm_a + norm_b)[None, :]
    grad_own = jnp.where(mask, grad_act * jax.nn.sigmoid(pre), 0.0).astype(bf16)
    grad_pre = gather_tok(grad_own)

    act_sum = jnp.sum(acts_t.astype(f32), axis=0)
    dec_data = lax.dot_general(acts_t, err, (((0,), (0,)), ((), ())), preferred_element_type=f32)
    dec_grad = dec_data + PENALTY * (act_sum / own_norm)[:, None] * dec32
    tokens_t = tokens.reshape(n_x, 2, own, width).transpose(3, 1, 0, 2).reshape(width, rows)
    enc_grad, bias_grad = tail(tokens_t, grad_pre)
    return err_own, enc_grad, dec_grad.astype(bf16), bias_grad


def solution(mesh):
    return jax.shard_map(
        body,
        mesh=mesh,
        in_specs=(
            P(None, "tok"),
            P("tok", "lat"),
            P("lat"),
            P("lat", "tok"),
            P("lat", None),
            P("lat"),
        ),
        out_specs=(P("lat", "tok"), P("tok", "lat"), P("lat", "tok"), P("lat")),
        check_vma=False,
    )
```

time: 155 us -> 153 us (0.987)
  waiting for transfers between devices: 53.4 us -> 69 us
  blocking collectives: 34.9 us -> 22.9 us
  Pallas kernels: 0 us -> 4.94 us
  matrix products: 11.3 us -> 7.52 us
  local copies, waits for them, and re-layouts: 12.2 us -> 9.34 us
  starting transfers between devices: 35.9 us -> 33.4 us
    all_to_all x1 -> x0, blocking collectives: 27.2 us -> none  [exchange(): return lax.all_to_all(x, axis, 0, 0, axis_index_groups=groups, tiled=True)]
    all_to_all x6, waiting for transfers between devices: 53.4 us -> 69 us  [exchange(): return lax.all_to_all(x, axis, 0, 0, axis_index_groups=groups, tiled=True)]
    all_gather x2 -> x4, blocking collectives: 7.7 us -> 22.9 us  [the longest x2 15.2 us: body(): two = lax.all_gather(line, both, axis_index_groups=groups, axis=0)]
    pallas_call x0 -> x2, Pallas kernels: none -> 4.94 us  [the longest x1 2.55 us: head(): pl.pallas_call(head_kernel, grid=(3,), in_specs=[pl.BlockSpec((rows, step...]
    dot_general x2 -> x0, matrix products: 4.78 us -> none  [the longest x1 2.91 us: body(): part = jnp.dot(tokens, enc_weight, preferred_element_type=f32).astype(bf16)]
    all_to_all x6, starting transfers between devices: 35.9 us -> 33.4 us  [exchange(): return lax.all_to_all(x, axis, 0, 0, axis_index_groups=groups, tiled=True)]
    unnamed x17 -> x25, local copies, waits for them, and re-layouts: 5.34 us -> 3.84 us
  transfers between devices with their start and end apart: 6 -> 6, of which waited for: 6 -> 6; matrix products, arithmetic and copies ran while one was open for 6% -> 5% of each run, Pallas kernels for 0% -> 0%
where the time goes in v4:
time: 153 us; the launch traced here: 152 us
  waiting for transfers between devices  69 us (45%)
  starting transfers between devices  33.4 us (22%)
  blocking collectives  22.9 us (15%)
  local copies, waits for them, and re-layouts  9.34 us (6%)
  matrix products  7.52 us (5%)
  Pallas kernels  4.94 us (3%)
  other arithmetic  2.97 us (2%)
  between operations  1.75 us (1%)
    all_to_all x6, waiting for transfers between devices, exchange(): return lax.all_to_all(x, axis, 0, 0, axis_index_groups=groups, tiled=True)  69 us
    all_to_all x6, starting transfers between devices, exchange(): return lax.all_to_all(x, axis, 0, 0, axis_index_groups=groups, tiled=True)  33.4 us
    all_gather x2, blocking collectives, body(): two = lax.all_gather(line, both, axis_index_groups=groups, axis=0)  15.2 us
    all_gather x2, blocking collectives, gather_tok(): lax.all_gather(got.reshape(-1, local_lat), 'tok', axis_index_groups=c_gro...  7.76 us
    unnamed x25, local copies, waits for them, and re-layouts  3.84 us
    dot_general x1, matrix products, body(): lax.dot_general(acts_t, err, (((0,), (0,)), ((), ())), preferred_element_...  3.51 us
  transfers between devices with their start and end apart: 6, of which 6 were waited for; matrix products, arithmetic and copies ran while one was open for 5% of the time, Pallas kernels for 0%

profile of v4, /device:TPU:1, one launch (start us, length us, event | category | flops | bytes accessed | tf_op | source)
XLA Modules:
  0.0 151.8 jit_solution(8575315158600342150)
XLA Ops:
  0.6 0.0 copy-start
  0.6 1.3 copy-done
  1.9 0.0 copy-start.2
  1.9 1.3 copy-done.2
  3.2 0.0 copy-start.11
  3.2 2.6 %shard_map.93 = bf16[512,512]{1,0:T(8,128)(2,1)} custom-call(bf16[512,1152]{1,0:T(8,128)(2,1)S(1)} %copy-done, bf16[1152,512]{1,0:T(8,128)(2,1)S(1)} %copy-done.2), custom_call_target="tpu_custom_call" | custom-call | tf_op jit(solution)/shard_map/pallas_call | solution.py:65
  5.7 10.3 %all-to-all-start = ((bf16[8,64,512]{2,1,0:T(8,128)(2,1)}), bf16[8,64,512]{2,1,0:T(8,128)(2,1)S(1)}, u32[]{:S(2)}, u32[]{:S(2)}) async-start(bf16[8,64,512]{2,1,0:T(8,128)(2,1)} %bitcast.2), calls=%async_computation | async-start | bytes 1048576 | tf_op jit(solution)/shard_map/all_to_all | solution.py:41
  16.7 0.0 copy-done.11
  16.7 0.1 and_reduce_fusion
  16.8 0.0 copy-done.5
  16.8 0.0 copy-start.9
  16.8 0.3 fusion.1
  17.2 8.4 %all-to-all-done = bf16[8,64,512]{2,1,0:T(8,128)(2,1)S(1)} async-done(((bf16[8,64,512]{2,1,0:T(8,128)(2,1)}), bf16[8,64,512]{2,1,0:T(8,128)(2,1)S(1)}, u32[]{:S(2)}, u32[]{:S(2)}) %all-to-all-start) | async-done | bytes 524320 | tf_op jit(solution)/shard_map/all_to_all | solution.py:41
  25.5 0.1 convert_reduce_fusion.2
  25.6 0.0 copy-start.3
  25.6 0.6 copy-done.3
  26.2 0.0 copy-done.8
  26.2 0.1 fusion.3
  26.4 0.7 broadcast_in_dim.24
  27.1 0.0 copy-done.9
  27.1 3.5 %all-to-all-start.1 = ((bf16[4,72,512]{2,1,0:T(8,128)(2,1)}), bf16[4,72,512]{2,1,0:T(8,128)(2,1)S(1)}, u32[]{:S(2)}, u32[]{:S(2)}) async-start(bf16[4,72,512]{2,1,0:T(8,128)(2,1)} %broadcast_in_dim.24), calls=%async_computation.1 | async-start | bytes 589824 | tf_op jit(solution)/shard_map/all_to_all | solution.py:41
  30.6 5.9 %all-to-all-done.1 = bf16[4,72,512]{2,1,0:T(8,128)(2,1)S(1)} async-done(((bf16[4,72,512]{2,1,0:T(8,128)(2,1)}), bf16[4,72,512]{2,1,0:T(8,128)(2,1)S(1)}, u32[]{:S(2)}, u32[]{:S(2)}) %all-to-all-start.1) | async-done | bytes 294944 | tf_op jit(solution)/shard_map/all_to_all | solution.py:41
  36.4 3.9 %all_gather.18 = bf16[576,512]{1,0:T(8,128)(2,1)S(1)} all-gather(bf16[288,512]{1,0:T(8,128)(2,1)S(1)} %bitcast.60), channel_id=1, replica_groups={{0,1},{2,3},{4,5},{6,7},{8,9},{10,11},{12,13},{14,15},{16,17},{18,19},{..., dimensions={0}, use_global_device_ids=true | all-gather | bytes 884736 | tf_op jit(solution)/shard_map/all_gather | solution.py:136
  40.3 0.1 slice_bitcast_fusion
  40.5 0.1 copy.24
  40.6 0.1 bitcast_select_fusion.1
  40.7 1.9 %convolution_convert_fusion = bf16[512,1152]{1,0:T(8,128)(2,1)} fusion(bf16[512,512]{1,0:T(8,128)(2,1)S(1)} %bitcast_select_fusion.1, bf16[512,1152]{1,0:T(8,128)(2,1)S(1)} %copy-done.5), kind=kOutput, calls=%fused_computation.2 | convolution fusion | flops 604569600 | bytes 2883584 | tf_op jit(solution)/shard_map/dot_general | solution.py:169
  42.6 4.4 %all-to-all-start.2 = ((bf16[16,32,1152]{2,1,0:T(8,128)(2,1)}), bf16[16,32,1152]{2,1,0:T(8,128)(2,1)S(1)}, u32[]{:S(2)}, u32[]{:S(2)}) async-start(bf16[16,32,1152]{2,1,0:T(8,128)(2,1)} %bitcast.61), calls=%async_computation.2 | async-start | bytes 2359296 | tf_op jit(solution)/shard_map/all_to_all | solution.py:41
  47.0 0.0 copy-done.1
  47.0 0.6 constant_dynamic-slice_fusion.4
  47.7 22.1 %all-to-all-done.2 = bf16[16,32,1152]{2,1,0:T(8,128)(2,1)S(1)} async-done(((bf16[16,32,1152]{2,1,0:T(8,128)(2,1)}), bf16[16,32,1152]{2,1,0:T(8,128)(2,1)S(1)}, u32[]{:S(2)}, u32[]{:S(2)}) %all-to-all-start.2) | async-done | bytes 1179680 | tf_op jit(solution)/shard_map/all_to_all | solution.py:41
  69.7 0.2 reduce_sum.89
  69.9 7.3 %all-gather = bf16[64,1152]{1,0:T(8,128)(2,1)S(1)} all-gather(bf16[32,1152]{1,0:T(8,128)(2,1)S(1)} %reduce_sum.89), channel_id=2, replica_groups={{0,128},{256,384},{8,136},{264,392},{16,144},{272,400},{24,152},{280,40..., dimensions={0}, use_global_device_ids=true | all-gather | bytes 221184 | tf_op jit(solution)/shard_map/all_gather | solution.py:173
  77.2 7.9 %all-gather.1 = bf16[64,1152]{1,0:T(8,128)(2,1)S(1)} all-gather(bf16[32,1152]{1,0:T(8,128)(2,1)S(1)} %reduce_sum.90), channel_id=3, replica_groups={{128,256},{0,384},{136,264},{8,392},{144,272},{16,400},{152,280},{24,40..., dimensions={0}, use_global_device_ids=true | all-gather | bytes 221184 | tf_op jit(solution)/shard_map/all_gather | solution.py:173
  85.2 0.8 subtract_convert_fusion
  85.9 1.1 broadcast_in_dim.25
  87.0 5.6 %all-to-all-start.3 = ((bf16[16,32,1152]{2,1,0:T(8,128)(2,1)}), bf16[16,32,1152]{2,1,0:T(8,128)(2,1)}, u32[]{:S(2)}, u32[]{:S(2)}) async-start(bf16[16,32,1152]{2,1,0:T(8,128)(2,1)} %broadcast_in_dim.25), calls=%async_computation.3 | async-start | bytes 2359296 | tf_op jit(solution)/shard_map/all_to_all | solution.py:41
  92.7 0.1 copy.25
  92.8 0.6 copy.28.x_ref
  93.5 0.0 copy-start.6
  93.5 0.1 copy.29
  93.5 0.6 copy.33
  94.2 0.2 convert_reduce_fusion
  94.4 21.9 %all-to-all-done.3 = bf16[16,32,1152]{2,1,0:T(8,128)(2,1)} async-done(((bf16[16,32,1152]{2,1,0:T(8,128)(2,1)}), bf16[16,32,1152]{2,1,0:T(8,128)(2,1)}, u32[]{:S(2)}, u32[]{:S(2)}) %all-to-all-start.3) | async-done | bytes 1179680 | tf_op jit(solution)/shard_map/all_to_all | solution.py:41
  116.2 0.0 copy-done.6
  116.2 2.1 %convolution_convert_fusion.1 = bf16[512,512]{1,0:T(8,128)(2,1)S(1)} fusion(bf16[512,1152]{1,0:T(8,128)(2,1)} %bitcast.17, bf16[512,1152]{1,0:T(8,128)(2,1)S(1)} %copy-done.6), kind=kOutput, calls=%fused_computation.6 | convolution fusion | flops 604241920 | bytes 2883584 | tf_op jit(solution)/shard_map/dot_general | solution.py:188
  118.4 0.1 copy.27
  118.5 0.0 copy-start.7
  118.5 0.9 bitcast_select_fusion
  119.4 6.2 %all-to-all-start.4 = ((bf16[8,64,512]{2,1,0:T(8,128)(2,1)}), bf16[8,64,512]{2,1,0:T(8,128)(2,1)S(1)}, u32[]{:S(2)}, u32[]{:S(2)}) async-start(bf16[8,64,512]{2,1,0:T(8,128)(2,1)} %bitcast_select_fusion), calls=%async_computation.4 | async-start | bytes 1048576 | tf_op jit(solution)/shard_map/all_to_all | solution.py:41
  125.6 0.0 copy-done.7
  125.7 0.6 constant_dynamic-slice_fusion
  126.4 8.8 %all-to-all-done.4 = bf16[8,64,512]{2,1,0:T(8,128)(2,1)S(1)} async-done(((bf16[8,64,512]{2,1,0:T(8,128)(2,1)}), bf16[8,64,512]{2,1,0:T(8,128)(2,1)S(1)}, u32[]{:S(2)}, u32[]{:S(2)}) %all-to-all-start.4) | async-done | bytes 524320 | tf_op jit(solution)/shard_map/all_to_all | solution.py:41
  135.1 0.1 convert_reduce_fusion.1
  135.2 0.0 copy-done.4
  135.2 0.0 copy-done.10
  135.2 0.1 select_convert_fusion
  135.3 0.7 broadcast_in_dim.26
  136.0 3.4 %all-to-all-start.5 = ((bf16[4,64,512]{2,1,0:T(8,128)(2,1)}), bf16[4,64,512]{2,1,0:T(8,128)(2,1)S(1)}, u32[]{:S(2)}, u32[]{:S(2)}) async-start(bf16[4,64,512]{2,1,0:T(8,128)(2,1)} %broadcast_in_dim.26), calls=%async_computation.5 | async-start | bytes 524288 | tf_op jit(solution)/shard_map/all_to_all | solution.py:41
  139.4 3.5 %fusion = bf16[512,1152]{1,0:T(8,128)(2,1)} fusion(bf16[512,512]{1,0:T(8,128)(2,1)S(1)} %bitcast.65, bf16[512,1152]{1,0:T(8,128)(2,1)} %bitcast.17, bf16[512,1152]{1,0:T(8,128)(2,1)} %param.9, f32[512]{0:T(512)S(1)} %get-tuple-element.18), kind=kOutput, calls=%fused_computation.1 | convolution fusion | flops 606339072 | bytes 4065280 | tf_op jit(solution)/shard_map/dot_general | solution.py:201
  142.9 2.0 %all-to-all-done.5 = bf16[4,64,512]{2,1,0:T(8,128)(2,1)S(1)} async-done(((bf16[4,64,512]{2,1,0:T(8,128)(2,1)}), bf16[4,64,512]{2,1,0:T(8,128)(2,1)S(1)}, u32[]{:S(2)}, u32[]{:S(2)}) %all-to-all-start.5) | async-done | bytes 262176 | tf_op jit(solution)/shard_map/all_to_all | solution.py:41
  145.0 3.9 %all_gather.23.g_ref = bf16[512,512]{1,0:T(8,128)(2,1)S(1)} all-gather(bf16[256,512]{1,0:T(8,128)(2,1)S(1)} %bitcast.62), channel_id=1, replica_groups={{0,1},{2,3},{4,5},{6,7},{8,9},{10,11},{12,13},{14,15},{16,17},{18,19},{..., dimensions={0}, use_global_device_ids=true | all-gather | bytes 786432 | tf_op jit(solution)/shard_map/all_gather | solution.py:136
  148.8 2.4 %shard_map.94 = (bf16[1152,512]{1,0:T(8,128)(2,1)}, f32[8,512]{1,0:T(8,128)S(1)}) custom-call(bf16[1152,512]{1,0:T(8,128)(2,1)S(1)} %copy.28.x_ref, bf16[512,512]{1,0:T(8,128)(2,1)S(1)} %all_gather.23.g_ref), custom_call_target="tpu_custom_call" | custom-call | tf_op jit(solution)/shard_map/pallas_call | solution.py:92
  151.2 0.6 slice.19
  (17 shorter events, 0.3 us)
Async XLA Ops:
  0.6 1.3 copy-start
  1.9 1.3 copy-start.2
  3.2 13.5 %copy-start.11 = (s32[1,32]{1,0:T(1,128)S(1)}, s32[1,32]{1,0:T(1,128)}, u32[]{:S(2)}) copy-start(s32[1,32]{1,0:T(1,128)} %param.10) | copy-start | bytes 388
  3.2 13.7 %copy-start.5 = (bf16[512,1152]{1,0:T(8,128)(2,1)S(1)}, bf16[512,1152]{1,0:T(8,128)(2,1)}, u32[]{:S(2)}) copy-start(bf16[512,1152]{1,0:T(8,128)(2,1)} %param.9) | copy-start | bytes 3538948
  5.7 19.8 %all-to-all-start = ((bf16[8,64,512]{2,1,0:T(8,128)(2,1)}), bf16[8,64,512]{2,1,0:T(8,128)(2,1)S(1)}, u32[]{:S(2)}, u32[]{:S(2)}) async-start(bf16[8,64,512]{2,1,0:T(8,128)(2,1)} %bitcast.2), calls=%async_computation | async-start | bytes 1048576 | tf_op jit(solution)/shard_map/all_to_all | solution.py:41
  16.0 10.2 %copy-start.8 = (f32[512]{0:T(512)S(1)}, f32[512]{0:T(512)}, u32[]{:S(2)}) copy-start(f32[512]{0:T(512)} %param.8) | copy-start | bytes 6148
  16.8 10.3 %copy-start.9 = (pred[512]{0:T(512)(128)(4,1)}, pred[512]{0:T(512)(128)(4,1)S(1)}, u32[]{:S(2)}) copy-start(pred[512]{0:T(512)(128)(4,1)S(1)} %and_reduce_fusion) | copy-start | bytes 1540
  25.6 0.7 copy-start.3
  27.1 9.3 %all-to-all-start.1 = ((bf16[4,72,512]{2,1,0:T(8,128)(2,1)}), bf16[4,72,512]{2,1,0:T(8,128)(2,1)S(1)}, u32[]{:S(2)}, u32[]{:S(2)}) async-start(bf16[4,72,512]{2,1,0:T(8,128)(2,1)} %broadcast_in_dim.24), calls=%async_computation.1 | async-start | bytes 589824 | tf_op jit(solution)/shard_map/all_to_all | solution.py:41
  42.6 4.5 %copy-start.1 = (bf16[512,1152]{1,0:T(8,128)(2,1)S(1)}, bf16[512,1152]{1,0:T(8,128)(2,1)}, u32[]{:S(2)}) copy-start(bf16[512,1152]{1,0:T(8,128)(2,1)} %x_ref.1) | copy-start | bytes 3538948
  42.6 27.2 %all-to-all-start.2 = ((bf16[16,32,1152]{2,1,0:T(8,128)(2,1)}), bf16[16,32,1152]{2,1,0:T(8,128)(2,1)S(1)}, u32[]{:S(2)}, u32[]{:S(2)}) async-start(bf16[16,32,1152]{2,1,0:T(8,128)(2,1)} %bitcast.61), calls=%async_computation.2 | async-start | bytes 2359296 | tf_op jit(solution)/shard_map/all_to_all | solution.py:41
  87.0 29.2 %all-to-all-start.3 = ((bf16[16,32,1152]{2,1,0:T(8,128)(2,1)}), bf16[16,32,1152]{2,1,0:T(8,128)(2,1)}, u32[]{:S(2)}, u32[]{:S(2)}) async-start(bf16[16,32,1152]{2,1,0:T(8,128)(2,1)} %broadcast_in_dim.25), calls=%async_computation.3 | async-start | bytes 2359296 | tf_op jit(solution)/shard_map/all_to_all | solution.py:41
  93.5 22.8 %copy-start.6 = (bf16[512,1152]{1,0:T(8,128)(2,1)S(1)}, bf16[512,1152]{1,0:T(8,128)(2,1)}, u32[]{:S(2)}) copy-start(bf16[512,1152]{1,0:T(8,128)(2,1)} %param.9) | copy-start | bytes 3538948
  118.5 7.1 %copy-start.7 = (f32[2,4,1,512]{3,1,2,0:T(4,128)S(1)}, f32[2,4,1,512]{3,1,2,0:T(4,128)}, u32[]{:S(2)}) copy-start(f32[2,4,1,512]{3,1,2,0:T(4,128)} %copy.33) | copy-start | bytes 49156
  119.4 15.8 %copy-start.4 = (f32[64,512]{1,0:T(8,128)S(1)}, f32[64,512]{1,0:T(8,128)}, u32[]{:S(2)}) copy-start(f32[64,512]{1,0:T(8,128)} %copy-done.3) | copy-start | bytes 393220
  119.4 15.8 %copy-start.10 = (pred[512]{0:T(512)(128)(4,1)S(1)}, pred[512]{0:T(512)(128)(4,1)}, u32[]{:S(2)}) copy-start(pred[512]{0:T(512)(128)(4,1)} %copy-done.9) | copy-start | bytes 1540
  119.4 15.7 %all-to-all-start.4 = ((bf16[8,64,512]{2,1,0:T(8,128)(2,1)}), bf16[8,64,512]{2,1,0:T(8,128)(2,1)S(1)}, u32[]{:S(2)}, u32[]{:S(2)}) async-start(bf16[8,64,512]{2,1,0:T(8,128)(2,1)} %bitcast_select_fusion), calls=%async_computation.4 | async-start | bytes 1048576 | tf_op jit(solution)/shard_map/all_to_all | solution.py:41
  136.0 8.9 %all-to-all-start.5 = ((bf16[4,64,512]{2,1,0:T(8,128)(2,1)}), bf16[4,64,512]{2,1,0:T(8,128)(2,1)S(1)}, u32[]{:S(2)}, u32[]{:S(2)}) async-start(bf16[4,64,512]{2,1,0:T(8,128)(2,1)} %broadcast_in_dim.26), calls=%async_computation.5 | async-start | bytes 524288 | tf_op jit(solution)/shard_map/all_to_all | solution.py:41

commit v5 on v4

v5 whole, which is shorter than its diff:
```python
import jax
import jax.numpy as jnp
from jax import lax
from jax.experimental import pallas as pl
from jax.experimental.pallas import tpu as pltpu
from jax.sharding import PartitionSpec as P

BR = 128
BL = 64
PENALTY = 0.3
EPSILON = 1e-06
EXTRA = 8

f32 = jnp.float32
bf16 = jnp.bfloat16


def lat_groups(n_lat, n_tok):
    side = round(n_lat**0.5)
    quads = side // 2
    line, near, far, swap = [], [], [], []
    for tok in range(n_tok):

        def device(pair, b):
            lat = b * side + pair if tok % 2 == 1 else pair * side + b
            return lat * n_tok + tok

        for pair in range(side):
            line.append([device(pair, b) for b in range(side)])
            swap += [(device(pair, b), device(pair ^ 1, b)) for b in range(side)]
        for p in range(2):
            for b in range(side):
                four = [device(2 * a + p, b) for a in range(quads)]
                near += [four[:2], four[2:]]
                far += [four[1:3], [four[0], four[3]]]
    return line, near, far, swap


def exchange(x, axis, groups):
    return lax.all_to_all(x, axis, 0, 0, axis_index_groups=groups, tiled=True)


def tail_kernel(x_ref, g_ref, out_ref, bias_ref):
    out_ref[...] = jnp.dot(x_ref[...], g_ref[...], preferred_element_type=f32).astype(bf16)

    @pl.when(pl.program_id(0) == 0)
    def _():
        ones = jnp.ones((8, g_ref.shape[0]), bf16)
        bias_ref[...] = jnp.dot(ones, g_ref[...], preferred_element_type=f32)[0]


def tail(x_t, g):
    depth, rows = x_t.shape
    cols = g.shape[1]
    step = depth // 3
    return pl.pallas_call(
        tail_kernel,
        grid=(3,),
        in_specs=[
            pl.BlockSpec((step, rows), lambda i: (i, 0)),
            pl.BlockSpec((rows, cols), lambda i: (0, 0)),
        ],
        out_specs=[
            pl.BlockSpec((step, cols), lambda i: (i, 0)),
            pl.BlockSpec((cols,), lambda i: (0,)),
        ],
        out_shape=[
            jax.ShapeDtypeStruct((depth, cols), bf16),
            jax.ShapeDtypeStruct((cols,), f32),
        ],
        compiler_params=pltpu.CompilerParams(vmem_limit_bytes=24 * 2**20),
    )(x_t, g)


def body(tokens, enc_weight, enc_bias, dec_weight, pairs, counts):
    rows, width = tokens.shape
    local_lat = enc_weight.shape[1]
    nblk = local_lat // BL
    slots = pairs.shape[1]
    n_lat = lax.axis_size("lat")
    n_tok = lax.axis_size("tok")
    lat = lax.axis_index("lat")
    tok = lax.axis_index("tok")
    half = tok * 2 // n_tok
    own = rows // n_tok
    share = rows // n_lat
    side = round(n_lat**0.5)
    quads = side // 2
    n_x = n_tok // 2
    even = tok % 2 == 0
    both = ("lat", "tok")
    line_groups, near, far, swap = lat_groups(n_lat, n_tok)
    x_groups = [[2 * x + c for x in range(n_x)] for c in range(2)]
    c_groups = [[2 * x, 2 * x + 1] for x in range(n_x)]

    def gather_tok(v):
        spread = jnp.broadcast_to(v[None], (n_x,) + v.shape)
        got = exchange(spread, "tok", x_groups)
        return lax.all_gather(
            got.reshape(-1, local_lat), "tok", axis_index_groups=c_groups, axis=0, tiled=True
        )

    codes = pairs[0]
    valid = jnp.arange(slots, dtype=jnp.int32) < counts[0]
    g_own = tok * own // BR
    hit = valid[:, None] & (
        codes[:, None] == g_own * nblk + jnp.arange(local_lat, dtype=jnp.int32)[None, :] // BL
    )
    mask = jnp.any(hit, axis=0)[None, :]

    dec32 = dec_weight.astype(f32)
    squares = jnp.sum(dec32 * dec32, axis=1).astype(bf16)
    part = jnp.dot(tokens, enc_weight, preferred_element_type=f32).astype(bf16)
    part, squares = lax.optimization_barrier((part, squares))
    got = exchange(part.reshape(n_tok, own, local_lat), "tok", None)
    pre = jnp.sum(got.astype(f32), axis=0) + enc_bias[None, :]
    acts_own = jnp.where(mask, jax.nn.softplus(pre), 0.0).astype(bf16)
    extra = jnp.broadcast_to(squares[None, :], (EXTRA, local_lat))
    got = gather_tok(jnp.concatenate([acts_own, extra], axis=0))
    got = got.reshape(2, n_x, own + EXTRA, local_lat)
    acts = got[:, :, :own]
    sq = got[:, :, own].astype(f32)
    norm_a = jnp.sqrt(jnp.sum(sq[:, : n_x // 2], axis=(0, 1)) + EPSILON)
    norm_b = jnp.sqrt(jnp.sum(sq[:, n_x // 2 :], axis=(0, 1)) + EPSILON)
    own_norm = jnp.where(half == 0, norm_a, norm_b)

    acts_even = acts.reshape(2, n_x, side, share, local_lat).transpose(0, 2, 1, 3, 4)
    acts_odd = acts.reshape(2, n_x, quads, 2, share, local_lat).transpose(3, 1, 0, 2, 4, 5)
    halves = jnp.where(
        even,
        acts_even.reshape(2, rows // 2, local_lat),
        acts_odd.reshape(2, rows // 2, local_lat),
    )
    y, z = lat // side, lat % side
    low = jnp.where(even, y, z) % 2 == 0
    acts_kept = jnp.where(low, halves[0], halves[1])
    acts_sent = jnp.where(low, halves[1], halves[0])

    sent = jnp.dot(acts_sent, dec_weight, preferred_element_type=f32).astype(bf16)
    came = lax.ppermute(sent, both, swap)
    kept = jnp.dot(acts_kept, dec_weight, preferred_element_type=f32)
    recon = (kept + came.astype(f32)).astype(bf16)
    got = exchange(recon.reshape(side, quads * share, width), both, line_groups)
    line = jnp.sum(got.astype(f32), axis=0).astype(bf16)
    for groups in (near, far):
        two = lax.all_gather(line, both, axis_index_groups=groups, axis=0)
        total = jnp.sum(two.astype(f32), axis=0)
        line = total.astype(bf16)
    x_rows = []
    for a in range(quads):
        at = jnp.where(even, (2 * a + y % 2) * side + z, y * side + 2 * a + z % 2)
        x_rows.append(lax.dynamic_slice_in_dim(tokens, at * share, share, 0))
    x_line = jnp.concatenate(x_rows, axis=0)
    err_line = (total - x_line.astype(f32)).astype(bf16)
    a_own = jnp.where(even, y, z) // 2
    err_own = lax.dynamic_slice_in_dim(err_line, a_own * share, share, 0)
    err_kept = exchange(
        jnp.broadcast_to(err_line[None], (side,) + err_line.shape), both, line_groups
    ).reshape(rows // 2, width)
    err_came = lax.ppermute(err_kept, both, swap)

    def back_of(e):
        return lax.dot_general(
            e, dec_weight, (((1,), (1,)), ((), ())), preferred_element_type=f32
        ).astype(bf16)

    back_kept, back_came = back_of(err_kept), back_of(err_came)
    back = jnp.stack(
        [jnp.where(low, back_kept, back_came), jnp.where(low, back_came, back_kept)]
    ).reshape(2, side, quads, share, local_lat)
    shape = (n_tok, own, local_lat)
    back = jnp.where(
        even,
        back.transpose(2, 0, 1, 3, 4).reshape(shape),
        back.transpose(1, 2, 0, 3, 4).reshape(shape),
    )
    got = exchange(back, "tok", None)
    grad_act = jnp.sum(got.astype(f32), axis=0) + PENALTY * (norm_a + norm_b)[None, :]
    grad_own = jnp.where(mask, grad_act * jax.nn.sigmoid(pre), 0.0).astype(bf16)
    grad_pre = gather_tok(grad_own)

    acts_t = jnp.concatenate([acts_kept, acts_sent], axis=0)
    err = jnp.concatenate([err_kept, err_came], axis=0)
    act_sum = jnp.sum(acts_t.astype(f32), axis=0)
    dec_data = lax.dot_general(acts_t, err, (((0,), (0,)), ((), ())), preferred_element_type=f32)
    dec_grad = dec_data + PENALTY * (act_sum / own_norm)[:, None] * dec32
    tokens_t = tokens.reshape(n_x, 2, own, width).transpose(3, 1, 0, 2).reshape(width, rows)
    enc_grad, bias_grad = tail(tokens_t, grad_pre)
    return err_own, enc_grad, dec_grad.astype(bf16), bias_grad


def solution(mesh):
    return jax.shard_map(
        body,
        mesh=mesh,
        in_specs=(
            P(None, "tok"),
            P("tok", "lat"),
            P("lat"),
            P("lat", "tok"),
            P("lat", None),
            P("lat"),
        ),
        out_specs=(P("lat", "tok"), P("tok", "lat"), P("lat", "tok"), P("lat")),
        check_vma=False,
    )
```

time: 153 us -> 156 us (1.020)
  waiting for transfers between devices: 69 us -> 59 us
  starting transfers between devices: 33.4 us -> 40.4 us
  other arithmetic: 2.97 us -> 8.84 us
  Pallas kernels: 4.94 us -> 2.4 us
  local copies, waits for them, and re-layouts: 9.34 us -> 11.1 us
    all_to_all x6, waiting for transfers between devices: 69 us -> 44.7 us  [exchange(): return lax.all_to_all(x, axis, 0, 0, axis_index_groups=groups, tiled=True)]
    ppermute x0 -> x2, waiting for transfers between devices: none -> 14.3 us  [the longest x1 8.99 us: body(): came = lax.ppermute(sent, both, swap)]
    ppermute x0 -> x2, starting transfers between devices: none -> 6.37 us  [the longest x1 4.45 us: body(): err_came = lax.ppermute(err_kept, both, swap)]
    pallas_call x1 -> x0, Pallas kernels: 2.55 us -> none  [head(): pl.pallas_call(head_kernel, grid=(3,), in_specs=[pl.BlockSpec((rows, step...]
    dot_general x2 -> x5, matrix products: 4.01 us -> 5.6 us  [the longest x2 2.13 us: back_of(): lax.dot_general(e, dec_weight, (((1,), (1,)), ((), ())), preferred_elemen...]
    unnamed x25 -> x29, local copies, waits for them, and re-layouts: 3.84 us -> 3.1 us
  transfers between devices with their start and end apart: 6 -> 8, of which waited for: 6 -> 8; matrix products, arithmetic and copies ran while one was open for 5% -> 8% of each run, Pallas kernels for 0% -> 0%
where the time goes in v5:
time: 156 us; the launch traced here: 155 us
  waiting for transfers between devices  59 us (38%)
  starting transfers between devices  40.4 us (26%)
  blocking collectives  22.9 us (15%)
  local copies, waits for them, and re-layouts  11.1 us (7%)
  matrix products  8.89 us (6%)
  other arithmetic  8.84 us (6%)
  Pallas kernels  2.4 us (2%)
  between operations  1.79 us (1%)
    all_to_all x6, waiting for transfers between devices, exchange(): return lax.all_to_all(x, axis, 0, 0, axis_index_groups=groups, tiled=True)  44.7 us
    all_to_all x6, starting transfers between devices, exchange(): return lax.all_to_all(x, axis, 0, 0, axis_index_groups=groups, tiled=True)  34 us
    all_gather x2, blocking collectives, body(): two = lax.all_gather(line, both, axis_index_groups=groups, axis=0)  14.9 us
    ppermute x1, waiting for transfers between devices, body(): came = lax.ppermute(sent, both, swap)  8.99 us
    all_gather x2, blocking collectives, gather_tok(): lax.all_gather(got.reshape(-1, local_lat), 'tok', axis_index_groups=c_gro...  7.97 us
    ppermute x1, waiting for transfers between devices, body(): err_came = lax.ppermute(err_kept, both, swap)  5.26 us
    ppermute x1, starting transfers between devices, body(): err_came = lax.ppermute(err_kept, both, swap)  4.45 us
    dot_general x1, matrix products, body(): lax.dot_general(acts_t, err, (((0,), (0,)), ((), ())), preferred_element_...  3.29 us
  transfers between devices with their start and end apart: 8, of which 8 were waited for; matrix products, arithmetic and copies ran while one was open for 8% of the time, Pallas kernels for 0%

profile of v5, /device:TPU:1, one launch (start us, length us, event | category | flops | bytes accessed | tf_op | source)
XLA Modules:
  0.0 155.2 jit_solution(2383582506241259487)
XLA Ops:
  0.6 0.0 copy-start
  0.6 0.0 copy-start.5
  0.7 1.7 %fusion.1 = bf16[512]{0:T(512)(128)(2,1)S(1)} fusion(bf16[512,1152]{1,0:T(8,128)(2,1)} %param.9), kind=kLoop, calls=%fused_computation.5 | loop fusion | flops 1768960 | bytes 1180672 | tf_op jit(solution)/shard_map/reduce_sum | solution.py:112
  2.4 0.0 copy-done
  2.4 0.2 copy-done.5
  2.6 1.6 %convolution_convert_fusion.1 = bf16[512,512]{1,0:T(8,128)(2,1)} fusion(bf16[512,1152]{1,0:T(8,128)(2,1)S(1)} %copy-done.5, bf16[1152,512]{1,0:T(8,128)(2,1)S(1)} %copy-done), kind=kOutput, calls=%fused_computation.6 | convolution fusion | flops 604241920 | bytes 2883584 | tf_op jit(solution)/shard_map/dot_general | solution.py:113
  4.3 10.4 %all-to-all-start = ((bf16[8,64,512]{2,1,0:T(8,128)(2,1)}), bf16[8,64,512]{2,1,0:T(8,128)(2,1)S(1)}, u32[]{:S(2)}, u32[]{:S(2)}) async-start(bf16[8,64,512]{2,1,0:T(8,128)(2,1)} %bitcast.2), calls=%async_computation | async-start | bytes 1048576 | tf_op jit(solution)/shard_map/all_to_all | solution.py:40
  15.4 0.0 copy-done.12
  15.4 0.1 and_reduce_fusion
  15.5 8.7 %all-to-all-done = bf16[8,64,512]{2,1,0:T(8,128)(2,1)S(1)} async-done(((bf16[8,64,512]{2,1,0:T(8,128)(2,1)}), bf16[8,64,512]{2,1,0:T(8,128)(2,1)S(1)}, u32[]{:S(2)}, u32[]{:S(2)}) %all-to-all-start) | async-done | bytes 524320 | tf_op jit(solution)/shard_map/all_to_all | solution.py:40
  24.2 0.1 convert_reduce_fusion.2
  24.2 0.0 copy-done.9
  24.2 0.0 copy-start.7
  24.3 0.1 fusion.6
  24.4 0.7 broadcast_in_dim.24
  25.1 0.0 copy-done.10
  25.1 0.0 copy-done.7
  25.1 3.5 %all-to-all-start.1 = ((bf16[4,72,512]{2,1,0:T(8,128)(2,1)}), bf16[4,72,512]{2,1,0:T(8,128)(2,1)S(1)}, u32[]{:S(2)}, u32[]{:S(2)}) async-start(bf16[4,72,512]{2,1,0:T(8,128)(2,1)} %broadcast_in_dim.24), calls=%async_computation.1 | async-start | bytes 589824 | tf_op jit(solution)/shard_map/all_to_all | solution.py:40
  28.6 5.8 %all-to-all-done.1 = bf16[4,72,512]{2,1,0:T(8,128)(2,1)S(1)} async-done(((bf16[4,72,512]{2,1,0:T(8,128)(2,1)}), bf16[4,72,512]{2,1,0:T(8,128)(2,1)S(1)}, u32[]{:S(2)}, u32[]{:S(2)}) %all-to-all-start.1) | async-done | bytes 294944 | tf_op jit(solution)/shard_map/all_to_all | solution.py:40
  34.5 3.9 %all_gather.18 = bf16[576,512]{1,0:T(8,128)(2,1)S(1)} all-gather(bf16[288,512]{1,0:T(8,128)(2,1)S(1)} %bitcast.60), channel_id=1, replica_groups={{0,1},{2,3},{4,5},{6,7},{8,9},{10,11},{12,13},{14,15},{16,17},{18,19},{..., dimensions={0}, use_global_device_ids=true | all-gather | bytes 884736 | tf_op jit(solution)/shard_map/all_gather | solution.py:99
  38.4 0.1 slice_bitcast_fusion
  38.5 0.7 copy-done.4
  39.3 0.0 copy-start.1
  39.3 0.1 bitcast_select_fusion.1
  39.5 1.3 copy-done.1
  40.7 0.5 convolution_convert_fusion
  41.2 1.9 %collective-permute-start = (bf16[256,1152]{1,0:T(8,128)(2,1)S(1)}, bf16[256,1152]{1,0:T(8,128)(2,1)S(1)}, u32[]{:S(2)}, u32[]{:S(2)}) collective-permute-start(bf16[256,1152]{1,0:T(8,128)(2,1)S(1)} %convolution_convert_fusion), channel_id=1, source_target_pairs={{0,64},{8,72},{16,80},{24,88},{32,96},{40,104},{48,112},{56,120},{... | collective-permute-start | bytes 1769480 | tf_op jit(solution)/shard_map/ppermute | solution.py:140
  43.2 9.0 %collective-permute-done = bf16[256,1152]{1,0:T(8,128)(2,1)S(1)} collective-permute-done((bf16[256,1152]{1,0:T(8,128)(2,1)S(1)}, bf16[256,1152]{1,0:T(8,128)(2,1)S(1)}, u32[]{:S(2)}, u32[]{:S(2)}) %collective-permute-start) | collective-permute-done | bytes 589856 | tf_op jit(solution)/shard_map/ppermute | solution.py:140
  52.2 1.3 add_convert_fusion
  53.5 3.5 %all-to-all-start.2 = ((bf16[8,32,1152]{2,1,0:T(8,128)(2,1)}), bf16[8,32,1152]{2,1,0:T(8,128)(2,1)S(1)}, u32[]{:S(2)}, u32[]{:S(2)}) async-start(bf16[8,32,1152]{2,1,0:T(8,128)(2,1)} %bitcast.13), calls=%async_computation.2 | async-start | bytes 1179648 | tf_op jit(solution)/shard_map/all_to_all | solution.py:40
  57.1 1.4 constant_dynamic-slice_fusion.4
  58.5 11.3 %all-to-all-done.2 = bf16[8,32,1152]{2,1,0:T(8,128)(2,1)S(1)} async-done(((bf16[8,32,1152]{2,1,0:T(8,128)(2,1)}), bf16[8,32,1152]{2,1,0:T(8,128)(2,1)S(1)}, u32[]{:S(2)}, u32[]{:S(2)}) %all-to-all-start.2) | async-done | bytes 589856 | tf_op jit(solution)/shard_map/all_to_all | solution.py:40
  69.8 0.1 reduce_sum.89
  69.9 6.1 %all-gather = bf16[64,1152]{1,0:T(8,128)(2,1)S(1)} all-gather(bf16[32,1152]{1,0:T(8,128)(2,1)S(1)} %reduce_sum.89), channel_id=2, replica_groups={{0,128},{256,384},{8,136},{264,392},{16,144},{272,400},{24,152},{280,40..., dimensions={0}, use_global_device_ids=true | all-gather | bytes 221184 | tf_op jit(solution)/shard_map/all_gather | solution.py:146
  76.0 8.8 %all-gather.1 = bf16[64,1152]{1,0:T(8,128)(2,1)S(1)} all-gather(bf16[32,1152]{1,0:T(8,128)(2,1)S(1)} %reduce_sum.90), channel_id=3, replica_groups={{128,256},{0,384},{136,264},{8,392},{144,272},{16,400},{152,280},{24,40..., dimensions={0}, use_global_device_ids=true | all-gather | bytes 221184 | tf_op jit(solution)/shard_map/all_gather | solution.py:146
  84.8 0.9 subtract_convert_fusion
  85.7 0.6 copy-done.8
  86.3 0.9 broadcast_in_dim.25
  87.2 4.2 %all-to-all-start.3 = ((bf16[8,32,1152]{2,1,0:T(8,128)(2,1)}), bf16[8,32,1152]{2,1,0:T(8,128)(2,1)}, u32[]{:S(2)}, u32[]{:S(2)}) async-start(bf16[8,32,1152]{2,1,0:T(8,128)(2,1)} %broadcast_in_dim.25), calls=%async_computation.3 | async-start | bytes 1179648 | tf_op jit(solution)/shard_map/all_to_all | solution.py:40
  91.4 1.1 copy.24
  92.6 1.6 %copy.28.x_ref = bf16[1152,512]{1,0:T(8,128)(2,1)S(1)} copy(bf16[1152,512]{0,1:T(8,128)(2,1)} %bitcast.54) | data formatting | bytes 2359296 | tf_op jit(solution)/shard_map/reshape | solution.py:187
  94.1 10.1 %all-to-all-done.3 = bf16[8,32,1152]{2,1,0:T(8,128)(2,1)} async-done(((bf16[8,32,1152]{2,1,0:T(8,128)(2,1)}), bf16[8,32,1152]{2,1,0:T(8,128)(2,1)}, u32[]{:S(2)}, u32[]{:S(2)}) %all-to-all-start.3) | async-done | bytes 589856 | tf_op jit(solution)/shard_map/all_to_all | solution.py:40
  104.2 4.5 %collective-permute-start.1 = (bf16[256,1152]{1,0:T(8,128)(2,1)}, bf16[256,1152]{1,0:T(8,128)(2,1)S(1)}, u32[]{:S(2)}, u32[]{:S(2)}) collective-permute-start(bf16[256,1152]{1,0:T(8,128)(2,1)} %bitcast.19), channel_id=1, source_target_pairs={{0,64},{8,72},{16,80},{24,88},{32,96},{40,104},{48,112},{56,120},{... | collective-permute-start | bytes 1769480 | tf_op jit(solution)/shard_map/ppermute | solution.py:160
  108.7 0.9 slice_convert_fusion
  109.6 1.6 %convolution_convert_fusion.3 = bf16[256,512]{1,0:T(8,128)(2,1)S(1)} fusion(bf16[256,1152]{1,0:T(8,128)(2,1)} %bitcast.19, bf16[512,1152]{1,0:T(8,128)(2,1)S(1)} %copy-done.1), kind=kOutput, calls=%fused_computation.8 | convolution fusion | flops 302120960 | bytes 2031616 | tf_op jit(solution)/shard_map/dot_general | solution.py:163
  111.2 5.3 %collective-permute-done.1 = bf16[256,1152]{1,0:T(8,128)(2,1)S(1)} collective-permute-done((bf16[256,1152]{1,0:T(8,128)(2,1)}, bf16[256,1152]{1,0:T(8,128)(2,1)S(1)}, u32[]{:S(2)}, u32[]{:S(2)}) %collective-permute-start.1) | collective-permute-done | bytes 589856 | tf_op jit(solution)/shard_map/ppermute | solution.py:160
  116.5 0.5 broadcast_select_fusion.1
  117.0 0.3 copy-done.13
  117.3 0.1 fusion.13
  117.3 0.1 copy.27
  117.5 0.9 bitcast_select_fusion
  118.3 8.3 %all-to-all-start.4 = ((bf16[8,64,512]{2,1,0:T(8,128)(2,1)}), bf16[8,64,512]{2,1,0:T(8,128)(2,1)}, u32[]{:S(2)}, u32[]{:S(2)}) async-start(bf16[8,64,512]{2,1,0:T(8,128)(2,1)} %bitcast_select_fusion), calls=%async_computation.4 | async-start | bytes 1048576 | tf_op jit(solution)/shard_map/all_to_all | solution.py:40
  126.7 1.1 convert_reduce_fusion
  127.8 0.6 fusion.10
  128.4 1.3 constant_dynamic-slice_fusion
  129.8 6.5 %all-to-all-done.4 = bf16[8,64,512]{2,1,0:T(8,128)(2,1)} async-done(((bf16[8,64,512]{2,1,0:T(8,128)(2,1)}), bf16[8,64,512]{2,1,0:T(8,128)(2,1)}, u32[]{:S(2)}, u32[]{:S(2)}) %all-to-all-start.4) | async-done | bytes 524320 | tf_op jit(solution)/shard_map/all_to_all | solution.py:40
  136.3 1.1 convert_reduce_fusion.1
  137.4 1.0 select_convert_fusion
  138.4 0.7 broadcast_in_dim.26
  139.1 4.0 %all-to-all-start.5 = ((bf16[4,64,512]{2,1,0:T(8,128)(2,1)}), bf16[4,64,512]{2,1,0:T(8,128)(2,1)}, u32[]{:S(2)}, u32[]{:S(2)}) async-start(bf16[4,64,512]{2,1,0:T(8,128)(2,1)} %broadcast_in_dim.26), calls=%async_computation.5 | async-start | bytes 524288 | tf_op jit(solution)/shard_map/all_to_all | solution.py:40
  143.2 3.3 %fusion = bf16[512,1152]{1,0:T(8,128)(2,1)} fusion(bf16[512,1152]{1,0:T(8,128)(2,1)S(1)} %copy-done.1, bf16[256,1152]{1,0:T(8,128)(2,1)} %copy-done.13, bf16[256,1152]{1,0:T(8,128)(2,1)} %bitcast.19, f32[512]{0:T(512)S(1)} %copy-done.11, bf16[256,512]{1,0:T(8,128)(2,1)} %copy-done.3, bf16[256,512]{1,0:T(8,128)(2,1)} %copy-done.2), kind=kOutput, calls=%fused_computation.1 | convolution fusion | flops 609746944 | bytes 4065280 | tf_op jit(solution)/shard_map/dot_general | solution.py:185
  146.5 2.3 %all-to-all-done.5 = bf16[4,64,512]{2,1,0:T(8,128)(2,1)} async-done(((bf16[4,64,512]{2,1,0:T(8,128)(2,1)}), bf16[4,64,512]{2,1,0:T(8,128)(2,1)}, u32[]{:S(2)}, u32[]{:S(2)}) %all-to-all-start.5) | async-done | bytes 262176 | tf_op jit(solution)/shard_map/all_to_all | solution.py:40
  148.8 4.1 %all_gather.23.g_ref = bf16[512,512]{1,0:T(8,128)(2,1)S(1)} all-gather(bf16[256,512]{1,0:T(8,128)(2,1)} %bitcast.27), channel_id=1, replica_groups={{0,1},{2,3},{4,5},{6,7},{8,9},{10,11},{12,13},{14,15},{16,17},{18,19},{..., dimensions={0}, use_global_device_ids=true | all-gather | bytes 786432 | tf_op jit(solution)/shard_map/all_gather | solution.py:99
  152.8 2.4 %shard_map.93 = (bf16[1152,512]{1,0:T(8,128)(2,1)}, f32[512]{0:T(512)}) custom-call(bf16[1152,512]{1,0:T(8,128)(2,1)S(1)} %copy.28.x_ref, bf16[512,512]{1,0:T(8,128)(2,1)S(1)} %all_gather.23.g_ref), custom_call_target="tpu_custom_call" | custom-call | tf_op jit(solution)/shard_map/pallas_call | solution.py:56
  (26 shorter events, 0.3 us)
Async XLA Ops:
  0.6 1.8 %copy-start = (bf16[1152,512]{1,0:T(8,128)(2,1)S(1)}, bf16[1152,512]{1,0:T(8,128)(2,1)}, u32[]{:S(2)}) copy-start(bf16[1152,512]{1,0:T(8,128)(2,1)} %param.7) | copy-start | bytes 3538948
  0.6 2.0 %copy-start.5 = (bf16[512,1152]{1,0:T(8,128)(2,1)S(1)}, bf16[512,1152]{1,0:T(8,128)(2,1)}, u32[]{:S(2)}) copy-start(bf16[512,1152]{1,0:T(8,128)(2,1)} %param.6) | copy-start | bytes 3538948
  2.6 12.7 %copy-start.12 = (s32[1,32]{1,0:T(1,128)S(1)}, s32[1,32]{1,0:T(1,128)}, u32[]{:S(2)}) copy-start(s32[1,32]{1,0:T(1,128)} %param.10) | copy-start | bytes 388
  4.3 20.0 %copy-start.9 = (f32[512]{0:T(512)S(1)}, f32[512]{0:T(512)}, u32[]{:S(2)}) copy-start(f32[512]{0:T(512)} %param.8) | copy-start | bytes 6148
  4.3 19.9 %all-to-all-start = ((bf16[8,64,512]{2,1,0:T(8,128)(2,1)}), bf16[8,64,512]{2,1,0:T(8,128)(2,1)S(1)}, u32[]{:S(2)}, u32[]{:S(2)}) async-start(bf16[8,64,512]{2,1,0:T(8,128)(2,1)} %bitcast.2), calls=%async_computation | async-start | bytes 1048576 | tf_op jit(solution)/shard_map/all_to_all | solution.py:40
  15.5 9.7 %copy-start.10 = (pred[512]{0:T(512)(128)(4,1)}, pred[512]{0:T(512)(128)(4,1)S(1)}, u32[]{:S(2)}) copy-start(pred[512]{0:T(512)(128)(4,1)S(1)} %and_reduce_fusion) | copy-start | bytes 1540
  24.2 0.9 copy-start.7
  25.1 9.3 %all-to-all-start.1 = ((bf16[4,72,512]{2,1,0:T(8,128)(2,1)}), bf16[4,72,512]{2,1,0:T(8,128)(2,1)S(1)}, u32[]{:S(2)}, u32[]{:S(2)}) async-start(bf16[4,72,512]{2,1,0:T(8,128)(2,1)} %broadcast_in_dim.24), calls=%async_computation.1 | async-start | bytes 589824 | tf_op jit(solution)/shard_map/all_to_all | solution.py:40
  38.4 0.8 copy-start.4
  39.3 1.5 copy-start.1
  39.4 14.0 %copy-start.2 = (bf16[256,512]{1,0:T(8,128)(2,1)}, bf16[256,512]{1,0:T(8,128)(2,1)S(1)}, u32[]{:S(2)}) copy-start(bf16[256,512]{1,0:T(8,128)(2,1)S(1)} %get-tuple-element.25) | copy-start | bytes 786436
  39.5 14.0 %copy-start.3 = (bf16[256,512]{1,0:T(8,128)(2,1)}, bf16[256,512]{1,0:T(8,128)(2,1)S(1)}, u32[]{:S(2)}) copy-start(bf16[256,512]{1,0:T(8,128)(2,1)S(1)} %get-tuple-element.24) | copy-start | bytes 786436
  41.2 10.9 %collective-permute-start = (bf16[256,1152]{1,0:T(8,128)(2,1)S(1)}, bf16[256,1152]{1,0:T(8,128)(2,1)S(1)}, u32[]{:S(2)}, u32[]{:S(2)}) collective-permute-start(bf16[256,1152]{1,0:T(8,128)(2,1)S(1)} %convolution_convert_fusion), channel_id=1, source_target_pairs={{0,64},{8,72},{16,80},{24,88},{32,96},{40,104},{48,112},{56,120},{... | collective-permute-start | bytes 1769480 | tf_op jit(solution)/shard_map/ppermute | solution.py:140
  53.5 16.3 %all-to-all-start.2 = ((bf16[8,32,1152]{2,1,0:T(8,128)(2,1)}), bf16[8,32,1152]{2,1,0:T(8,128)(2,1)S(1)}, u32[]{:S(2)}, u32[]{:S(2)}) async-start(bf16[8,32,1152]{2,1,0:T(8,128)(2,1)} %bitcast.13), calls=%async_computation.2 | async-start | bytes 1179648 | tf_op jit(solution)/shard_map/all_to_all | solution.py:40
  84.8 6.7 %copy-start.6 = (bf16[512,1152]{1,0:T(8,128)(2,1)S(1)}, bf16[512,1152]{1,0:T(8,128)(2,1)}, u32[]{:S(2)}) copy-start(bf16[512,1152]{1,0:T(8,128)(2,1)} %param.6) | copy-start | bytes 3538948
  85.7 0.6 copy-start.8
  87.2 17.0 %all-to-all-start.3 = ((bf16[8,32,1152]{2,1,0:T(8,128)(2,1)}), bf16[8,32,1152]{2,1,0:T(8,128)(2,1)}, u32[]{:S(2)}, u32[]{:S(2)}) async-start(bf16[8,32,1152]{2,1,0:T(8,128)(2,1)} %broadcast_in_dim.25), calls=%async_computation.3 | async-start | bytes 1179648 | tf_op jit(solution)/shard_map/all_to_all | solution.py:40
  104.2 12.2 %collective-permute-start.1 = (bf16[256,1152]{1,0:T(8,128)(2,1)}, bf16[256,1152]{1,0:T(8,128)(2,1)S(1)}, u32[]{:S(2)}, u32[]{:S(2)}) collective-permute-start(bf16[256,1152]{1,0:T(8,128)(2,1)} %bitcast.19), channel_id=1, source_target_pairs={{0,64},{8,72},{16,80},{24,88},{32,96},{40,104},{48,112},{56,120},{... | collective-permute-start | bytes 1769480 | tf_op jit(solution)/shard_map/ppermute | solution.py:160
  116.5 0.8 copy-start.13
  118.3 17.9 %all-to-all-start.4 = ((bf16[8,64,512]{2,1,0:T(8,128)(2,1)}), bf16[8,64,512]{2,1,0:T(8,128)(2,1)}, u32[]{:S(2)}, u32[]{:S(2)}) async-start(bf16[8,64,512]{2,1,0:T(8,128)(2,1)} %bitcast_select_fusion), calls=%async_computation.4 | async-start | bytes 1048576 | tf_op jit(solution)/shard_map/all_to_all | solution.py:40
  128.4 14.7 %copy-start.11 = (f32[512]{0:T(512)S(1)}, f32[512]{0:T(512)}, u32[]{:S(2)}) copy-start(f32[512]{0:T(512)} %get-tuple-element.26) | copy-start | bytes 6148
  139.1 9.7 %all-to-all-start.5 = ((bf16[4,64,512]{2,1,0:T(8,128)(2,1)}), bf16[4,64,512]{2,1,0:T(8,128)(2,1)}, u32[]{:S(2)}, u32[]{:S(2)}) async-start(bf16[4,64,512]{2,1,0:T(8,128)(2,1)} %broadcast_in_dim.26), calls=%async_computation.5 | async-start | bytes 524288 | tf_op jit(solution)/shard_map/all_to_all | solution.py:40

commit v6 on v5

v6 whole, which is shorter than its diff:
```python
import jax
import jax.numpy as jnp
from jax import lax
from jax.experimental import pallas as pl
from jax.experimental.pallas import tpu as pltpu
from jax.sharding import PartitionSpec as P

BR = 128
BL = 64
PENALTY = 0.3
EPSILON = 1e-06
EXTRA = 8

f32 = jnp.float32
bf16 = jnp.bfloat16


def lat_groups(n_lat, n_tok):
    side = round(n_lat**0.5)
    quads = side // 2
    big, near, far = [], [], []
    for tok in range(n_tok):

        def device(a, p, b):
            pair = 2 * a + p
            lat = b * side + pair if tok % 2 == 1 else pair * side + b
            return lat * n_tok + tok

        for a in range(quads):
            big.append([device(a, p, b) for p in range(2) for b in range(side)])
        for p in range(2):
            for b in range(side):
                four = [device(a, p, b) for a in range(quads)]
                near += [four[:2], four[2:]]
                far += [four[1:3], [four[0], four[3]]]
    return big, near, far


def exchange(x, axis, groups):
    return lax.all_to_all(x, axis, 0, 0, axis_index_groups=groups, tiled=True)


def tail_kernel(x_ref, g_ref, out_ref, bias_ref):
    out_ref[...] = jnp.dot(x_ref[...], g_ref[...], preferred_element_type=f32).astype(bf16)

    @pl.when(pl.program_id(0) == 0)
    def _():
        ones = jnp.ones((8, g_ref.shape[0]), bf16)
        bias_ref[...] = jnp.dot(ones, g_ref[...], preferred_element_type=f32)[0]


def tail(x_t, g):
    depth, rows = x_t.shape
    cols = g.shape[1]
    step = depth // 3
    return pl.pallas_call(
        tail_kernel,
        grid=(3,),
        in_specs=[
            pl.BlockSpec((step, rows), lambda i: (i, 0)),
            pl.BlockSpec((rows, cols), lambda i: (0, 0)),
        ],
        out_specs=[
            pl.BlockSpec((step, cols), lambda i: (i, 0)),
            pl.BlockSpec((cols,), lambda i: (0,)),
        ],
        out_shape=[
            jax.ShapeDtypeStruct((depth, cols), bf16),
            jax.ShapeDtypeStruct((cols,), f32),
        ],
        compiler_params=pltpu.CompilerParams(vmem_limit_bytes=24 * 2**20),
    )(x_t, g)


def body(tokens, enc_weight, enc_bias, dec_weight, pairs, counts):
    rows, width = tokens.shape
    local_lat = enc_weight.shape[1]
    nblk = local_lat // BL
    slots = pairs.shape[1]
    n_lat = lax.axis_size("lat")
    n_tok = lax.axis_size("tok")
    lat = lax.axis_index("lat")
    tok = lax.axis_index("tok")
    own = rows // n_tok
    share = rows // n_lat
    side = round(n_lat**0.5)
    n_x = n_tok // 2
    x, core = tok // 2, tok % 2
    y, z = lat // side, lat % side
    both = ("lat", "tok")
    big, near, far = lat_groups(n_lat, n_tok)
    chunks = 2 * side
    part_rows = n_x * own
    chunk = part_rows // chunks
    x_groups = [[2 * i + c for i in range(n_x)] for c in range(2)]
    c_groups = [[2 * i, 2 * i + 1] for i in range(n_x)]

    def swap(v):
        return lax.ppermute(v, "tok", [(t, t ^ 1) for t in range(n_tok)])

    def gather_x(v):
        spread = jnp.broadcast_to(v[None], (n_x,) + v.shape)
        return exchange(spread, "tok", x_groups)

    def chunk_tokens(c):
        at = jnp.where(c == 0, y % 2 * side + z, z % 2 * side + y) * chunk
        at = (2 * (at // own) + c) * own + at % own
        return lax.dynamic_slice_in_dim(tokens, at, chunk, 0)

    codes = pairs[0]
    valid = jnp.arange(slots, dtype=jnp.int32) < counts[0]
    g_own = tok * own // BR
    hit = valid[:, None] & (
        codes[:, None] == g_own * nblk + jnp.arange(local_lat, dtype=jnp.int32)[None, :] // BL
    )
    mask = jnp.any(hit, axis=0)[None, :]

    dec32 = dec_weight.astype(f32)
    squares = jnp.sum(dec32 * dec32, axis=1)
    part = jnp.dot(tokens, enc_weight, preferred_element_type=f32).astype(bf16)
    part, squares = lax.optimization_barrier((part, squares))
    dec_came = swap(dec_weight)
    x_line = jnp.concatenate([chunk_tokens(core), swap(chunk_tokens(1 - core))], axis=1)
    dec_both = jnp.concatenate([dec_weight, dec_came], axis=1)
    came32 = dec_came.astype(f32)
    squares = (squares + jnp.sum(came32 * came32, axis=1)).astype(bf16)

    got = exchange(part.reshape(n_tok, own, local_lat), "tok", None)
    pre = jnp.sum(got.astype(f32), axis=0) + enc_bias[None, :]
    acts_own = jnp.where(mask, jax.nn.softplus(pre), 0.0).astype(bf16)
    extra = jnp.broadcast_to(squares[None, :], (EXTRA, local_lat))
    got = gather_x(jnp.concatenate([acts_own, extra], axis=0))
    acts = got[:, :own].reshape(part_rows, local_lat)
    sq = got[:, own].astype(f32)
    norm_a = jnp.sqrt(jnp.sum(sq[: n_x // 2], axis=0) + EPSILON)
    norm_b = jnp.sqrt(jnp.sum(sq[n_x // 2 :], axis=0) + EPSILON)
    own_norm = jnp.where(x < n_x // 2, norm_a, norm_b)

    recon = jnp.dot(acts, dec_both, preferred_element_type=f32).astype(bf16)
    got = exchange(recon.reshape(chunks, chunk, 2 * width), both, big)
    line = jnp.sum(got.astype(f32), axis=0).astype(bf16)
    for groups in (near, far):
        two = lax.all_gather(line, both, axis_index_groups=groups, axis=0)
        total = jnp.sum(two.astype(f32), axis=0)
        line = total.astype(bf16)
    err_line = (total - x_line.astype(f32)).astype(bf16)
    spread = jnp.broadcast_to(err_line[None], (chunks,) + err_line.shape)
    err = exchange(spread, both, big).reshape(part_rows, 2 * width)

    back = lax.dot_general(
        err, dec_both, (((1,), (1,)), ((), ())), preferred_element_type=f32
    ).astype(bf16)
    got = exchange(back.reshape(n_x, own, local_lat), "tok", x_groups)
    grad_act = jnp.sum(got.astype(f32), axis=0) + PENALTY * (norm_a + norm_b)[None, :]
    grad_own = jnp.where(mask, grad_act * jax.nn.sigmoid(pre), 0.0).astype(bf16)
    grad_pre = lax.all_gather(
        gather_x(grad_own).reshape(part_rows, local_lat),
        "tok",
        axis_index_groups=c_groups,
        axis=0,
        tiled=True,
    )

    acts_all = jnp.concatenate([acts, swap(acts)], axis=0)
    err_mine, err_came = err[:, :width], swap(err[:, width:])
    err_all = jnp.concatenate([err_mine, err_came], axis=0)
    at = jnp.where(y % 2 == core, 0, part_rows) + y // 2 * own + z * share
    err_own = lax.dynamic_slice_in_dim(err_all, at, share, 0)
    act_sum = jnp.sum(acts_all.astype(f32), axis=0)
    dec_data = lax.dot_general(
        acts_all, err_all, (((0,), (0,)), ((), ())), preferred_element_type=f32
    )
    dec_grad = dec_data + PENALTY * (act_sum / own_norm)[:, None] * dec32
    tokens_t = tokens.reshape(n_x, 2, own, width).transpose(3, 1, 0, 2).reshape(width, rows)
    enc_grad, bias_grad = tail(tokens_t, grad_pre)
    return err_own, enc_grad, dec_grad.astype(bf16), bias_grad


def solution(mesh):
    return jax.shard_map(
        body,
        mesh=mesh,
        in_specs=(
            P(None, "tok"),
            P("tok", "lat"),
            P("lat"),
            P("lat", "tok"),
            P("lat", None),
            P("lat"),
        ),
        out_specs=(P("lat", "tok"), P("tok", "lat"), P("lat", "tok"), P("lat")),
        check_vma=False,
    )
```

time: 156 us -> 161 us (1.032)
  waiting for transfers between devices: 59 us -> 44.4 us
  starting transfers between devices: 40.4 us -> 52 us
  matrix products: 8.89 us -> 11.5 us
  other arithmetic: 8.84 us -> 11 us
  local copies, waits for them, and re-layouts: 11.1 us -> 13.1 us
    ppermute x2 -> x4, starting transfers between devices: 6.37 us -> 26.8 us  [swap(): return lax.ppermute(v, 'tok', [(t, t ^ 1) for t in range(n_tok)])]
    ppermute x2 -> x4, waiting for transfers between devices: 14.3 us -> 0.57 us  [swap(): return lax.ppermute(v, 'tok', [(t, t ^ 1) for t in range(n_tok)])]
    all_to_all x6, starting transfers between devices: 34 us -> 25.3 us  [exchange(): return lax.all_to_all(x, axis, 0, 0, axis_index_groups=groups, tiled=True)]
    slice x0 -> x2, local copies, waits for them, and re-layouts: none -> 4.08 us  [the longest x1 2.41 us: body(): err_mine, err_came = (err[:, :width], swap(err[:, width:]))]
    all_gather x2, blocking collectives: 14.9 us -> 18.6 us  [body(): two = lax.all_gather(line, both, axis_index_groups=groups, axis=0)]
    all_gather x2 -> x1, blocking collectives: 7.97 us -> 4.98 us  [body(): lax.all_gather(gather_x(grad_own).reshape(part_rows, local_lat), 'tok', a...]
    reduce_sum x1, other arithmetic: 0.08 us -> 2.08 us  [body(): line = jnp.sum(got.astype(f32), axis=0).astype(bf16)]
    dot_general x5 -> x3, matrix products: 7.26 us -> 8.55 us  [the longest x1 3.03 us: body(): lax.dot_general(acts_all, err_all, (((0,), (0,)), ((), ())), preferred_el...]
  transfers between devices with their start and end apart: 8 -> 10, of which waited for: 8 -> 6; matrix products, arithmetic and copies ran while one was open for 8% -> 11% of each run, Pallas kernels for 0% -> 2%
where the time goes in v6:
time: 161 us; the launch traced here: 160 us
  starting transfers between devices  52 us (32%)
  waiting for transfers between devices  44.4 us (28%)
  blocking collectives  23.5 us (15%)
  local copies, waits for them, and re-layouts  13.1 us (8%)
  matrix products  11.5 us (7%)
  other arithmetic  11 us (7%)
  Pallas kernels  2.4 us (1%)
  between operations  1.72 us (1%)
    all_to_all x6, waiting for transfers between devices, exchange(): return lax.all_to_all(x, axis, 0, 0, axis_index_groups=groups, tiled=True)  43.9 us
    ppermute x4, starting transfers between devices, swap(): return lax.ppermute(v, 'tok', [(t, t ^ 1) for t in range(n_tok)])  26.8 us
    all_to_all x6, starting transfers between devices, exchange(): return lax.all_to_all(x, axis, 0, 0, axis_index_groups=groups, tiled=True)  25.3 us
    all_gather x2, blocking collectives, body(): two = lax.all_gather(line, both, axis_index_groups=groups, axis=0)  18.6 us
    all_gather x1, blocking collectives, body(): lax.all_gather(gather_x(grad_own).reshape(part_rows, local_lat), 'tok', a...  4.98 us
  transfers between devices with their start and end apart: 10, of which 6 were waited for; matrix products, arithmetic and copies ran while one was open for 11% of the time, Pallas kernels for 2%

profile of v6, /device:TPU:1, one launch (start us, length us, event | category | flops | bytes accessed | tf_op | source)
XLA Modules:
  0.0 159.6 jit_solution(1676774750151064375)
XLA Ops:
  0.6 0.0 copy-start
  0.6 0.0 copy-start.1
  0.7 8.9 %collective-permute-start = (bf16[512,1152]{1,0:T(8,128)(2,1)}, bf16[512,1152]{1,0:T(8,128)(2,1)}, u32[]{:S(2)}, u32[]{:S(2)}) collective-permute-start(bf16[512,1152]{1,0:T(8,128)(2,1)} %param.9), channel_id=1, source_target_pairs={{0,1},{1,0},{2,3},{3,2},{4,5},{5,4},{6,7},{7,6},{8,9},{9,8},{10,11... | collective-permute-start | bytes 3538952 | tf_op jit(solution)/shard_map/ppermute | solution.py:99
  9.6 0.0 copy-done
  9.6 2.9 %convolution_convert_fusion.1 = bf16[512,512]{1,0:T(8,128)(2,1)} fusion(bf16[512,1152]{1,0:T(8,128)(2,1)} %param.6, bf16[1152,512]{1,0:T(8,128)(2,1)S(1)} %copy-done), kind=kOutput, calls=%fused_computation.10 | convolution fusion | flops 604241920 | bytes 2883584 | tf_op jit(solution)/shard_map/dot_general | solution.py:120
  12.5 0.0 copy-done.1
  12.5 0.3 fusion.1
  12.8 4.1 %all-to-all-start = ((bf16[8,64,512]{2,1,0:T(8,128)(2,1)}), bf16[8,64,512]{2,1,0:T(8,128)(2,1)}, u32[]{:S(2)}, u32[]{:S(2)}) async-start(bf16[8,64,512]{2,1,0:T(8,128)(2,1)} %bitcast.2), calls=%async_computation | async-start | bytes 1048576 | tf_op jit(solution)/shard_map/all_to_all | solution.py:40
  17.6 0.0 copy-done.10
  17.6 0.1 and_reduce_fusion
  17.7 1.4 constant_dynamic-update-slice_fusion.1
  19.1 7.4 %all-to-all-done = bf16[8,64,512]{2,1,0:T(8,128)(2,1)} async-done(((bf16[8,64,512]{2,1,0:T(8,128)(2,1)}), bf16[8,64,512]{2,1,0:T(8,128)(2,1)}, u32[]{:S(2)}, u32[]{:S(2)}) %all-to-all-start) | async-done | bytes 524320 | tf_op jit(solution)/shard_map/all_to_all | solution.py:40
  26.5 1.1 convert_reduce_fusion.1
  27.6 0.0 copy-start.5
  27.6 0.6 copy-done.5
  28.2 0.0 copy-done.9
  28.2 0.1 fusion.3
  28.3 0.0 collective-permute-done
  28.3 1.6 multiply_reduce_fusion
  30.0 0.7 broadcast_in_dim.24
  30.7 4.1 %all-to-all-start.1 = ((bf16[4,72,512]{2,1,0:T(8,128)(2,1)}), bf16[4,72,512]{2,1,0:T(8,128)(2,1)}, u32[]{:S(2)}, u32[]{:S(2)}) async-start(bf16[4,72,512]{2,1,0:T(8,128)(2,1)} %broadcast_in_dim.24), calls=%async_computation.1 | async-start | bytes 589824 | tf_op jit(solution)/shard_map/all_to_all | solution.py:40
  34.8 1.4 constant_dynamic-update-slice_fusion
  36.2 4.5 %all-to-all-done.1 = bf16[4,72,512]{2,1,0:T(8,128)(2,1)} async-done(((bf16[4,72,512]{2,1,0:T(8,128)(2,1)}), bf16[4,72,512]{2,1,0:T(8,128)(2,1)}, u32[]{:S(2)}, u32[]{:S(2)}) %all-to-all-start.1) | async-done | bytes 294944 | tf_op jit(solution)/shard_map/all_to_all | solution.py:40
  40.8 1.7 %slice.26 = bf16[4,64,512]{2,1,0:T(8,128)(2,1)} slice(bf16[4,72,512]{2,1,0:T(8,128)(2,1)} %all-to-all-done.1), slice={[0:4], [0:64], [0:512]} | slice | bytes 524288 | tf_op jit(solution)/shard_map/slice | solution.py:133
  42.4 2.7 %convolution_convert_fusion = bf16[256,2304]{1,0:T(8,128)(2,1)} fusion(bf16[256,512]{1,0:T(8,128)(2,1)} %bitcast.3, bf16[512,2304]{1,0:T(8,128)(2,1)S(1)} %constant_dynamic-update-slice_fusion), kind=kOutput, calls=%fused_computation | convolution fusion | flops 604569600 | bytes 3801088 | tf_op jit(solution)/shard_map/dot_general | solution.py:139
  45.2 4.4 %all-to-all-start.2 = ((bf16[16,16,2304]{2,1,0:T(8,128)(2,1)}), bf16[16,16,2304]{2,1,0:T(8,128)(2,1)}, u32[]{:S(2)}, u32[]{:S(2)}) async-start(bf16[16,16,2304]{2,1,0:T(8,128)(2,1)} %bitcast.23), calls=%async_computation.2 | async-start | bytes 2359296 | tf_op jit(solution)/shard_map/all_to_all | solution.py:40
  49.7 1.5 constant_dynamic-slice_fusion.1
  51.2 6.0 %collective-permute-start.1 = (bf16[16,1152]{1,0:T(8,128)(2,1)}, bf16[16,1152]{1,0:T(8,128)(2,1)}, u32[]{:S(2)}, u32[]{:S(2)}) collective-permute-start(bf16[16,1152]{1,0:T(8,128)(2,1)} %get-tuple-element.17), channel_id=1, source_target_pairs={{0,1},{1,0},{2,3},{3,2},{4,5},{5,4},{6,7},{7,6},{8,9},{9,8},{10,11... | collective-permute-start | bytes 110600 | tf_op jit(solution)/shard_map/ppermute | solution.py:99
  57.3 13.8 %all-to-all-done.2 = bf16[16,16,2304]{2,1,0:T(8,128)(2,1)} async-done(((bf16[16,16,2304]{2,1,0:T(8,128)(2,1)}), bf16[16,16,2304]{2,1,0:T(8,128)(2,1)}, u32[]{:S(2)}, u32[]{:S(2)}) %all-to-all-start.2) | async-done | bytes 1179680 | tf_op jit(solution)/shard_map/all_to_all | solution.py:40
  71.0 2.1 %reduce_sum.99 = bf16[16,2304]{1,0:T(8,128)(2,1)} reduce(bf16[16,16,2304]{2,1,0:T(8,128)(2,1)} %all-to-all-done.2, bf16[]{:T(256)} %constant.137.clone.1), dimensions={0}, to_apply=%region_4.5 | reduce | flops 552960 | bytes 1253378 | tf_op jit(solution)/shard_map/reduce_sum | solution.py:141
  73.1 9.9 %all-gather = bf16[32,2304]{1,0:T(8,128)(2,1)} all-gather(bf16[16,2304]{1,0:T(8,128)(2,1)} %reduce_sum.99), channel_id=2, replica_groups={{0,128},{256,384},{8,136},{264,392},{16,144},{272,400},{24,152},{280,40..., dimensions={0}, use_global_device_ids=true | all-gather | bytes 221184 | tf_op jit(solution)/shard_map/all_gather | solution.py:143
  83.0 1.6 reduce_sum.100
  84.6 8.6 %all-gather.1 = bf16[32,2304]{1,0:T(8,128)(2,1)S(1)} all-gather(bf16[16,2304]{1,0:T(8,128)(2,1)} %reduce_sum.100), channel_id=3, replica_groups={{128,256},{0,384},{136,264},{8,392},{144,272},{16,400},{152,280},{24,40..., dimensions={0}, use_global_device_ids=true | all-gather | bytes 221184 | tf_op jit(solution)/shard_map/all_gather | solution.py:143
  93.3 0.0 collective-permute-done.1
  93.3 0.8 subtract_convert_fusion
  94.1 1.1 broadcast_in_dim.25
  95.2 4.8 %all-to-all-start.3 = ((bf16[16,16,2304]{2,1,0:T(8,128)(2,1)}), bf16[16,16,2304]{2,1,0:T(8,128)(2,1)}, u32[]{:S(2)}, u32[]{:S(2)}) async-start(bf16[16,16,2304]{2,1,0:T(8,128)(2,1)} %broadcast_in_dim.25), calls=%async_computation.3 | async-start | bytes 2359296 | tf_op jit(solution)/shard_map/all_to_all | solution.py:40
  100.0 5.7 %collective-permute-start.3 = (bf16[256,512]{1,0:T(8,128)(2,1)}, bf16[256,512]{1,0:T(8,128)(2,1)S(1)}, u32[]{:S(2)}, u32[]{:S(2)}) collective-permute-start(bf16[256,512]{1,0:T(8,128)(2,1)} %bitcast.3), channel_id=1, source_target_pairs={{0,1},{1,0},{2,3},{3,2},{4,5},{5,4},{6,7},{7,6},{8,9},{9,8},{10,11... | collective-permute-start | bytes 786440 | tf_op jit(solution)/shard_map/ppermute | solution.py:99
  105.7 0.8 slice_convert_fusion
  106.5 0.6 collective-permute-done.3
  107.1 0.7 copy-done.7
  107.8 1.1 convert_reduce_fusion
  108.9 13.3 %all-to-all-done.3 = bf16[16,16,2304]{2,1,0:T(8,128)(2,1)} async-done(((bf16[16,16,2304]{2,1,0:T(8,128)(2,1)}), bf16[16,16,2304]{2,1,0:T(8,128)(2,1)}, u32[]{:S(2)}, u32[]{:S(2)}) %all-to-all-start.3) | async-done | bytes 1179680 | tf_op jit(solution)/shard_map/all_to_all | solution.py:40
  122.2 2.8 %convolution_convert_fusion.2 = bf16[256,512]{1,0:T(8,128)(2,1)} fusion(bf16[256,2304]{1,0:T(8,128)(2,1)} %bitcast.7, bf16[512,2304]{1,0:T(8,128)(2,1)S(1)} %constant_dynamic-update-slice_fusion), kind=kOutput, calls=%fused_computation.11 | convolution fusion | flops 604110848 | bytes 3801088 | tf_op jit(solution)/shard_map/dot_general | solution.py:150
  125.0 3.4 %all-to-all-start.4 = ((bf16[4,64,512]{2,1,0:T(8,128)(2,1)}), bf16[4,64,512]{2,1,0:T(8,128)(2,1)S(1)}, u32[]{:S(2)}, u32[]{:S(2)}) async-start(bf16[4,64,512]{2,1,0:T(8,128)(2,1)} %bitcast.27), calls=%async_computation.4 | async-start | bytes 524288 | tf_op jit(solution)/shard_map/all_to_all | solution.py:40
  128.4 0.0 copy-start.6
  128.4 2.4 %fusion.11 = (bf16[256,1152]{1,0:T(8,128)(2,1)}, bf16[256,1152]{1,0:T(8,128)(2,1)}) fusion(bf16[256,2304]{1,0:T(8,128)(2,1)} %bitcast.7), kind=kLoop, calls=%fused_computation.48 | loop fusion | bytes 2359296 | tf_op jit(solution)/shard_map/slice | solution.py:165
  130.8 6.1 %collective-permute-start.2 = (bf16[256,1152]{1,0:T(8,128)(2,1)}, bf16[256,1152]{1,0:T(8,128)(2,1)}, u32[]{:S(2)}, u32[]{:S(2)}) collective-permute-start(bf16[256,1152]{1,0:T(8,128)(2,1)} %get-tuple-element.14), channel_id=1, source_target_pairs={{0,1},{1,0},{2,3},{3,2},{4,5},{5,4},{6,7},{7,6},{8,9},{9,8},{10,11... | collective-permute-start | bytes 1769480 | tf_op jit(solution)/shard_map/ppermute | solution.py:99
  136.9 0.0 all-to-all-done.4
  137.0 0.0 copy-done.6
  137.0 0.1 select_convert_fusion
  137.0 0.7 broadcast_in_dim.26
  137.8 4.5 %all-to-all-start.5 = ((bf16[4,64,512]{2,1,0:T(8,128)(2,1)}), bf16[4,64,512]{2,1,0:T(8,128)(2,1)}, u32[]{:S(2)}, u32[]{:S(2)}) async-start(bf16[4,64,512]{2,1,0:T(8,128)(2,1)} %broadcast_in_dim.26), calls=%async_computation.5 | async-start | bytes 524288 | tf_op jit(solution)/shard_map/all_to_all | solution.py:40
  142.2 0.0 copy-done.4
  142.2 0.1 copy.17
  142.3 0.6 copy.20.x_ref
  143.0 4.9 %all-to-all-done.5 = bf16[4,64,512]{2,1,0:T(8,128)(2,1)} async-done(((bf16[4,64,512]{2,1,0:T(8,128)(2,1)}), bf16[4,64,512]{2,1,0:T(8,128)(2,1)}, u32[]{:S(2)}, u32[]{:S(2)}) %all-to-all-start.5) | async-done | bytes 262176 | tf_op jit(solution)/shard_map/all_to_all | solution.py:40
  147.9 5.0 %all_gather.19.g_ref = bf16[512,512]{1,0:T(8,128)(2,1)S(1)} all-gather(bf16[256,512]{1,0:T(8,128)(2,1)} %bitcast.12), channel_id=1, replica_groups={{0,1},{2,3},{4,5},{6,7},{8,9},{10,11},{12,13},{14,15},{16,17},{18,19},{..., dimensions={0}, use_global_device_ids=true | all-gather | bytes 786432 | tf_op jit(solution)/shard_map/all_gather | solution.py:156
  152.9 2.4 %shard_map.93 = (bf16[1152,512]{1,0:T(8,128)(2,1)}, f32[512]{0:T(512)}) custom-call(bf16[1152,512]{1,0:T(8,128)(2,1)S(1)} %copy.20.x_ref, bf16[512,512]{1,0:T(8,128)(2,1)S(1)} %all_gather.19.g_ref), custom_call_target="tpu_custom_call" | custom-call | tf_op jit(solution)/shard_map/pallas_call | solution.py:56
  155.3 0.0 collective-permute-done.2
  155.3 0.0 copy-done.2
  155.3 0.0 copy-done.3
  155.3 3.0 %fusion = bf16[512,1152]{1,0:T(8,128)(2,1)} fusion(bf16[512,1152]{1,0:T(8,128)(2,1)S(1)} %copy-done.2, bf16[256,1152]{1,0:T(8,128)(2,1)} %collective-permute-done.2, bf16[256,1152]{1,0:T(8,128)(2,1)S(1)} %copy-done.3, f32[512]{0:T(512)S(1)} %get-tuple-element.18, bf16[256,512]{1,0:T(8,128)(2,1)S(1)} %copy-done.8, bf16[256,512]{1,0:T(8,128)(2,1)} %bitcast.3), kind=kOutput, calls=%fused_computation.2 | convolution fusion | flops 609746944 | bytes 4065280 | tf_op jit(solution)/shard_map/dot_general | solution.py:170
  158.3 1.3 fusion.4
  (17 shorter events, 0.1 us)
Async XLA Ops:
  0.6 9.0 %copy-start = (bf16[1152,512]{1,0:T(8,128)(2,1)S(1)}, bf16[1152,512]{1,0:T(8,128)(2,1)}, u32[]{:S(2)}) copy-start(bf16[1152,512]{1,0:T(8,128)(2,1)} %param.7) | copy-start | bytes 3538948
  0.6 11.9 %copy-start.1 = (bf16[512,1152]{1,0:T(8,128)(2,1)S(1)}, bf16[512,1152]{1,0:T(8,128)(2,1)}, u32[]{:S(2)}) copy-start(bf16[512,1152]{1,0:T(8,128)(2,1)} %param.9) | copy-start | bytes 3538948
  0.7 27.7 %collective-permute-start = (bf16[512,1152]{1,0:T(8,128)(2,1)}, bf16[512,1152]{1,0:T(8,128)(2,1)}, u32[]{:S(2)}, u32[]{:S(2)}) collective-permute-start(bf16[512,1152]{1,0:T(8,128)(2,1)} %param.9), channel_id=1, source_target_pairs={{0,1},{1,0},{2,3},{3,2},{4,5},{5,4},{6,7},{7,6},{8,9},{9,8},{10,11... | collective-permute-start | bytes 3538952 | tf_op jit(solution)/shard_map/ppermute | solution.py:99
  12.5 5.1 %copy-start.10 = (s32[1,32]{1,0:T(1,128)S(1)}, s32[1,32]{1,0:T(1,128)}, u32[]{:S(2)}) copy-start(s32[1,32]{1,0:T(1,128)} %param.10) | copy-start | bytes 388
  12.8 13.6 %all-to-all-start = ((bf16[8,64,512]{2,1,0:T(8,128)(2,1)}), bf16[8,64,512]{2,1,0:T(8,128)(2,1)}, u32[]{:S(2)}, u32[]{:S(2)}) async-start(bf16[8,64,512]{2,1,0:T(8,128)(2,1)} %bitcast.2), calls=%async_computation | async-start | bytes 1048576 | tf_op jit(solution)/shard_map/all_to_all | solution.py:40
  17.7 10.5 %copy-start.9 = (f32[512]{0:T(512)S(1)}, f32[512]{0:T(512)}, u32[]{:S(2)}) copy-start(f32[512]{0:T(512)} %param.8) | copy-start | bytes 6148
  27.6 0.7 copy-start.5
  30.7 10.1 %all-to-all-start.1 = ((bf16[4,72,512]{2,1,0:T(8,128)(2,1)}), bf16[4,72,512]{2,1,0:T(8,128)(2,1)}, u32[]{:S(2)}, u32[]{:S(2)}) async-start(bf16[4,72,512]{2,1,0:T(8,128)(2,1)} %broadcast_in_dim.24), calls=%async_computation.1 | async-start | bytes 589824 | tf_op jit(solution)/shard_map/all_to_all | solution.py:40
  45.2 25.8 %all-to-all-start.2 = ((bf16[16,16,2304]{2,1,0:T(8,128)(2,1)}), bf16[16,16,2304]{2,1,0:T(8,128)(2,1)}, u32[]{:S(2)}, u32[]{:S(2)}) async-start(bf16[16,16,2304]{2,1,0:T(8,128)(2,1)} %bitcast.23), calls=%async_computation.2 | async-start | bytes 2359296 | tf_op jit(solution)/shard_map/all_to_all | solution.py:40
  51.2 42.1 %collective-permute-start.1 = (bf16[16,1152]{1,0:T(8,128)(2,1)}, bf16[16,1152]{1,0:T(8,128)(2,1)}, u32[]{:S(2)}, u32[]{:S(2)}) collective-permute-start(bf16[16,1152]{1,0:T(8,128)(2,1)} %get-tuple-element.17), channel_id=1, source_target_pairs={{0,1},{1,0},{2,3},{3,2},{4,5},{5,4},{6,7},{7,6},{8,9},{9,8},{10,11... | collective-permute-start | bytes 110600 | tf_op jit(solution)/shard_map/ppermute | solution.py:99
  95.2 27.0 %all-to-all-start.3 = ((bf16[16,16,2304]{2,1,0:T(8,128)(2,1)}), bf16[16,16,2304]{2,1,0:T(8,128)(2,1)}, u32[]{:S(2)}, u32[]{:S(2)}) async-start(bf16[16,16,2304]{2,1,0:T(8,128)(2,1)} %broadcast_in_dim.25), calls=%async_computation.3 | async-start | bytes 2359296 | tf_op jit(solution)/shard_map/all_to_all | solution.py:40
  100.0 7.1 %collective-permute-start.3 = (bf16[256,512]{1,0:T(8,128)(2,1)}, bf16[256,512]{1,0:T(8,128)(2,1)S(1)}, u32[]{:S(2)}, u32[]{:S(2)}) collective-permute-start(bf16[256,512]{1,0:T(8,128)(2,1)} %bitcast.3), channel_id=1, source_target_pairs={{0,1},{1,0},{2,3},{3,2},{4,5},{5,4},{6,7},{7,6},{8,9},{9,8},{10,11... | collective-permute-start | bytes 786440 | tf_op jit(solution)/shard_map/ppermute | solution.py:99
  107.1 0.7 copy-start.7
  125.0 11.9 %all-to-all-start.4 = ((bf16[4,64,512]{2,1,0:T(8,128)(2,1)}), bf16[4,64,512]{2,1,0:T(8,128)(2,1)S(1)}, u32[]{:S(2)}, u32[]{:S(2)}) async-start(bf16[4,64,512]{2,1,0:T(8,128)(2,1)} %bitcast.27), calls=%async_computation.4 | async-start | bytes 524288 | tf_op jit(solution)/shard_map/all_to_all | solution.py:40
  128.4 8.6 %copy-start.6 = (f32[64,512]{1,0:T(8,128)S(1)}, f32[64,512]{1,0:T(8,128)}, u32[]{:S(2)}) copy-start(f32[64,512]{1,0:T(8,128)} %copy-done.5) | copy-start | bytes 393220
  130.8 11.4 %copy-start.4 = (bf16[512,1152]{1,0:T(8,128)(2,1)S(1)}, bf16[512,1152]{1,0:T(8,128)(2,1)}, u32[]{:S(2)}) copy-start(bf16[512,1152]{1,0:T(8,128)(2,1)} %param.6) | copy-start | bytes 3538948
  130.8 24.4 %collective-permute-start.2 = (bf16[256,1152]{1,0:T(8,128)(2,1)}, bf16[256,1152]{1,0:T(8,128)(2,1)}, u32[]{:S(2)}, u32[]{:S(2)}) collective-permute-start(bf16[256,1152]{1,0:T(8,128)(2,1)} %get-tuple-element.14), channel_id=1, source_target_pairs={{0,1},{1,0},{2,3},{3,2},{4,5},{5,4},{6,7},{7,6},{8,9},{9,8},{10,11... | collective-permute-start | bytes 1769480 | tf_op jit(solution)/shard_map/ppermute | solution.py:99
  137.8 10.1 %all-to-all-start.5 = ((bf16[4,64,512]{2,1,0:T(8,128)(2,1)}), bf16[4,64,512]{2,1,0:T(8,128)(2,1)}, u32[]{:S(2)}, u32[]{:S(2)}) async-start(bf16[4,64,512]{2,1,0:T(8,128)(2,1)} %broadcast_in_dim.26), calls=%async_computation.5 | async-start | bytes 524288 | tf_op jit(solution)/shard_map/all_to_all | solution.py:40
  147.9 7.4 %copy-start.2 = (bf16[512,1152]{1,0:T(8,128)(2,1)S(1)}, bf16[512,1152]{1,0:T(8,128)(2,1)}, u32[]{:S(2)}) copy-start(bf16[512,1152]{1,0:T(8,128)(2,1)} %param.9) | copy-start | bytes 3538948
  147.9 7.4 %copy-start.3 = (bf16[256,1152]{1,0:T(8,128)(2,1)S(1)}, bf16[256,1152]{1,0:T(8,128)(2,1)}, u32[]{:S(2)}) copy-start(bf16[256,1152]{1,0:T(8,128)(2,1)} %get-tuple-element.15) | copy-start | bytes 1769476
  147.9 7.4 %copy-start.8 = (bf16[256,512]{1,0:T(8,128)(2,1)S(1)}, bf16[256,512]{1,0:T(8,128)(2,1)}, u32[]{:S(2)}) copy-start(bf16[256,512]{1,0:T(8,128)(2,1)} %copy-done.7) | copy-start | bytes 786436

commit v7 on v4

v7 whole, which is shorter than its diff:
```python
import jax
import jax.numpy as jnp
from jax import lax
from jax.experimental import pallas as pl
from jax.experimental.pallas import tpu as pltpu
from jax.sharding import PartitionSpec as P

BR = 128
BL = 64
PENALTY = 0.3
EPSILON = 1e-06
EXTRA = 8

f32 = jnp.float32
bf16 = jnp.bfloat16


def lat_groups(n_lat, n_tok):
    side = round(n_lat**0.5)
    quads = side // 2
    big, near, far = [], [], []
    for tok in range(n_tok):
        swap = tok % 2 == 1

        def device(a, p, b):
            pair = 2 * a + p
            lat = b * side + pair if swap else pair * side + b
            return lat * n_tok + tok

        for a in range(quads):
            big.append([device(a, p, b) for p in range(2) for b in range(side)])
        for p in range(2):
            for b in range(side):
                four = [device(a, p, b) for a in range(quads)]
                near += [four[:2], four[2:]]
                far += [four[1:3], [four[0], four[3]]]
    return big, near, far


def exchange(x, axis, groups):
    return lax.all_to_all(x, axis, 0, 0, axis_index_groups=groups, tiled=True)


def tail_kernel(x_ref, g_ref, out_ref, bias_ref):
    out_ref[...] = jnp.dot(x_ref[...], g_ref[...], preferred_element_type=f32).astype(bf16)

    @pl.when(pl.program_id(0) == 0)
    def _():
        ones = jnp.ones((8, g_ref.shape[0]), bf16)
        bias_ref[...] = jnp.dot(ones, g_ref[...], preferred_element_type=f32)[0]


def tail(x_t, g):
    depth, rows = x_t.shape
    cols = g.shape[1]
    step = depth // 3
    return pl.pallas_call(
        tail_kernel,
        grid=(3,),
        in_specs=[
            pl.BlockSpec((step, rows), lambda i: (i, 0)),
            pl.BlockSpec((rows, cols), lambda i: (0, 0)),
        ],
        out_specs=[
            pl.BlockSpec((step, cols), lambda i: (i, 0)),
            pl.BlockSpec((cols,), lambda i: (0,)),
        ],
        out_shape=[
            jax.ShapeDtypeStruct((depth, cols), bf16),
            jax.ShapeDtypeStruct((cols,), f32),
        ],
        compiler_params=pltpu.CompilerParams(vmem_limit_bytes=24 * 2**20),
    )(x_t, g)


def body(tokens, enc_weight, enc_bias, dec_weight, pairs, counts):
    rows, width = tokens.shape
    local_lat = enc_weight.shape[1]
    nblk = local_lat // BL
    slots = pairs.shape[1]
    n_lat = lax.axis_size("lat")
    n_tok = lax.axis_size("tok")
    lat = lax.axis_index("lat")
    tok = lax.axis_index("tok")
    half = tok * 2 // n_tok
    own = rows // n_tok
    share = rows // n_lat
    side = round(n_lat**0.5)
    n_x = n_tok // 2
    even = tok % 2 == 0
    y, z = lat // side, lat % side
    chunks = 2 * side
    chunk = rows // chunks
    both = ("lat", "tok")
    big, near, far = lat_groups(n_lat, n_tok)
    x_groups = [[2 * x + c for x in range(n_x)] for c in range(2)]
    c_groups = [[2 * x, 2 * x + 1] for x in range(n_x)]

    def gather_tok(v):
        spread = jnp.broadcast_to(v[None], (n_x,) + v.shape)
        got = exchange(spread, "tok", x_groups)
        return lax.all_gather(
            got.reshape(-1, local_lat), "tok", axis_index_groups=c_groups, axis=0, tiled=True
        )

    codes = pairs[0]
    valid = jnp.arange(slots, dtype=jnp.int32) < counts[0]
    g_own = tok * own // BR
    hit = valid[:, None] & (
        codes[:, None] == g_own * nblk + jnp.arange(local_lat, dtype=jnp.int32)[None, :] // BL
    )
    mask = jnp.any(hit, axis=0)[None, :]

    dec32 = dec_weight.astype(f32)
    squares = jnp.sum(dec32 * dec32, axis=1).astype(bf16)
    part = jnp.dot(tokens, enc_weight, preferred_element_type=f32).astype(bf16)
    part, squares = lax.optimization_barrier((part, squares))
    got = exchange(part.reshape(n_tok, own, local_lat), "tok", None)
    pre = jnp.sum(got.astype(f32), axis=0) + enc_bias[None, :]
    acts_own = jnp.where(mask, jax.nn.softplus(pre), 0.0).astype(bf16)
    extra = jnp.broadcast_to(squares[None, :], (EXTRA, local_lat))
    got = gather_tok(jnp.concatenate([acts_own, extra], axis=0))
    got = got.reshape(2, n_x, own + EXTRA, local_lat)
    acts = got[:, :, :own].reshape(rows, local_lat)
    sq = got[:, :, own].astype(f32)
    norm_a = jnp.sqrt(jnp.sum(sq[:, : n_x // 2], axis=(0, 1)) + EPSILON)
    norm_b = jnp.sqrt(jnp.sum(sq[:, n_x // 2 :], axis=(0, 1)) + EPSILON)
    own_norm = jnp.where(half == 0, norm_a, norm_b)

    recon = jnp.dot(acts, dec_weight, preferred_element_type=f32).astype(bf16)
    got = exchange(recon.reshape(chunks, chunk, width), both, big)
    line = jnp.sum(got.astype(f32), axis=0).astype(bf16)
    for groups in (near, far):
        two = lax.all_gather(line, both, axis_index_groups=groups, axis=0)
        total = jnp.sum(two.astype(f32), axis=0)
        line = total.astype(bf16)
    at = jnp.where(even, y % 2 * side + z, z % 2 * side + y) * chunk
    at = 2 * (at // own % n_x) * own + at // (n_x * own) * own + at % own
    x_line = lax.dynamic_slice_in_dim(tokens, at, chunk, 0)
    err_line = (total - x_line.astype(f32)).astype(bf16)
    err = exchange(jnp.broadcast_to(err_line[None], (chunks,) + err_line.shape), both, big)
    err = err.reshape(rows, width)

    back = lax.dot_general(
        err, dec_weight, (((1,), (1,)), ((), ())), preferred_element_type=f32
    ).astype(bf16)
    order = [[tok for group in x_groups for tok in group]]
    got = exchange(back.reshape(n_tok, own, local_lat), "tok", order)
    err_own = lax.dynamic_slice_in_dim(
        err, (y % 2 * n_x + y // 2) * own + z * share, share, 0
    )
    grad_act = jnp.sum(got.astype(f32), axis=0) + PENALTY * (norm_a + norm_b)[None, :]
    grad_own = jnp.where(mask, grad_act * jax.nn.sigmoid(pre), 0.0).astype(bf16)
    grad_pre = gather_tok(grad_own)

    act_sum = jnp.sum(acts.astype(f32), axis=0)
    dec_data = lax.dot_general(acts, err, (((0,), (0,)), ((), ())), preferred_element_type=f32)
    dec_grad = dec_data + PENALTY * (act_sum / own_norm)[:, None] * dec32
    tokens_t = tokens.reshape(n_x, 2, own, width).transpose(3, 1, 0, 2).reshape(width, rows)
    enc_grad, bias_grad = tail(tokens_t, grad_pre)
    return err_own, enc_grad, dec_grad.astype(bf16), bias_grad


def solution(mesh):
    return jax.shard_map(
        body,
        mesh=mesh,
        in_specs=(
            P(None, "tok"),
            P("tok", "lat"),
            P("lat"),
            P("lat", "tok"),
            P("lat", None),
            P("lat"),
        ),
        out_specs=(P("lat", "tok"), P("tok", "lat"), P("lat", "tok"), P("lat")),
        check_vma=False,
    )
```

time: 153 us -> 149 us (0.974)
  blocking collectives: 22.9 us -> 31 us
  waiting for transfers between devices: 69 us -> 62.6 us
  local copies, waits for them, and re-layouts: 9.34 us -> 5.03 us
  starting transfers between devices: 33.4 us -> 29.9 us
  matrix products: 7.52 us -> 10.4 us
  Pallas kernels: 4.94 us -> 2.4 us
  other arithmetic: 2.97 us -> 5.07 us
    all_to_all x0 -> x1, blocking collectives: none -> 8.4 us  [exchange(): return lax.all_to_all(x, axis, 0, 0, axis_index_groups=groups, tiled=True)]
    all_to_all x6 -> x5, waiting for transfers between devices: 69 us -> 62.6 us  [exchange(): return lax.all_to_all(x, axis, 0, 0, axis_index_groups=groups, tiled=True)]
    all_to_all x6 -> x5, starting transfers between devices: 33.4 us -> 29.9 us  [exchange(): return lax.all_to_all(x, axis, 0, 0, axis_index_groups=groups, tiled=True)]
    unnamed x25 -> x23, local copies, waits for them, and re-layouts: 3.84 us -> 1.09 us
    pallas_call x1 -> x0, Pallas kernels: 2.55 us -> none  [head(): pl.pallas_call(head_kernel, grid=(3,), in_specs=[pl.BlockSpec((rows, step...]
    dot_general x2 -> x3, matrix products: 5.37 us -> 7.04 us  [the longest x1 3.55 us: body(): lax.dot_general(acts, err, (((0,), (0,)), ((), ())), preferred_element_ty...]
  transfers between devices with their start and end apart: 6 -> 5, of which waited for: 6 -> 5; matrix products, arithmetic and copies ran while one was open for 5% -> 5% of each run, Pallas kernels for 0% -> 0%
where the time goes in v7:
time: 149 us; the launch traced here: 148 us
  waiting for transfers between devices  62.6 us (42%)
  blocking collectives  31 us (21%)
  starting transfers between devices  29.9 us (20%)
  matrix products  10.4 us (7%)
  other arithmetic  5.07 us (3%)
  local copies, waits for them, and re-layouts  5.03 us (3%)
  Pallas kernels  2.4 us (2%)
  between operations  1.73 us (1%)
    all_to_all x5, waiting for transfers between devices, exchange(): return lax.all_to_all(x, axis, 0, 0, axis_index_groups=groups, tiled=True)  62.6 us
    all_to_all x5, starting transfers between devices, exchange(): return lax.all_to_all(x, axis, 0, 0, axis_index_groups=groups, tiled=True)  29.9 us
    all_gather x2, blocking collectives, body(): two = lax.all_gather(line, both, axis_index_groups=groups, axis=0)  15.4 us
    all_to_all x1, blocking collectives, exchange(): return lax.all_to_all(x, axis, 0, 0, axis_index_groups=groups, tiled=True)  8.4 us
    all_gather x2, blocking collectives, gather_tok(): lax.all_gather(got.reshape(-1, local_lat), 'tok', axis_index_groups=c_gro...  7.19 us
    dot_general x1, matrix products, body(): lax.dot_general(acts, err, (((0,), (0,)), ((), ())), preferred_element_ty...  3.55 us
    dot_general x1, matrix products, body(): lax.dot_general(err, dec_weight, (((1,), (1,)), ((), ())), preferred_elem...  3.35 us
  transfers between devices with their start and end apart: 5, of which 5 were waited for; matrix products, arithmetic and copies ran while one was open for 5% of the time, Pallas kernels for 0%

profile of v7, /device:TPU:1, one launch (start us, length us, event | category | flops | bytes accessed | tf_op | source)
XLA Modules:
  0.0 148.2 jit_solution(6753104625283802205)
XLA Ops:
  0.6 0.0 copy-start
  0.6 0.0 copy-start.2
  0.7 1.7 %fusion.1 = bf16[512]{0:T(512)(128)(2,1)S(1)} fusion(bf16[512,1152]{1,0:T(8,128)(2,1)} %param.9), kind=kLoop, calls=%fused_computation.5 | loop fusion | flops 1768960 | bytes 1180672 | tf_op jit(solution)/shard_map/reduce_sum | solution.py:115
  2.4 0.0 copy-done
  2.4 0.2 copy-done.2
  2.6 0.0 copy-start.10
  2.6 1.6 %convolution_convert_fusion.2 = bf16[512,512]{1,0:T(8,128)(2,1)} fusion(bf16[512,1152]{1,0:T(8,128)(2,1)S(1)} %copy-done.2, bf16[1152,512]{1,0:T(8,128)(2,1)S(1)} %copy-done), kind=kOutput, calls=%fused_computation.7 | convolution fusion | flops 604241920 | bytes 2883584 | tf_op jit(solution)/shard_map/dot_general | solution.py:116
  4.3 0.0 copy-start.9
  4.3 10.4 %all-to-all-start = ((bf16[8,64,512]{2,1,0:T(8,128)(2,1)}), bf16[8,64,512]{2,1,0:T(8,128)(2,1)S(1)}, u32[]{:S(2)}, u32[]{:S(2)}) async-start(bf16[8,64,512]{2,1,0:T(8,128)(2,1)} %bitcast.2), calls=%async_computation | async-start | bytes 1048576 | tf_op jit(solution)/shard_map/all_to_all | solution.py:41
  15.4 0.0 copy-done.10
  15.4 0.1 and_reduce_fusion
  15.5 8.7 %all-to-all-done = bf16[8,64,512]{2,1,0:T(8,128)(2,1)S(1)} async-done(((bf16[8,64,512]{2,1,0:T(8,128)(2,1)}), bf16[8,64,512]{2,1,0:T(8,128)(2,1)S(1)}, u32[]{:S(2)}, u32[]{:S(2)}) %all-to-all-start) | async-done | bytes 524320 | tf_op jit(solution)/shard_map/all_to_all | solution.py:41
  24.2 0.1 convert_reduce_fusion.2
  24.2 0.0 copy-done.9
  24.2 0.0 copy-start.4
  24.3 0.1 fusion.3
  24.4 0.0 copy-start.6
  24.4 8.4 %all_to_all.30 = bf16[4,72,512]{2,1,0:T(8,128)(2,1)S(1)} all-to-all(bf16[4,72,512]{2,1,0:T(8,128)(2,1)S(1)} %broadcast_in_dim.24), channel_id=1, replica_groups={{0,2,4,6},{1,3,5,7},{8,10,12,14},{9,11,13,15},{16,18,20,22},{17,19,21,2..., dimensions={0} | all-to-all | bytes 589824 | tf_op jit(solution)/shard_map/all_to_all | solution.py:41
  32.8 3.9 %all_gather.18 = bf16[576,512]{1,0:T(8,128)(2,1)S(1)} all-gather(bf16[288,512]{1,0:T(8,128)(2,1)S(1)} %bitcast.34), channel_id=1, replica_groups={{0,1},{2,3},{4,5},{6,7},{8,9},{10,11},{12,13},{14,15},{16,17},{18,19},{..., dimensions={0}, use_global_device_ids=true | all-gather | bytes 884736 | tf_op jit(solution)/shard_map/all_gather | solution.py:102
  36.7 0.0 copy-start.1
  36.7 0.8 copy-done.1
  37.6 0.0 copy-done.4
  37.6 0.0 copy-start.7
  37.6 0.0 copy-done.6
  37.6 1.9 %convolution_convert_fusion = bf16[512,1152]{1,0:T(8,128)(2,1)} fusion(bf16[512,512]{1,0:T(8,128)(2,1)S(1)} %bitcast.39, bf16[512,1152]{1,0:T(8,128)(2,1)S(1)} %copy-done.6), kind=kOutput, calls=%fused_computation.2 | convolution fusion | flops 604569600 | bytes 2883584 | tf_op jit(solution)/shard_map/dot_general | solution.py:130
  39.5 0.0 copy-done.7
  39.5 4.2 %all-to-all-start.2 = ((bf16[16,32,1152]{2,1,0:T(8,128)(2,1)}), bf16[16,32,1152]{2,1,0:T(8,128)(2,1)S(1)}, u32[]{:S(2)}, u32[]{:S(2)}) async-start(bf16[16,32,1152]{2,1,0:T(8,128)(2,1)} %bitcast.35), calls=%async_computation.2 | async-start | bytes 2359296 | tf_op jit(solution)/shard_map/all_to_all | solution.py:41
  43.9 22.7 %all-to-all-done.2 = bf16[16,32,1152]{2,1,0:T(8,128)(2,1)S(1)} async-done(((bf16[16,32,1152]{2,1,0:T(8,128)(2,1)}), bf16[16,32,1152]{2,1,0:T(8,128)(2,1)S(1)}, u32[]{:S(2)}, u32[]{:S(2)}) %all-to-all-start.2) | async-done | bytes 1179680 | tf_op jit(solution)/shard_map/all_to_all | solution.py:41
  66.5 0.8 reduce_sum.89
  67.3 7.5 %all-gather = bf16[64,1152]{1,0:T(8,128)(2,1)S(1)} all-gather(bf16[32,1152]{1,0:T(8,128)(2,1)} %reduce_sum.89), channel_id=2, replica_groups={{0,128},{256,384},{8,136},{264,392},{16,144},{272,400},{24,152},{280,40..., dimensions={0}, use_global_device_ids=true | all-gather | bytes 221184 | tf_op jit(solution)/shard_map/all_gather | solution.py:134
  74.9 7.9 %all-gather.1 = bf16[64,1152]{1,0:T(8,128)(2,1)S(1)} all-gather(bf16[32,1152]{1,0:T(8,128)(2,1)S(1)} %reduce_sum.90), channel_id=3, replica_groups={{128,256},{0,384},{136,264},{8,392},{144,272},{16,400},{152,280},{24,40..., dimensions={0}, use_global_device_ids=true | all-gather | bytes 221184 | tf_op jit(solution)/shard_map/all_gather | solution.py:134
  82.9 1.1 broadcast_in_dim.25
  84.0 0.0 copy-start.3
  84.0 5.7 %all-to-all-start.3 = ((bf16[16,32,1152]{2,1,0:T(8,128)(2,1)}), bf16[16,32,1152]{2,1,0:T(8,128)(2,1)}, u32[]{:S(2)}, u32[]{:S(2)}) async-start(bf16[16,32,1152]{2,1,0:T(8,128)(2,1)} %broadcast_in_dim.25), calls=%async_computation.3 | async-start | bytes 2359296 | tf_op jit(solution)/shard_map/all_to_all | solution.py:41
  89.7 0.0 copy-done.3
  89.7 0.1 copy.14
  89.8 0.6 copy.15.x_ref
  90.5 0.9 slice_convert_fusion
  91.4 1.2 convert_reduce_fusion
  92.5 20.7 %all-to-all-done.3 = bf16[16,32,1152]{2,1,0:T(8,128)(2,1)} async-done(((bf16[16,32,1152]{2,1,0:T(8,128)(2,1)}), bf16[16,32,1152]{2,1,0:T(8,128)(2,1)}, u32[]{:S(2)}, u32[]{:S(2)}) %all-to-all-start.3) | async-done | bytes 1179680 | tf_op jit(solution)/shard_map/all_to_all | solution.py:41
  113.2 0.0 copy-start.8
  113.2 3.3 %convolution_convert_fusion.1 = bf16[512,512]{1,0:T(8,128)(2,1)} fusion(bf16[512,1152]{1,0:T(8,128)(2,1)} %bitcast.9, bf16[512,1152]{1,0:T(8,128)(2,1)} %param.9), kind=kOutput, calls=%fused_computation.6 | convolution fusion | flops 604241920 | bytes 2883584 | tf_op jit(solution)/shard_map/dot_general | solution.py:144
  116.6 6.1 %all-to-all-start.4 = ((bf16[8,64,512]{2,1,0:T(8,128)(2,1)}), bf16[8,64,512]{2,1,0:T(8,128)(2,1)S(1)}, u32[]{:S(2)}, u32[]{:S(2)}) async-start(bf16[8,64,512]{2,1,0:T(8,128)(2,1)} %bitcast.41), calls=%async_computation.4 | async-start | bytes 1048576 | tf_op jit(solution)/shard_map/all_to_all | solution.py:41
  122.7 0.0 copy-done.8
  122.7 0.0 copy-start.5
  122.8 3.5 %fusion = bf16[512,1152]{1,0:T(8,128)(2,1)} fusion(bf16[512,512]{1,0:T(8,128)(2,1)S(1)} %bitcast.40, bf16[512,1152]{1,0:T(8,128)(2,1)} %bitcast.9, bf16[512,1152]{1,0:T(8,128)(2,1)} %param.9, f32[512]{0:T(512)S(1)} %get-tuple-element.14), kind=kOutput, calls=%fused_computation.1 | convolution fusion | flops 606339072 | bytes 4065280 | tf_op jit(solution)/shard_map/dot_general | solution.py:157
  126.3 5.8 %all-to-all-done.4 = bf16[8,64,512]{2,1,0:T(8,128)(2,1)S(1)} async-done(((bf16[8,64,512]{2,1,0:T(8,128)(2,1)}), bf16[8,64,512]{2,1,0:T(8,128)(2,1)S(1)}, u32[]{:S(2)}, u32[]{:S(2)}) %all-to-all-start.4) | async-done | bytes 524320 | tf_op jit(solution)/shard_map/all_to_all | solution.py:41
  132.1 0.1 convert_reduce_fusion.1
  132.2 0.0 copy-done.5
  132.2 0.1 select_convert_fusion
  132.2 0.7 broadcast_in_dim.26
  133.0 3.4 %all-to-all-start.5 = ((bf16[4,64,512]{2,1,0:T(8,128)(2,1)}), bf16[4,64,512]{2,1,0:T(8,128)(2,1)S(1)}, u32[]{:S(2)}, u32[]{:S(2)}) async-start(bf16[4,64,512]{2,1,0:T(8,128)(2,1)} %broadcast_in_dim.26), calls=%async_computation.5 | async-start | bytes 524288 | tf_op jit(solution)/shard_map/all_to_all | solution.py:41
  136.4 1.3 constant_dynamic-slice_fusion
  137.7 4.8 %all-to-all-done.5 = bf16[4,64,512]{2,1,0:T(8,128)(2,1)S(1)} async-done(((bf16[4,64,512]{2,1,0:T(8,128)(2,1)}), bf16[4,64,512]{2,1,0:T(8,128)(2,1)S(1)}, u32[]{:S(2)}, u32[]{:S(2)}) %all-to-all-start.5) | async-done | bytes 262176 | tf_op jit(solution)/shard_map/all_to_all | solution.py:41
  142.5 3.3 %all_gather.23.g_ref = bf16[512,512]{1,0:T(8,128)(2,1)S(1)} all-gather(bf16[256,512]{1,0:T(8,128)(2,1)S(1)} %bitcast.36), channel_id=1, replica_groups={{0,1},{2,3},{4,5},{6,7},{8,9},{10,11},{12,13},{14,15},{16,17},{18,19},{..., dimensions={0}, use_global_device_ids=true | all-gather | bytes 786432 | tf_op jit(solution)/shard_map/all_gather | solution.py:102
  145.8 2.4 %shard_map.93 = (bf16[1152,512]{1,0:T(8,128)(2,1)}, f32[512]{0:T(512)}) custom-call(bf16[1152,512]{1,0:T(8,128)(2,1)S(1)} %copy.15.x_ref, bf16[512,512]{1,0:T(8,128)(2,1)S(1)} %all_gather.23.g_ref), custom_call_target="tpu_custom_call" | custom-call | tf_op jit(solution)/shard_map/pallas_call | solution.py:57
  (12 shorter events, 0.2 us)
Async XLA Ops:
  0.6 1.8 %copy-start = (bf16[1152,512]{1,0:T(8,128)(2,1)S(1)}, bf16[1152,512]{1,0:T(8,128)(2,1)}, u32[]{:S(2)}) copy-start(bf16[1152,512]{1,0:T(8,128)(2,1)} %param.7) | copy-start | bytes 3538948
  0.6 2.0 %copy-start.2 = (bf16[512,1152]{1,0:T(8,128)(2,1)S(1)}, bf16[512,1152]{1,0:T(8,128)(2,1)}, u32[]{:S(2)}) copy-start(bf16[512,1152]{1,0:T(8,128)(2,1)} %param.6) | copy-start | bytes 3538948
  2.6 12.7 %copy-start.10 = (s32[1,32]{1,0:T(1,128)S(1)}, s32[1,32]{1,0:T(1,128)}, u32[]{:S(2)}) copy-start(s32[1,32]{1,0:T(1,128)} %param.10) | copy-start | bytes 388
  4.3 20.0 %copy-start.9 = (f32[512]{0:T(512)S(1)}, f32[512]{0:T(512)}, u32[]{:S(2)}) copy-start(f32[512]{0:T(512)} %param.8) | copy-start | bytes 6148
  4.3 19.9 %all-to-all-start = ((bf16[8,64,512]{2,1,0:T(8,128)(2,1)}), bf16[8,64,512]{2,1,0:T(8,128)(2,1)S(1)}, u32[]{:S(2)}, u32[]{:S(2)}) async-start(bf16[8,64,512]{2,1,0:T(8,128)(2,1)} %bitcast.2), calls=%async_computation | async-start | bytes 1048576 | tf_op jit(solution)/shard_map/all_to_all | solution.py:41
  24.2 13.3 %copy-start.4 = (f32[64,512]{1,0:T(8,128)}, f32[64,512]{1,0:T(8,128)S(1)}, u32[]{:S(2)}) copy-start(f32[64,512]{1,0:T(8,128)S(1)} %convert_reduce_fusion.2) | copy-start | bytes 393220
  24.4 13.2 %copy-start.6 = (bf16[512,1152]{1,0:T(8,128)(2,1)S(1)}, bf16[512,1152]{1,0:T(8,128)(2,1)}, u32[]{:S(2)}) copy-start(bf16[512,1152]{1,0:T(8,128)(2,1)} %param.9) | copy-start | bytes 3538948
  36.7 0.8 copy-start.1
  37.6 1.9 %copy-start.7 = (bf16[2,4,64,512]{3,2,1,0:T(8,128)(2,1)}, bf16[2,4,64,512]{3,2,1,0:T(8,128)(2,1)S(1)}, u32[]{:S(2)}) copy-start(bf16[2,4,64,512]{3,2,1,0:T(8,128)(2,1)S(1)} %slice.16) | copy-start | bytes 1572868
  39.5 27.0 %all-to-all-start.2 = ((bf16[16,32,1152]{2,1,0:T(8,128)(2,1)}), bf16[16,32,1152]{2,1,0:T(8,128)(2,1)S(1)}, u32[]{:S(2)}, u32[]{:S(2)}) async-start(bf16[16,32,1152]{2,1,0:T(8,128)(2,1)} %bitcast.35), calls=%async_computation.2 | async-start | bytes 2359296 | tf_op jit(solution)/shard_map/all_to_all | solution.py:41
  84.0 5.7 %copy-start.3 = (bf16[512,1152]{1,0:T(8,128)(2,1)S(1)}, bf16[512,1152]{1,0:T(8,128)(2,1)}, u32[]{:S(2)}) copy-start(bf16[512,1152]{1,0:T(8,128)(2,1)} %param.6) | copy-start | bytes 3538948
  84.0 29.3 %all-to-all-start.3 = ((bf16[16,32,1152]{2,1,0:T(8,128)(2,1)}), bf16[16,32,1152]{2,1,0:T(8,128)(2,1)}, u32[]{:S(2)}, u32[]{:S(2)}) async-start(bf16[16,32,1152]{2,1,0:T(8,128)(2,1)} %broadcast_in_dim.25), calls=%async_computation.3 | async-start | bytes 2359296 | tf_op jit(solution)/shard_map/all_to_all | solution.py:41
  113.2 9.5 %copy-start.8 = (bf16[2,4,64,512]{3,2,1,0:T(8,128)(2,1)S(1)}, bf16[2,4,64,512]{3,2,1,0:T(8,128)(2,1)}, u32[]{:S(2)}) copy-start(bf16[2,4,64,512]{3,2,1,0:T(8,128)(2,1)} %copy-done.7) | copy-start | bytes 1572868
  116.6 15.5 %all-to-all-start.4 = ((bf16[8,64,512]{2,1,0:T(8,128)(2,1)}), bf16[8,64,512]{2,1,0:T(8,128)(2,1)S(1)}, u32[]{:S(2)}, u32[]{:S(2)}) async-start(bf16[8,64,512]{2,1,0:T(8,128)(2,1)} %bitcast.41), calls=%async_computation.4 | async-start | bytes 1048576 | tf_op jit(solution)/shard_map/all_to_all | solution.py:41
  122.7 9.4 %copy-start.5 = (f32[64,512]{1,0:T(8,128)S(1)}, f32[64,512]{1,0:T(8,128)}, u32[]{:S(2)}) copy-start(f32[64,512]{1,0:T(8,128)} %copy-done.4) | copy-start | bytes 393220
  133.0 9.5 %all-to-all-start.5 = ((bf16[4,64,512]{2,1,0:T(8,128)(2,1)}), bf16[4,64,512]{2,1,0:T(8,128)(2,1)S(1)}, u32[]{:S(2)}, u32[]{:S(2)}) async-start(bf16[4,64,512]{2,1,0:T(8,128)(2,1)} %broadcast_in_dim.26), calls=%async_computation.5 | async-start | bytes 524288 | tf_op jit(solution)/shard_map/all_to_all | solution.py:41

commit v8 on v7

--- a/solution.py
+++ b/solution.py
@@ -10,6 +10,7 @@
 PENALTY = 0.3
 EPSILON = 1e-06
 EXTRA = 8
+PIECES = 4
 
 f32 = jnp.float32
 bf16 = jnp.bfloat16
@@ -41,35 +42,43 @@
     return lax.all_to_all(x, axis, 0, 0, axis_index_groups=groups, tiled=True)
 
 
-def tail_kernel(x_ref, g_ref, out_ref, bias_ref):
-    out_ref[...] = jnp.dot(x_ref[...], g_ref[...], preferred_element_type=f32).astype(bf16)
+def params():
+    return pltpu.CompilerParams(vmem_limit_bytes=32 * 2**20)
 
-    @pl.when(pl.program_id(0) == 0)
-    def _():
-        ones = jnp.ones((8, g_ref.shape[0]), bf16)
-        bias_ref[...] = jnp.dot(ones, g_ref[...], preferred_element_type=f32)[0]
+
+HBM = pl.BlockSpec(memory_space=pltpu.HBM)
+VMEM = pl.BlockSpec(memory_space=pltpu.VMEM)
+
+
+def blocks(extent, count):
+    size = extent // count
+    return [pl.ds(i * size, size) for i in range(count)]
+
+
+def tail_kernel(x_ref, g_ref, out_ref, bias_ref, out, sems):
+    sent = []
+    for i, m in enumerate(blocks(x_ref.shape[0], PIECES)):
+        out[m] = jnp.dot(x_ref[m], g_ref[...], preferred_element_type=f32).astype(bf16)
+        sent.append(pltpu.make_async_copy(out.at[m], out_ref.at[m], sems.at[i]))
+        sent[i].start()
+    ones = jnp.ones((8, g_ref.shape[0]), bf16)
+    bias_ref[...] = jnp.dot(ones, g_ref[...], preferred_element_type=f32)[0]
+    for copy in sent:
+        copy.wait()
 
 
 def tail(x_t, g):
-    depth, rows = x_t.shape
-    cols = g.shape[1]
-    step = depth // 3
+    shape = (x_t.shape[0], g.shape[1])
     return pl.pallas_call(
         tail_kernel,
-        grid=(3,),
-        in_specs=[
-            pl.BlockSpec((step, rows), lambda i: (i, 0)),
-            pl.BlockSpec((rows, cols), lambda i: (0, 0)),
+        in_specs=[VMEM, VMEM],
+        out_specs=[HBM, pl.BlockSpec((g.shape[1],), lambda: (0,))],
+        out_shape=[
+            jax.ShapeDtypeStruct(shape, bf16),
+            jax.ShapeDtypeStruct((g.shape[1],), f32),
         ],
-        out_specs=[
-            pl.BlockSpec((step, cols), lambda i: (i, 0)),
-            pl.BlockSpec((cols,), lambda i: (0,)),
-        ],
-        out_shape=[
-            jax.ShapeDtypeStruct((depth, cols), bf16),
-            jax.ShapeDtypeStruct((cols,), f32),
-        ],
-        compiler_params=pltpu.CompilerParams(vmem_limit_bytes=24 * 2**20),
+        scratch_shapes=[pltpu.VMEM(shape, bf16), pltpu.SemaphoreType.DMA((PIECES,))],
+        compiler_params=params(),
     )(x_t, g)
 
 
@@ -111,10 +120,10 @@
     )
     mask = jnp.any(hit, axis=0)[None, :]
 
-    dec32 = dec_weight.astype(f32)
+    part = jnp.dot(tokens, enc_weight, preferred_element_type=f32).astype(bf16)
+    part, dec_late = lax.optimization_barrier((part, dec_weight))
+    dec32 = dec_late.astype(f32)
     squares = jnp.sum(dec32 * dec32, axis=1).astype(bf16)
-    part = jnp.dot(tokens, enc_weight, preferred_element_type=f32).astype(bf16)
-    part, squares = lax.optimization_barrier((part, squares))
     got = exchange(part.reshape(n_tok, own, local_lat), "tok", None)
     pre = jnp.sum(got.astype(f32), axis=0) + enc_bias[None, :]
     acts_own = jnp.where(mask, jax.nn.softplus(pre), 0.0).astype(bf16)
@@ -127,7 +136,7 @@
     norm_b = jnp.sqrt(jnp.sum(sq[:, n_x // 2 :], axis=(0, 1)) + EPSILON)
     own_norm = jnp.where(half == 0, norm_a, norm_b)
 
-    recon = jnp.dot(acts, dec_weight, preferred_element_type=f32).astype(bf16)
+    recon = jnp.dot(acts, dec_late, preferred_element_type=f32).astype(bf16)
     got = exchange(recon.reshape(chunks, chunk, width), both, big)
     line = jnp.sum(got.astype(f32), axis=0).astype(bf16)
     for groups in (near, far):

time: 149 us -> 149 us (level)
  no operation moved by 1% of the time
where the time goes in v8:
time: 149 us; the launch traced here: 148 us
  waiting for transfers between devices  62.3 us (42%)
  blocking collectives  30.6 us (21%)
  starting transfers between devices  29.8 us (20%)
  matrix products  11.8 us (8%)
  local copies, waits for them, and re-layouts  6.05 us (4%)
  other arithmetic  3.91 us (3%)
  Pallas kernels  2.1 us (1%)
  between operations  1.73 us (1%)
    all_to_all x5, waiting for transfers between devices, exchange(): return lax.all_to_all(x, axis, 0, 0, axis_index_groups=groups, tiled=True)  62.3 us
    all_to_all x5, starting transfers between devices, exchange(): return lax.all_to_all(x, axis, 0, 0, axis_index_groups=groups, tiled=True)  29.8 us
    all_gather x2, blocking collectives, body(): two = lax.all_gather(line, both, axis_index_groups=groups, axis=0)  15.2 us
    all_to_all x1, blocking collectives, exchange(): return lax.all_to_all(x, axis, 0, 0, axis_index_groups=groups, tiled=True)  8.27 us
    all_gather x2, blocking collectives, gather_tok(): lax.all_gather(got.reshape(-1, local_lat), 'tok', axis_index_groups=c_gro...  7.19 us
    dot_general x1, matrix products, body(): lax.dot_general(acts, err, (((0,), (0,)), ((), ())), preferred_element_ty...  3.55 us
    dot_general x1, matrix products, body(): lax.dot_general(err, dec_weight, (((1,), (1,)), ((), ())), preferred_elem...  3.35 us
    dot_general x1, matrix products, body(): part = jnp.dot(tokens, enc_weight, preferred_element_type=f32).astype(bf16)  3 us
  transfers between devices with their start and end apart: 5, of which 5 were waited for; matrix products, arithmetic and copies ran while one was open for 5% of the time, Pallas kernels for 0%

profile of v8, /device:TPU:1, one launch (start us, length us, event | category | flops | bytes accessed | tf_op | source)
XLA Modules:
  0.0 148.3 jit_solution(13391904299164607480)
XLA Ops:
  0.6 0.0 copy-start
  0.6 0.0 copy-start.9
  0.7 1.3 copy-done
  1.9 0.0 copy-start.5
  1.9 3.0 %convolution_convert_fusion.2 = bf16[512,512]{1,0:T(8,128)(2,1)} fusion(bf16[512,1152]{1,0:T(8,128)(2,1)} %param.6, bf16[1152,512]{1,0:T(8,128)(2,1)S(1)} %copy-done), kind=kOutput, calls=%fused_computation.7 | convolution fusion | flops 604241920 | bytes 2883584 | tf_op jit(solution)/shard_map/dot_general | solution.py:123
  4.9 10.3 %all-to-all-start = ((bf16[8,64,512]{2,1,0:T(8,128)(2,1)}), bf16[8,64,512]{2,1,0:T(8,128)(2,1)S(1)}, u32[]{:S(2)}, u32[]{:S(2)}) async-start(bf16[8,64,512]{2,1,0:T(8,128)(2,1)} %bitcast.2), calls=%async_computation | async-start | bytes 1048576 | tf_op jit(solution)/shard_map/all_to_all | solution.py:42
  15.2 0.0 copy-start.8
  15.9 0.0 copy-done.9
  15.9 0.1 and_reduce_fusion
  16.0 0.0 copy-done.5
  16.0 0.3 fusion.1
  16.3 8.4 %all-to-all-done = bf16[8,64,512]{2,1,0:T(8,128)(2,1)S(1)} async-done(((bf16[8,64,512]{2,1,0:T(8,128)(2,1)}), bf16[8,64,512]{2,1,0:T(8,128)(2,1)S(1)}, u32[]{:S(2)}, u32[]{:S(2)}) %all-to-all-start) | async-done | bytes 524320 | tf_op jit(solution)/shard_map/all_to_all | solution.py:42
  24.7 0.1 convert_reduce_fusion.2
  24.8 0.0 copy-done.8
  24.8 0.0 copy-start.3
  24.8 0.1 fusion.3
  24.9 8.3 %all_to_all.30 = bf16[4,72,512]{2,1,0:T(8,128)(2,1)S(1)} all-to-all(bf16[4,72,512]{2,1,0:T(8,128)(2,1)S(1)} %broadcast_in_dim.24), channel_id=1, replica_groups={{0,2,4,6},{1,3,5,7},{8,10,12,14},{9,11,13,15},{16,18,20,22},{17,19,21,2..., dimensions={0} | all-to-all | bytes 589824 | tf_op jit(solution)/shard_map/all_to_all | solution.py:42
  33.2 0.0 copy-done.3
  33.2 3.9 %all_gather.18 = bf16[576,512]{1,0:T(8,128)(2,1)S(1)} all-gather(bf16[288,512]{1,0:T(8,128)(2,1)S(1)} %bitcast.34), channel_id=1, replica_groups={{0,1},{2,3},{4,5},{6,7},{8,9},{10,11},{12,13},{14,15},{16,17},{18,19},{..., dimensions={0}, use_global_device_ids=true | all-gather | bytes 884736 | tf_op jit(solution)/shard_map/all_gather | solution.py:111
  37.1 0.0 copy-start.1
  37.1 0.8 copy-done.1
  38.0 0.0 copy-start.6
  38.0 1.9 %convolution_convert_fusion = bf16[512,1152]{1,0:T(8,128)(2,1)} fusion(bf16[512,512]{1,0:T(8,128)(2,1)S(1)} %bitcast.38, bf16[512,1152]{1,0:T(8,128)(2,1)S(1)} %copy-done.5), kind=kOutput, calls=%fused_computation.2 | convolution fusion | flops 604569600 | bytes 2883584 | tf_op jit(solution)/shard_map/dot_general | solution.py:139
  39.8 0.0 copy-done.6
  39.8 4.2 %all-to-all-start.2 = ((bf16[16,32,1152]{2,1,0:T(8,128)(2,1)}), bf16[16,32,1152]{2,1,0:T(8,128)(2,1)S(1)}, u32[]{:S(2)}, u32[]{:S(2)}) async-start(bf16[16,32,1152]{2,1,0:T(8,128)(2,1)} %bitcast.6), calls=%async_computation.2 | async-start | bytes 2359296 | tf_op jit(solution)/shard_map/all_to_all | solution.py:42
  44.2 22.7 %all-to-all-done.2 = bf16[16,32,1152]{2,1,0:T(8,128)(2,1)S(1)} async-done(((bf16[16,32,1152]{2,1,0:T(8,128)(2,1)}), bf16[16,32,1152]{2,1,0:T(8,128)(2,1)S(1)}, u32[]{:S(2)}, u32[]{:S(2)}) %all-to-all-start.2) | async-done | bytes 1179680 | tf_op jit(solution)/shard_map/all_to_all | solution.py:42
  66.9 0.2 reduce_sum.89
  67.1 7.3 %all-gather = bf16[64,1152]{1,0:T(8,128)(2,1)S(1)} all-gather(bf16[32,1152]{1,0:T(8,128)(2,1)S(1)} %reduce_sum.89), channel_id=2, replica_groups={{0,128},{256,384},{8,136},{264,392},{16,144},{272,400},{24,152},{280,40..., dimensions={0}, use_global_device_ids=true | all-gather | bytes 221184 | tf_op jit(solution)/shard_map/all_gather | solution.py:143
  74.4 7.9 %all-gather.1 = bf16[64,1152]{1,0:T(8,128)(2,1)S(1)} all-gather(bf16[32,1152]{1,0:T(8,128)(2,1)S(1)} %reduce_sum.90), channel_id=3, replica_groups={{128,256},{0,384},{136,264},{8,392},{144,272},{16,400},{152,280},{24,40..., dimensions={0}, use_global_device_ids=true | all-gather | bytes 221184 | tf_op jit(solution)/shard_map/all_gather | solution.py:143
  82.3 0.9 subtract_convert_fusion
  83.2 1.1 broadcast_in_dim.25
  84.3 0.0 copy-start.2
  84.3 5.8 %all-to-all-start.3 = ((bf16[16,32,1152]{2,1,0:T(8,128)(2,1)}), bf16[16,32,1152]{2,1,0:T(8,128)(2,1)}, u32[]{:S(2)}, u32[]{:S(2)}) async-start(bf16[16,32,1152]{2,1,0:T(8,128)(2,1)} %broadcast_in_dim.25), calls=%async_computation.3 | async-start | bytes 2359296 | tf_op jit(solution)/shard_map/all_to_all | solution.py:42
  90.1 0.0 copy-done.2
  90.2 0.1 copy.14
  90.3 0.6 copy.15.x_ref
  90.9 0.9 slice_convert_fusion
  91.8 1.2 convert_reduce_fusion
  93.0 20.7 %all-to-all-done.3 = bf16[16,32,1152]{2,1,0:T(8,128)(2,1)} async-done(((bf16[16,32,1152]{2,1,0:T(8,128)(2,1)}), bf16[16,32,1152]{2,1,0:T(8,128)(2,1)}, u32[]{:S(2)}, u32[]{:S(2)}) %all-to-all-start.3) | async-done | bytes 1179680 | tf_op jit(solution)/shard_map/all_to_all | solution.py:42
  113.6 0.0 copy-start.7
  113.6 3.4 %convolution_convert_fusion.1 = bf16[512,512]{1,0:T(8,128)(2,1)} fusion(bf16[512,1152]{1,0:T(8,128)(2,1)} %bitcast.9, bf16[512,1152]{1,0:T(8,128)(2,1)} %param.9), kind=kOutput, calls=%fused_computation.6 | convolution fusion | flops 604241920 | bytes 2883584 | tf_op jit(solution)/shard_map/dot_general | solution.py:153
  117.0 6.2 %all-to-all-start.4 = ((bf16[8,64,512]{2,1,0:T(8,128)(2,1)}), bf16[8,64,512]{2,1,0:T(8,128)(2,1)S(1)}, u32[]{:S(2)}, u32[]{:S(2)}) async-start(bf16[8,64,512]{2,1,0:T(8,128)(2,1)} %bitcast.40), calls=%async_computation.4 | async-start | bytes 1048576 | tf_op jit(solution)/shard_map/all_to_all | solution.py:42
  123.2 0.0 copy-done.7
  123.2 0.0 copy-start.4
  123.2 3.5 %fusion = bf16[512,1152]{1,0:T(8,128)(2,1)} fusion(bf16[512,512]{1,0:T(8,128)(2,1)S(1)} %bitcast.39, bf16[512,1152]{1,0:T(8,128)(2,1)} %bitcast.9, bf16[512,1152]{1,0:T(8,128)(2,1)} %param.9, f32[512]{0:T(512)S(1)} %get-tuple-element.14), kind=kOutput, calls=%fused_computation.1 | convolution fusion | flops 606339072 | bytes 4065280 | tf_op jit(solution)/shard_map/dot_general | solution.py:166
  126.7 5.8 %all-to-all-done.4 = bf16[8,64,512]{2,1,0:T(8,128)(2,1)S(1)} async-done(((bf16[8,64,512]{2,1,0:T(8,128)(2,1)}), bf16[8,64,512]{2,1,0:T(8,128)(2,1)S(1)}, u32[]{:S(2)}, u32[]{:S(2)}) %all-to-all-start.4) | async-done | bytes 524320 | tf_op jit(solution)/shard_map/all_to_all | solution.py:42
  132.5 0.1 convert_reduce_fusion.1
  132.6 0.0 copy-done.4
  132.6 0.1 select_convert_fusion
  132.7 0.7 broadcast_in_dim.26
  133.4 3.4 %all-to-all-start.5 = ((bf16[4,64,512]{2,1,0:T(8,128)(2,1)}), bf16[4,64,512]{2,1,0:T(8,128)(2,1)S(1)}, u32[]{:S(2)}, u32[]{:S(2)}) async-start(bf16[4,64,512]{2,1,0:T(8,128)(2,1)} %broadcast_in_dim.26), calls=%async_computation.5 | async-start | bytes 524288 | tf_op jit(solution)/shard_map/all_to_all | solution.py:42
  136.8 1.3 constant_dynamic-slice_fusion
  138.1 4.8 %all-to-all-done.5 = bf16[4,64,512]{2,1,0:T(8,128)(2,1)S(1)} async-done(((bf16[4,64,512]{2,1,0:T(8,128)(2,1)}), bf16[4,64,512]{2,1,0:T(8,128)(2,1)S(1)}, u32[]{:S(2)}, u32[]{:S(2)}) %all-to-all-start.5) | async-done | bytes 262176 | tf_op jit(solution)/shard_map/all_to_all | solution.py:42
  142.9 3.3 %all_gather.23.g_ref = bf16[512,512]{1,0:T(8,128)(2,1)S(1)} all-gather(bf16[256,512]{1,0:T(8,128)(2,1)S(1)} %bitcast.35), channel_id=1, replica_groups={{0,1},{2,3},{4,5},{6,7},{8,9},{10,11},{12,13},{14,15},{16,17},{18,19},{..., dimensions={0}, use_global_device_ids=true | all-gather | bytes 786432 | tf_op jit(solution)/shard_map/all_gather | solution.py:111
  146.2 2.1 %shard_map.93 = (bf16[1152,512]{1,0:T(8,128)(2,1)}, f32[512]{0:T(512)}) custom-call(bf16[1152,512]{1,0:T(8,128)(2,1)S(1)} %copy.15.x_ref, bf16[512,512]{1,0:T(8,128)(2,1)S(1)} %all_gather.23.g_ref), custom_call_target="tpu_custom_call" | custom-call | tf_op jit(solution)/shard_map/pallas_call | solution.py:72
  (11 shorter events, 0.2 us)
Async XLA Ops:
  0.6 1.3 copy-start
  0.6 15.3 %copy-start.9 = (s32[1,32]{1,0:T(1,128)S(1)}, s32[1,32]{1,0:T(1,128)}, u32[]{:S(2)}) copy-start(s32[1,32]{1,0:T(1,128)} %param.10) | copy-start | bytes 388
  1.9 14.1 %copy-start.5 = (bf16[512,1152]{1,0:T(8,128)(2,1)S(1)}, bf16[512,1152]{1,0:T(8,128)(2,1)}, u32[]{:S(2)}) copy-start(bf16[512,1152]{1,0:T(8,128)(2,1)} %param.9) | copy-start | bytes 3538948
  4.9 19.8 %all-to-all-start = ((bf16[8,64,512]{2,1,0:T(8,128)(2,1)}), bf16[8,64,512]{2,1,0:T(8,128)(2,1)S(1)}, u32[]{:S(2)}, u32[]{:S(2)}) async-start(bf16[8,64,512]{2,1,0:T(8,128)(2,1)} %bitcast.2), calls=%async_computation | async-start | bytes 1048576 | tf_op jit(solution)/shard_map/all_to_all | solution.py:42
  15.2 9.6 %copy-start.8 = (f32[512]{0:T(512)S(1)}, f32[512]{0:T(512)}, u32[]{:S(2)}) copy-start(f32[512]{0:T(512)} %param.8) | copy-start | bytes 6148
  24.8 8.4 %copy-start.3 = (f32[64,512]{1,0:T(8,128)}, f32[64,512]{1,0:T(8,128)S(1)}, u32[]{:S(2)}) copy-start(f32[64,512]{1,0:T(8,128)S(1)} %convert_reduce_fusion.2) | copy-start | bytes 393220
  37.1 0.8 copy-start.1
  38.0 1.9 %copy-start.6 = (bf16[2,4,64,512]{3,2,1,0:T(8,128)(2,1)}, bf16[2,4,64,512]{3,2,1,0:T(8,128)(2,1)S(1)}, u32[]{:S(2)}) copy-start(bf16[2,4,64,512]{3,2,1,0:T(8,128)(2,1)S(1)} %slice.16) | copy-start | bytes 1572868
  39.8 27.0 %all-to-all-start.2 = ((bf16[16,32,1152]{2,1,0:T(8,128)(2,1)}), bf16[16,32,1152]{2,1,0:T(8,128)(2,1)S(1)}, u32[]{:S(2)}, u32[]{:S(2)}) async-start(bf16[16,32,1152]{2,1,0:T(8,128)(2,1)} %bitcast.6), calls=%async_computation.2 | async-start | bytes 2359296 | tf_op jit(solution)/shard_map/all_to_all | solution.py:42
  84.3 5.8 %copy-start.2 = (bf16[512,1152]{1,0:T(8,128)(2,1)S(1)}, bf16[512,1152]{1,0:T(8,128)(2,1)}, u32[]{:S(2)}) copy-start(bf16[512,1152]{1,0:T(8,128)(2,1)} %param.6) | copy-start | bytes 3538948
  84.3 29.3 %all-to-all-start.3 = ((bf16[16,32,1152]{2,1,0:T(8,128)(2,1)}), bf16[16,32,1152]{2,1,0:T(8,128)(2,1)}, u32[]{:S(2)}, u32[]{:S(2)}) async-start(bf16[16,32,1152]{2,1,0:T(8,128)(2,1)} %broadcast_in_dim.25), calls=%async_computation.3 | async-start | bytes 2359296 | tf_op jit(solution)/shard_map/all_to_all | solution.py:42
  113.6 9.5 %copy-start.7 = (bf16[2,4,64,512]{3,2,1,0:T(8,128)(2,1)S(1)}, bf16[2,4,64,512]{3,2,1,0:T(8,128)(2,1)}, u32[]{:S(2)}) copy-start(bf16[2,4,64,512]{3,2,1,0:T(8,128)(2,1)} %copy-done.6) | copy-start | bytes 1572868
  117.0 15.5 %all-to-all-start.4 = ((bf16[8,64,512]{2,1,0:T(8,128)(2,1)}), bf16[8,64,512]{2,1,0:T(8,128)(2,1)S(1)}, u32[]{:S(2)}, u32[]{:S(2)}) async-start(bf16[8,64,512]{2,1,0:T(8,128)(2,1)} %bitcast.40), calls=%async_computation.4 | async-start | bytes 1048576 | tf_op jit(solution)/shard_map/all_to_all | solution.py:42
  123.2 9.4 %copy-start.4 = (f32[64,512]{1,0:T(8,128)S(1)}, f32[64,512]{1,0:T(8,128)}, u32[]{:S(2)}) copy-start(f32[64,512]{1,0:T(8,128)} %copy-done.3) | copy-start | bytes 393220
  133.4 9.5 %all-to-all-start.5 = ((bf16[4,64,512]{2,1,0:T(8,128)(2,1)}), bf16[4,64,512]{2,1,0:T(8,128)(2,1)S(1)}, u32[]{:S(2)}, u32[]{:S(2)}) async-start(bf16[4,64,512]{2,1,0:T(8,128)(2,1)} %broadcast_in_dim.26), calls=%async_computation.5 | async-start | bytes 524288 | tf_op jit(solution)/shard_map/all_to_all | solution.py:42

commit v9 on v8

--- a/solution.py
+++ b/solution.py
@@ -19,7 +19,7 @@
 def lat_groups(n_lat, n_tok):
     side = round(n_lat**0.5)
     quads = side // 2
-    big, near, far = [], [], []
+    big, small = [], []
     for tok in range(n_tok):
         swap = tok % 2 == 1
 
@@ -33,9 +33,8 @@
         for p in range(2):
             for b in range(side):
                 four = [device(a, p, b) for a in range(quads)]
-                near += [four[:2], four[2:]]
-                far += [four[1:3], [four[0], four[3]]]
-    return big, near, far
+                small.append(four)
+    return big, small
 
 
 def exchange(x, axis, groups):
@@ -101,7 +100,7 @@
     chunks = 2 * side
     chunk = rows // chunks
     both = ("lat", "tok")
-    big, near, far = lat_groups(n_lat, n_tok)
+    big, small = lat_groups(n_lat, n_tok)
     x_groups = [[2 * x + c for x in range(n_x)] for c in range(2)]
     c_groups = [[2 * x, 2 * x + 1] for x in range(n_x)]
 
@@ -139,10 +138,8 @@
     recon = jnp.dot(acts, dec_late, preferred_element_type=f32).astype(bf16)
     got = exchange(recon.reshape(chunks, chunk, width), both, big)
     line = jnp.sum(got.astype(f32), axis=0).astype(bf16)
-    for groups in (near, far):
-        two = lax.all_gather(line, both, axis_index_groups=groups, axis=0)
-        total = jnp.sum(two.astype(f32), axis=0)
-        line = total.astype(bf16)
+    got = exchange(jnp.broadcast_to(line[None], (side // 2,) + line.shape), both, small)
+    total = jnp.sum(got.astype(f32), axis=0)
     at = jnp.where(even, y % 2 * side + z, z % 2 * side + y) * chunk
     at = 2 * (at // own % n_x) * own + at // (n_x * own) * own + at % own
     x_line = lax.dynamic_slice_in_dim(tokens, at, chunk, 0)

time: 149 us -> 150 us (level)
  waiting for transfers between devices: 62.3 us -> 48.2 us
  blocking collectives: 30.6 us -> 42.6 us
  starting transfers between devices: 29.8 us -> 32.4 us
    all_to_all x1 -> x2, blocking collectives: 8.27 us -> 35.4 us  [exchange(): return lax.all_to_all(x, axis, 0, 0, axis_index_groups=groups, tiled=True)]
    all_gather x2 -> x0, blocking collectives: 15.2 us -> none  [body(): two = lax.all_gather(line, both, axis_index_groups=groups, axis=0)]
    all_to_all x5, waiting for transfers between devices: 62.3 us -> 48.2 us  [exchange(): return lax.all_to_all(x, axis, 0, 0, axis_index_groups=groups, tiled=True)]
    all_to_all x5, starting transfers between devices: 29.8 us -> 32.4 us  [exchange(): return lax.all_to_all(x, axis, 0, 0, axis_index_groups=groups, tiled=True)]
where the time goes in v9:
time: 150 us; the launch traced here: 148 us
  waiting for transfers between devices  48.2 us (32%)
  blocking collectives  42.6 us (28%)
  starting transfers between devices  32.4 us (22%)
  matrix products  10.7 us (7%)
  local copies, waits for them, and re-layouts  6.78 us (5%)
  other arithmetic  3.9 us (3%)
  Pallas kernels  2.1 us (1%)
  between operations  1.6 us (1%)
    all_to_all x5, waiting for transfers between devices, exchange(): return lax.all_to_all(x, axis, 0, 0, axis_index_groups=groups, tiled=True)  48.2 us
    all_to_all x2, blocking collectives, exchange(): return lax.all_to_all(x, axis, 0, 0, axis_index_groups=groups, tiled=True)  35.4 us
    all_to_all x5, starting transfers between devices, exchange(): return lax.all_to_all(x, axis, 0, 0, axis_index_groups=groups, tiled=True)  32.4 us
    all_gather x2, blocking collectives, gather_tok(): lax.all_gather(got.reshape(-1, local_lat), 'tok', axis_index_groups=c_gro...  7.19 us
    dot_general x1, matrix products, body(): lax.dot_general(acts, err, (((0,), (0,)), ((), ())), preferred_element_ty...  3.55 us
    dot_general x1, matrix products, body(): lax.dot_general(err, dec_weight, (((1,), (1,)), ((), ())), preferred_elem...  3.35 us
    dot_general x1, matrix products, body(): part = jnp.dot(tokens, enc_weight, preferred_element_type=f32).astype(bf16)  3 us
  transfers between devices with their start and end apart: 5, of which 5 were waited for; matrix products, arithmetic and copies ran while one was open for 5% of the time, Pallas kernels for 0%

profile of v9, /device:TPU:1, one launch (start us, length us, event | category | flops | bytes accessed | tf_op | source)
XLA Modules:
  0.0 148.4 jit_solution(10464034122742077775)
XLA Ops:
  0.6 0.0 copy-start
  0.6 0.0 copy-start.9
  0.7 1.3 copy-done
  1.9 0.0 copy-start.5
  1.9 3.0 %convolution_convert_fusion.2 = bf16[512,512]{1,0:T(8,128)(2,1)} fusion(bf16[512,1152]{1,0:T(8,128)(2,1)} %param.6, bf16[1152,512]{1,0:T(8,128)(2,1)S(1)} %copy-done), kind=kOutput, calls=%fused_computation.7 | convolution fusion | flops 604241920 | bytes 2883584 | tf_op jit(solution)/shard_map/dot_general | solution.py:122
  4.9 10.3 %all-to-all-start = ((bf16[8,64,512]{2,1,0:T(8,128)(2,1)}), bf16[8,64,512]{2,1,0:T(8,128)(2,1)S(1)}, u32[]{:S(2)}, u32[]{:S(2)}) async-start(bf16[8,64,512]{2,1,0:T(8,128)(2,1)} %bitcast.2), calls=%async_computation | async-start | bytes 1048576 | tf_op jit(solution)/shard_map/all_to_all | solution.py:41
  15.2 0.0 copy-start.8
  15.9 0.0 copy-done.9
  15.9 0.1 and_reduce_fusion
  16.0 0.0 copy-done.5
  16.0 0.3 fusion.1
  16.3 8.4 %all-to-all-done = bf16[8,64,512]{2,1,0:T(8,128)(2,1)S(1)} async-done(((bf16[8,64,512]{2,1,0:T(8,128)(2,1)}), bf16[8,64,512]{2,1,0:T(8,128)(2,1)S(1)}, u32[]{:S(2)}, u32[]{:S(2)}) %all-to-all-start) | async-done | bytes 524320 | tf_op jit(solution)/shard_map/all_to_all | solution.py:41
  24.7 0.1 convert_reduce_fusion.2
  24.8 0.0 copy-done.8
  24.8 0.0 copy-start.3
  24.8 0.1 fusion.3
  24.9 8.3 %all_to_all.35 = bf16[4,72,512]{2,1,0:T(8,128)(2,1)S(1)} all-to-all(bf16[4,72,512]{2,1,0:T(8,128)(2,1)S(1)} %broadcast_in_dim.26), channel_id=1, replica_groups={{0,2,4,6},{1,3,5,7},{8,10,12,14},{9,11,13,15},{16,18,20,22},{17,19,21,2..., dimensions={0} | all-to-all | bytes 589824 | tf_op jit(solution)/shard_map/all_to_all | solution.py:41
  33.2 0.0 copy-done.3
  33.2 3.9 %all_gather.6 = bf16[576,512]{1,0:T(8,128)(2,1)S(1)} all-gather(bf16[288,512]{1,0:T(8,128)(2,1)S(1)} %bitcast.31), channel_id=1, replica_groups={{0,1},{2,3},{4,5},{6,7},{8,9},{10,11},{12,13},{14,15},{16,17},{18,19},{..., dimensions={0}, use_global_device_ids=true | all-gather | bytes 884736 | tf_op jit(solution)/shard_map/all_gather | solution.py:110
  37.1 0.0 copy-start.1
  37.1 0.8 copy-done.1
  38.0 0.0 copy-start.6
  38.0 0.8 convolution_convert_fusion
  38.8 0.0 copy-done.6
  38.8 27.2 %all_to_all.36 = bf16[16,32,1152]{2,1,0:T(8,128)(2,1)S(1)} all-to-all(bf16[16,32,1152]{2,1,0:T(8,128)(2,1)S(1)} %bitcast.32), channel_id=1, replica_groups={{0,8,16,24,32,40,48,56,64,72,80,88,96,104,112,120},{128,136,144,152,160..., dimensions={0} | all-to-all | bytes 2359296 | tf_op jit(solution)/shard_map/all_to_all | solution.py:41
  66.0 0.2 reduce_sum.77
  66.2 0.7 broadcast_in_dim.27
  66.9 10.7 %all-to-all-start.3 = ((bf16[4,32,1152]{2,1,0:T(8,128)(2,1)}), bf16[4,32,1152]{2,1,0:T(8,128)(2,1)S(1)}, u32[]{:S(2)}, u32[]{:S(2)}) async-start(bf16[4,32,1152]{2,1,0:T(8,128)(2,1)} %broadcast_in_dim.27), calls=%async_computation.3 | async-start | bytes 589824 | tf_op jit(solution)/shard_map/all_to_all | solution.py:41
  77.6 8.2 %all-to-all-done.3 = bf16[4,32,1152]{2,1,0:T(8,128)(2,1)S(1)} async-done(((bf16[4,32,1152]{2,1,0:T(8,128)(2,1)}), bf16[4,32,1152]{2,1,0:T(8,128)(2,1)S(1)}, u32[]{:S(2)}, u32[]{:S(2)}) %all-to-all-start.3) | async-done | bytes 294944 | tf_op jit(solution)/shard_map/all_to_all | solution.py:41
  85.8 0.9 subtract_convert_fusion
  86.8 1.1 broadcast_in_dim.28
  87.9 0.0 copy-start.2
  87.9 4.5 %all-to-all-start.4 = ((bf16[16,32,1152]{2,1,0:T(8,128)(2,1)}), bf16[16,32,1152]{2,1,0:T(8,128)(2,1)}, u32[]{:S(2)}, u32[]{:S(2)}) async-start(bf16[16,32,1152]{2,1,0:T(8,128)(2,1)} %broadcast_in_dim.28), calls=%async_computation.4 | async-start | bytes 2359296 | tf_op jit(solution)/shard_map/all_to_all | solution.py:41
  92.4 0.0 copy-done.2
  92.5 0.1 copy.14
  92.6 0.6 copy.15.x_ref
  93.2 0.9 slice_convert_fusion
  94.1 1.2 convert_reduce_fusion
  95.3 21.1 %all-to-all-done.4 = bf16[16,32,1152]{2,1,0:T(8,128)(2,1)} async-done(((bf16[16,32,1152]{2,1,0:T(8,128)(2,1)}), bf16[16,32,1152]{2,1,0:T(8,128)(2,1)}, u32[]{:S(2)}, u32[]{:S(2)}) %all-to-all-start.4) | async-done | bytes 1179680 | tf_op jit(solution)/shard_map/all_to_all | solution.py:41
  116.4 0.0 copy-start.7
  116.4 3.4 %convolution_convert_fusion.1 = bf16[512,512]{1,0:T(8,128)(2,1)} fusion(bf16[512,1152]{1,0:T(8,128)(2,1)} %bitcast.7, bf16[512,1152]{1,0:T(8,128)(2,1)} %param.9), kind=kOutput, calls=%fused_computation.6 | convolution fusion | flops 604241920 | bytes 2883584 | tf_op jit(solution)/shard_map/dot_general | solution.py:150
  119.7 3.5 %all-to-all-start.5 = ((bf16[8,64,512]{2,1,0:T(8,128)(2,1)}), bf16[8,64,512]{2,1,0:T(8,128)(2,1)S(1)}, u32[]{:S(2)}, u32[]{:S(2)}) async-start(bf16[8,64,512]{2,1,0:T(8,128)(2,1)} %bitcast.36), calls=%async_computation.5 | async-start | bytes 1048576 | tf_op jit(solution)/shard_map/all_to_all | solution.py:41
  123.2 0.0 copy-done.7
  123.2 0.0 copy-start.4
  123.3 3.5 %fusion = bf16[512,1152]{1,0:T(8,128)(2,1)} fusion(bf16[512,512]{1,0:T(8,128)(2,1)S(1)} %bitcast.35, bf16[512,1152]{1,0:T(8,128)(2,1)} %bitcast.7, bf16[512,1152]{1,0:T(8,128)(2,1)} %param.9, f32[512]{0:T(512)S(1)} %get-tuple-element.14), kind=kOutput, calls=%fused_computation.1 | convolution fusion | flops 606339072 | bytes 4065280 | tf_op jit(solution)/shard_map/dot_general | solution.py:163
  126.8 5.8 %all-to-all-done.5 = bf16[8,64,512]{2,1,0:T(8,128)(2,1)S(1)} async-done(((bf16[8,64,512]{2,1,0:T(8,128)(2,1)}), bf16[8,64,512]{2,1,0:T(8,128)(2,1)S(1)}, u32[]{:S(2)}, u32[]{:S(2)}) %all-to-all-start.5) | async-done | bytes 524320 | tf_op jit(solution)/shard_map/all_to_all | solution.py:41
  132.6 0.1 convert_reduce_fusion.1
  132.7 0.0 copy-done.4
  132.7 0.1 select_convert_fusion
  132.7 0.7 broadcast_in_dim.29
  133.5 3.4 %all-to-all-start.6 = ((bf16[4,64,512]{2,1,0:T(8,128)(2,1)}), bf16[4,64,512]{2,1,0:T(8,128)(2,1)S(1)}, u32[]{:S(2)}, u32[]{:S(2)}) async-start(bf16[4,64,512]{2,1,0:T(8,128)(2,1)} %broadcast_in_dim.29), calls=%async_computation.6 | async-start | bytes 524288 | tf_op jit(solution)/shard_map/all_to_all | solution.py:41
  136.9 1.3 constant_dynamic-slice_fusion
  138.2 4.8 %all-to-all-done.6 = bf16[4,64,512]{2,1,0:T(8,128)(2,1)S(1)} async-done(((bf16[4,64,512]{2,1,0:T(8,128)(2,1)}), bf16[4,64,512]{2,1,0:T(8,128)(2,1)S(1)}, u32[]{:S(2)}, u32[]{:S(2)}) %all-to-all-start.6) | async-done | bytes 262176 | tf_op jit(solution)/shard_map/all_to_all | solution.py:41
  143.0 3.3 %all_gather.7.g_ref = bf16[512,512]{1,0:T(8,128)(2,1)S(1)} all-gather(bf16[256,512]{1,0:T(8,128)(2,1)S(1)} %bitcast.33), channel_id=1, replica_groups={{0,1},{2,3},{4,5},{6,7},{8,9},{10,11},{12,13},{14,15},{16,17},{18,19},{..., dimensions={0}, use_global_device_ids=true | all-gather | bytes 786432 | tf_op jit(solution)/shard_map/all_gather | solution.py:110
  146.3 2.1 %shard_map.93 = (bf16[1152,512]{1,0:T(8,128)(2,1)}, f32[512]{0:T(512)}) custom-call(bf16[1152,512]{1,0:T(8,128)(2,1)S(1)} %copy.15.x_ref, bf16[512,512]{1,0:T(8,128)(2,1)S(1)} %all_gather.7.g_ref), custom_call_target="tpu_custom_call" | custom-call | tf_op jit(solution)/shard_map/pallas_call | solution.py:71
  (10 shorter events, 0.2 us)
Async XLA Ops:
  0.6 1.3 copy-start
  0.6 15.3 %copy-start.9 = (s32[1,32]{1,0:T(1,128)S(1)}, s32[1,32]{1,0:T(1,128)}, u32[]{:S(2)}) copy-start(s32[1,32]{1,0:T(1,128)} %param.10) | copy-start | bytes 388
  1.9 14.1 %copy-start.5 = (bf16[512,1152]{1,0:T(8,128)(2,1)S(1)}, bf16[512,1152]{1,0:T(8,128)(2,1)}, u32[]{:S(2)}) copy-start(bf16[512,1152]{1,0:T(8,128)(2,1)} %param.9) | copy-start | bytes 3538948
  4.9 19.8 %all-to-all-start = ((bf16[8,64,512]{2,1,0:T(8,128)(2,1)}), bf16[8,64,512]{2,1,0:T(8,128)(2,1)S(1)}, u32[]{:S(2)}, u32[]{:S(2)}) async-start(bf16[8,64,512]{2,1,0:T(8,128)(2,1)} %bitcast.2), calls=%async_computation | async-start | bytes 1048576 | tf_op jit(solution)/shard_map/all_to_all | solution.py:41
  15.2 9.6 %copy-start.8 = (f32[512]{0:T(512)S(1)}, f32[512]{0:T(512)}, u32[]{:S(2)}) copy-start(f32[512]{0:T(512)} %param.8) | copy-start | bytes 6148
  24.8 8.4 %copy-start.3 = (f32[64,512]{1,0:T(8,128)}, f32[64,512]{1,0:T(8,128)S(1)}, u32[]{:S(2)}) copy-start(f32[64,512]{1,0:T(8,128)S(1)} %convert_reduce_fusion.2) | copy-start | bytes 393220
  37.1 0.8 copy-start.1
  38.0 0.9 copy-start.6
  66.9 18.9 %all-to-all-start.3 = ((bf16[4,32,1152]{2,1,0:T(8,128)(2,1)}), bf16[4,32,1152]{2,1,0:T(8,128)(2,1)S(1)}, u32[]{:S(2)}, u32[]{:S(2)}) async-start(bf16[4,32,1152]{2,1,0:T(8,128)(2,1)} %broadcast_in_dim.27), calls=%async_computation.3 | async-start | bytes 589824 | tf_op jit(solution)/shard_map/all_to_all | solution.py:41
  87.9 4.6 %copy-start.2 = (bf16[512,1152]{1,0:T(8,128)(2,1)S(1)}, bf16[512,1152]{1,0:T(8,128)(2,1)}, u32[]{:S(2)}) copy-start(bf16[512,1152]{1,0:T(8,128)(2,1)} %param.6) | copy-start | bytes 3538948
  87.9 28.5 %all-to-all-start.4 = ((bf16[16,32,1152]{2,1,0:T(8,128)(2,1)}), bf16[16,32,1152]{2,1,0:T(8,128)(2,1)}, u32[]{:S(2)}, u32[]{:S(2)}) async-start(bf16[16,32,1152]{2,1,0:T(8,128)(2,1)} %broadcast_in_dim.28), calls=%async_computation.4 | async-start | bytes 2359296 | tf_op jit(solution)/shard_map/all_to_all | solution.py:41
  116.4 6.9 %copy-start.7 = (bf16[2,4,64,512]{3,2,1,0:T(8,128)(2,1)S(1)}, bf16[2,4,64,512]{3,2,1,0:T(8,128)(2,1)}, u32[]{:S(2)}) copy-start(bf16[2,4,64,512]{3,2,1,0:T(8,128)(2,1)} %copy-done.6) | copy-start | bytes 1572868
  119.7 12.9 %all-to-all-start.5 = ((bf16[8,64,512]{2,1,0:T(8,128)(2,1)}), bf16[8,64,512]{2,1,0:T(8,128)(2,1)S(1)}, u32[]{:S(2)}, u32[]{:S(2)}) async-start(bf16[8,64,512]{2,1,0:T(8,128)(2,1)} %bitcast.36), calls=%async_computation.5 | async-start | bytes 1048576 | tf_op jit(solution)/shard_map/all_to_all | solution.py:41
  123.2 9.4 %copy-start.4 = (f32[64,512]{1,0:T(8,128)S(1)}, f32[64,512]{1,0:T(8,128)}, u32[]{:S(2)}) copy-start(f32[64,512]{1,0:T(8,128)} %copy-done.3) | copy-start | bytes 393220
  133.5 9.5 %all-to-all-start.6 = ((bf16[4,64,512]{2,1,0:T(8,128)(2,1)}), bf16[4,64,512]{2,1,0:T(8,128)(2,1)S(1)}, u32[]{:S(2)}, u32[]{:S(2)}) async-start(bf16[4,64,512]{2,1,0:T(8,128)(2,1)} %broadcast_in_dim.29), calls=%async_computation.6 | async-start | bytes 524288 | tf_op jit(solution)/shard_map/all_to_all | solution.py:41
